TPU v7x, 32 devices: a whole 2x2x4 slice. The times are simulated.
32 devices in a mesh: aux: 8 (over z, x), pair: 4 (over y, core).
Axes of the slice: x: 2, y: 2, z: 4, core: 2. Of those that a mesh axis runs over, the one named last changes fastest.
Arguments:
- shell_ints: bfloat16 [2048, 16, 64, 64], P('aux', 'pair'), may hold values from -0.119628906 to 0.119628906
- block_ids: int32 [16, 2], P('pair'), may hold values from 0 to 15
- block_count: int32 [4], P('pair'), may hold values from 1 to 4, 10 in all
- occ_coef: bfloat16 [16, 64, 512], replicated, may hold values from -0.75 to 0.75
- occ_pick: int32 [512], replicated, may hold values from 0 to 511, each once
- vir_coef: bfloat16 [16, 64, 384], replicated, may hold values from -0.1875 to 0.1875
- occ_energy: float32 [512], replicated, may hold values from -1.5 to -0.3
- vir_energy: float32 [384], replicated, may hold values from 0.2 to 3
Outputs:
- pair_energy: float32 [8], P('aux')
- vir_density: float32 [384, 384], P('pair')
Inputs may be any that keep to these rules, and one draw needn't show every extreme that they name: `block_ids`: basis block numbers of the mu and nu side. `block_count`: the busiest group holds exactly 4 live blocks. `occ_pick`: each of the 512 numbers appears once.
All inputs are finite; a program needn't handle non-finite values.
Results may differ from a plain program's by a relative error of at most 0.01.
Values may be sent and summed in bfloat16 or wider, within the bound.
No kernel may reach another device: no remote copies, remote signals or barrier semaphores. Data moves between devices by JAX's collectives and lax.ppermute only.
A program may use at most 128 MiB of HBM per device.

v0:
```python
import jax
import jax.numpy as jnp
from jax import lax
from jax.sharding import PartitionSpec as P


def shifted(value, axis, steps):
    count = lax.axis_size(axis)
    pairs = [(source, (source + steps) % count) for source in range(count)]
    return lax.ppermute(value, axis, pairs)


def group_part(half, vir_rows, nrows):
    slots, width, virtual = vir_rows.shape
    orbitals = half.shape[1]
    flat = half.reshape(nrows, orbitals, slots * width)
    total = jnp.einsum(
        "qik,ka->qia",
        flat,
        vir_rows.reshape(slots * width, virtual),
        preferred_element_type=jnp.float32,
    )
    return lax.optimization_barrier(total.astype(jnp.bfloat16)).astype(jnp.float32)


def slot_tables(ids, live, occ_coef, vir_coef, picker):
    blocks = jnp.arange(occ_coef.shape[0], dtype=jnp.int32)
    nu_onehot = (ids[:, 1][:, None] == blocks[None, :]).astype(jnp.bfloat16)
    mu_onehot = (ids[:, 0][:, None] == blocks[None, :]).astype(jnp.bfloat16) * live[:, None]
    occ_rows = jnp.einsum(
        "kt,tno->kno", nu_onehot, occ_coef, preferred_element_type=jnp.float32
    ).astype(jnp.bfloat16)
    occ_sel = jnp.einsum(
        "kno,oi->kni", occ_rows, picker, preferred_element_type=jnp.float32
    ).astype(jnp.bfloat16)
    vir_rows = jnp.einsum(
        "kt,tma->kma", mu_onehot, vir_coef, preferred_element_type=jnp.float32
    ).astype(jnp.bfloat16)
    return (occ_sel, vir_rows)


def per_device(
    shell_ints, block_ids, block_count, occ_coef, occ_pick, vir_coef, occ_energy, vir_energy
):
    aux_rows, slots, width, _ = shell_ints.shape
    n_aux = lax.axis_size("aux")
    n_pair = lax.axis_size("pair")
    nocc = occ_coef.shape[2]
    virtual = vir_coef.shape[2]
    batch = occ_pick[:n_aux]
    levels = jnp.arange(nocc, dtype=jnp.int32)
    picker = (levels[:, None] == batch[None, :]).astype(jnp.bfloat16)
    live = (jnp.arange(slots, dtype=jnp.int32) < block_count[0]).astype(jnp.bfloat16)
    occ_sel, vir_rows = slot_tables(block_ids, live, occ_coef, vir_coef, picker)
    half = jnp.einsum(
        "qkmn,kni->qikm", shell_ints, occ_sel, preferred_element_type=jnp.float32
    ).astype(jnp.bfloat16)
    partial_value = group_part(half, vir_rows, aux_rows).astype(jnp.bfloat16)
    moved = lax.all_to_all(partial_value, "aux", split_axis=1, concat_axis=0, tiled=True)
    fitted = lax.psum_scatter(
        moved.astype(jnp.float32).astype(jnp.bfloat16), "pair", scatter_dimension=0, tiled=True
    )
    index = lax.axis_index("aux")
    own_rows = fitted[:, 0, :]
    mate_rows = shifted(own_rows, "aux", n_aux // 2)
    block = jnp.einsum("qa,qb->ab", own_rows, mate_rows, preferred_element_type=jnp.float32)
    coulomb = lax.psum(block.astype(jnp.bfloat16), "pair").astype(jnp.float32)
    mate = (index - n_aux // 2) % n_aux
    own_level = jnp.sum(jnp.where(levels == batch[index], occ_energy, 0.0))
    mate_level = jnp.sum(jnp.where(levels == batch[mate], occ_energy, 0.0))
    denom = own_level + mate_level - vir_energy[:, None] - vir_energy[None, :]
    amplitude = coulomb / denom
    energy = jnp.sum(amplitude * (2.0 * coulomb - coulomb.T)).reshape(1)
    share = virtual // n_pair
    first_row = lax.axis_index("pair") * share
    upper = lax.dynamic_slice_in_dim(amplitude, first_row, share, 0)
    column = lax.dynamic_slice_in_dim(amplitude, first_row, share, 1)
    left_rows = 2.0 * upper - column.T
    density_rows = jnp.dot(left_rows, amplitude.T, precision=lax.Precision.HIGHEST)
    vir_density = lax.psum(density_rows, "aux")
    return (energy, vir_density)


def solution(mesh):
    placed = (P("aux", "pair", None, None), P("pair", None), P("pair"), P(), P(), P(), P(), P())
    return jax.shard_map(
        per_device,
        mesh=mesh,
        in_specs=placed,
        out_specs=(P("aux"), P("pair", None)),
        check_vma=False,
    )
```

profile of v0, /device:TPU:1, one launch (start us, length us, event | category | flops | bytes accessed | tf_op | source)
XLA Modules:
  0.0 222.6 jit_solution(836564285748781024)
XLA Ops:
  7.2 0.0 reduce-scatter.2.cloned.1.call-start
  7.2 0.8 slice_bitcast_fusion
  8.1 0.7 slice.10
  9.4 0.7 fusion.3
  10.1 4.8 %fusion.9 = bf16[4,8,256,64]{2,1,3,0:T(8,128)(2,1)S(1)} fusion(bf16[256,4,64,64]{0,3,2,1:T(8,128)(2,1)} %param.8, bf16[4,64,512]{2,0,1:T(4,128)(2,1)S(1)} %fusion.3, s32[8]{0:T(128)S(1)} %slice.10), kind=kOutput, calls=%fused_computation.14 | convolution fusion | flops 69212160 | bytes 9699360 | tf_op jit(solution)/shard_map/qkmn,kni->qikm/dot_general | solution.py:55
  14.9 0.6 fusion.5
  15.5 0.8 bitcast_convert_fusion
  16.3 42.4 %all_to_all.18 = bf16[256,8,384]{2,0,1:T(8,128)(2,1)} all-to-all(bf16[256,8,384]{2,0,1:T(8,128)(2,1)S(1)} %bitcast_convert_fusion), channel_id=1, replica_groups=mesh['aux'=8,'pair'=4] {'aux'}, dimensions={1} | all-to-all | bytes 3145728 | tf_op jit(solution)/shard_map/all_to_all | solution.py:59
  58.7 0.0 all-reduce.3.cloned.1.call-start
  58.8 28.5 %reduce-scatter.2.cloned.1.call-done = bf16[512,1,384]{2,0,1:T(8,128)(2,1)} async-done(((bf16[2048,1,384]{2,0,1:T(8,128)(2,1)}), bf16[512,1,384]{2,0,1:T(8,128)(2,1)}) %reduce-scatter.2.cloned.1.call-update) | async-done | bytes 393232 | tf_op jit(solution)/shard_map/reduce_scatter | solution.py:60
  87.2 2.1 collective-permute-start
  89.3 0.6 fusion.34
  89.9 1.9 select_reduce_fusion
  93.1 13.8 %collective-permute-done = bf16[512,384]{1,0:T(8,128)(2,1)S(1)} collective-permute-done((bf16[512,384]{1,0:T(8,128)(2,1)}, bf16[512,384]{1,0:T(8,128)(2,1)S(1)}, u32[]{:S(2)}, u32[]{:S(2)}) %collective-permute-start) | collective-permute-done | bytes 393248 | tf_op jit(solution)/shard_map/ppermute | solution.py:10
  106.9 2.1 convolution_convert_fusion
  109.0 0.0 all-reduce.5.cloned.1.call-start
  109.1 31.5 %all-reduce.3.cloned.1.call-done = bf16[384,384]{1,0:T(8,128)(2,1)} async-done(((bf16[384,384]{1,0:T(8,128)(2,1)}), bf16[384,384]{1,0:T(8,128)(2,1)}) %all-reduce.3.cloned.1.call-update) | async-done | bytes 294928 | tf_op jit(solution)/shard_map/psum | solution.py:67
  140.5 1.1 copy.10
  141.6 1.9 subtract_divide_fusion
  143.5 0.1 constant_dynamic-slice_fusion
  143.6 0.1 copy.20
  143.7 1.2 fusion.15
  144.9 69.6 %all-reduce.5.cloned.1.call-done = f32[96,384]{1,0:T(8,128)} async-done(((f32[96,384]{1,0:T(8,128)}), f32[96,384]{1,0:T(8,128)}) %all-reduce.5.cloned.1.call-update) | async-done | bytes 147472 | tf_op jit(solution)/shard_map/psum | solution.py:80
  214.5 1.6 copy.39
  (13 shorter events, 0.1 us)
Async XLA Ops:
  7.2 2.2 %copy-start = (bf16[16,64,512]{2,1,0:T(8,128)(2,1)S(1)}, bf16[16,64,512]{2,1,0:T(8,128)(2,1)}, u32[]{:S(2)}) copy-start(bf16[16,64,512]{2,1,0:T(8,128)(2,1)} %param.11) | copy-start | bytes 3145732
  7.2 7.8 %copy-start.1 = (bf16[16,64,384]{2,1,0:T(8,128)(2,1)S(1)}, bf16[16,64,384]{2,1,0:T(8,128)(2,1)}, u32[]{:S(2)}) copy-start(bf16[16,64,384]{2,1,0:T(8,128)(2,1)} %param.13) | copy-start | bytes 2359300
  7.2 80.0 %reduce-scatter.2.cloned.1.call-start = ((), (), s32[]{:S(2)}) async-start(), calls=%async_computation.2 | async-start | bytes 1966080 | tf_op jit(solution)/shard_map/reduce_scatter | solution.py:60
  10.1 79.8 %copy-start.3 = (f32[512]{0:T(512)S(1)}, f32[512]{0:T(512)}, u32[]{:S(2)}) copy-start(f32[512]{0:T(512)} %param.14) | copy-start | bytes 6148
  10.1 98.9 %copy-start.2 = (f32[384]{0:T(512)S(1)}, f32[384]{0:T(512)}, u32[]{:S(2)}) copy-start(f32[384]{0:T(512)} %param.15) | copy-start | bytes 4612
  58.7 81.8 %all-reduce.3.cloned.1.call-start = ((), (), s32[]{:S(2)}) async-start(), calls=%async_computation.3 | async-start | bytes 589824 | tf_op jit(solution)/shard_map/psum | solution.py:67
  87.2 19.6 %collective-permute-start = (bf16[512,384]{1,0:T(8,128)(2,1)}, bf16[512,384]{1,0:T(8,128)(2,1)S(1)}, u32[]{:S(2)}, u32[]{:S(2)}) collective-permute-start(bf16[512,384]{1,0:T(8,128)(2,1)} %bitcast.55), channel_id=1, source_target_pairs={{0,16},{4,20},{8,24},{12,28},{16,0},{20,4},{24,8},{28,12},{1,17},{... | collective-permute-start | bytes 1179656 | tf_op jit(solution)/shard_map/ppermute | solution.py:10
  109.0 105.5 %all-reduce.5.cloned.1.call-start = ((), (), s32[]{:S(2)}) async-start(), calls=%async_computation.4 | async-start | bytes 294912 | tf_op jit(solution)/shard_map/psum | solution.py:80
Sparse Core Ops, SparseCore 0:
  58.8 28.3 reduce-scatter.1
  109.1 31.3 all-reduce.2
  145.1 69.4 all-reduce.4
where the time goes:
time: 226 us; the launch traced here: 223 us
  waiting for transfers between devices  143 us (63%)
  blocking collectives  42.4 us (19%)
  between operations  15.7 us (7%)
  matrix products  10.1 us (4%)
  local copies, waits for them, and re-layouts  5.05 us (2%)
  other arithmetic  3.78 us (2%)
    psum x1, waiting for transfers between devices, per_device(): vir_density = lax.psum(density_rows, 'aux')  69.6 us
    all_to_all x1, blocking collectives, per_device(): lax.all_to_all(partial_value, 'aux', split_axis=1, concat_axis=0, tiled=T...  42.4 us
    psum x1, waiting for transfers between devices, per_device(): coulomb = lax.psum(block.astype(jnp.bfloat16), 'pair').astype(jnp.float32)  31.5 us
    reduce_scatter x1, waiting for transfers between devices, per_device(): lax.psum_scatter(moved.astype(jnp.float32).astype(jnp.bfloat16), 'pair',...  28.5 us
    ppermute x1, waiting for transfers between devices, shifted(): return lax.ppermute(value, axis, pairs)  13.8 us
    dot_general x1, matrix products, per_device(): jnp.einsum('qkmn,kni->qikm', shell_ints, occ_sel, preferred_element_type=...  4.81 us
  transfers between devices with their start and end apart: 4, of which 4 were waited for; matrix products, arithmetic and copies ran while one was open for 1% of the time, Pallas kernels for 0%

commit v1 on v0

v1 whole, which is shorter than its diff:
```python
import functools

import jax
import jax.numpy as jnp
from jax import lax
from jax.experimental import pallas as pl
from jax.experimental.pallas import tpu as pltpu
from jax.sharding import PartitionSpec as P

VMEM = pltpu.VMEM
SMEM = pltpu.SMEM


def swapped(value, axis, mask):
    count = lax.axis_size(axis)
    return lax.ppermute(value, axis, [(source, source ^ mask) for source in range(count)])


def coulomb_kernel(ids_ref, place_ref, vir_ref, *refs):
    n_pair = (len(refs) - 3) // 2
    parts_in, parts_out = refs[:n_pair], refs[n_pair:-3]
    rows_ref, left_ref, right_ref = refs[-3:]
    slots = ids_ref.shape[0] // n_pair
    width, virtual = vir_ref.shape[1], vir_ref.shape[2]
    span = slots * width

    @pl.when(pl.program_id(0) == 0)
    def _():
        for at in range(n_pair * slots):
            block = ids_ref[at]
            row = vir_ref[jnp.maximum(block, 0)]
            rows_ref[pl.ds(at * width, width), :] = jnp.where(block >= 0, row, jnp.zeros_like(row))

    for side, target in enumerate((left_ref, right_ref)):
        total = jnp.zeros((virtual, parts_in[0].shape[-1]), jnp.float32)
        for group in range(n_pair):
            total += lax.dot_general(
                rows_ref[pl.ds(group * span, span), :],
                parts_in[group][0, side],
                (((0,), (0,)), ((), ())),
                preferred_element_type=jnp.float32,
            )
        target[...] = total.astype(jnp.bfloat16)
    share = virtual // len(parts_out)
    for part, out in enumerate(parts_out):
        first = pl.multiple_of((place_ref[0] ^ part) * share, share)
        out[0] = lax.dot_general(
            left_ref[pl.ds(first, share), :],
            right_ref[...],
            (((1,), (1,)), ((), ())),
            preferred_element_type=jnp.float32,
        ).astype(jnp.bfloat16)


def coulomb_parts(ids, place, vir_coef, parts, quad):
    pairs, _, span, aux_rows = parts[0].shape
    virtual = vir_coef.shape[2]
    share = virtual // quad
    n_pair = len(parts)
    return pl.pallas_call(
        coulomb_kernel,
        grid=(pairs,),
        in_specs=[
            pl.BlockSpec(memory_space=SMEM),
            pl.BlockSpec(memory_space=SMEM),
            pl.BlockSpec(vir_coef.shape, lambda r: (0, 0, 0)),
        ]
        + [pl.BlockSpec((1, 2, span, aux_rows), lambda r: (r, 0, 0, 0))] * n_pair,
        out_specs=[pl.BlockSpec((1, share, virtual), lambda r: (r, 0, 0))] * quad,
        out_shape=[jax.ShapeDtypeStruct((pairs, share, virtual), jnp.bfloat16)] * quad,
        scratch_shapes=[
            VMEM((n_pair * span, virtual), jnp.bfloat16),
            VMEM((virtual, aux_rows), jnp.bfloat16),
            VMEM((virtual, aux_rows), jnp.bfloat16),
        ],
        compiler_params=pltpu.CompilerParams(vmem_limit_bytes=48 * 1024 * 1024),
        name="coulomb_parts",
    )(ids, place, vir_coef, *parts)


def density_kernel(place_ref, level_ref, vir_ref, virt_ref, *refs):
    quad, n_pair, pairs = refs[0], refs[1], refs[2]
    chunks = refs[3 : 3 + quad]
    own_ref, outs = refs[3 + quad], refs[4 + quad : 3 + quad + n_pair]
    energy_ref, block_ref, even_ref, odd_ref, total_ref = refs[3 + quad + n_pair :]
    virtual = block_ref.shape[0]
    share = virtual // quad
    rows = virtual // n_pair
    step = pl.program_id(0)
    for part in range(quad):
        first = pl.multiple_of((place_ref[0] ^ part) * share, share)
        block_ref[pl.ds(first, share), :] = chunks[part][0].astype(jnp.float32)
    block = block_ref[...]
    flipped = block.T
    inverse = 1.0 / (level_ref[step] - vir_ref[...] - virt_ref[...])
    energy = jnp.sum(block * (2.0 * block - flipped) * inverse)
    even = ((block + flipped) * inverse).astype(jnp.bfloat16)
    odd = ((block - flipped) * inverse).astype(jnp.bfloat16)
    even_ref[...] = even
    odd_ref[...] = odd
    for part in range(n_pair):
        first = pl.multiple_of((place_ref[1] ^ part) * rows, rows)
        term = 0.5 * jnp.dot(even_ref[pl.ds(first, rows), :], even, preferred_element_type=jnp.float32)
        term -= 1.5 * jnp.dot(odd_ref[pl.ds(first, rows), :], odd, preferred_element_type=jnp.float32)
        if pairs > 1:
            term += jnp.where(step == 0, 0.0, total_ref[part])
            total_ref[part] = term
        if part == 0:
            own_ref[...] = term
        else:
            outs[part - 1][pl.ds(0, rows), :] = term.astype(jnp.bfloat16)
    high = jnp.full((16, virtual), energy, jnp.float32).astype(jnp.bfloat16)
    rest = energy - high.astype(jnp.float32)
    middle = rest.astype(jnp.bfloat16)
    low = (rest - middle.astype(jnp.float32)).astype(jnp.bfloat16)
    kind = lax.broadcasted_iota(jnp.int32, (16, virtual), 0)
    lane = lax.broadcasted_iota(jnp.int32, (16, virtual), 1)
    packed = jnp.where(kind == 0, high, jnp.where(kind == 1, middle, jnp.where(kind == 2, low, jnp.zeros_like(low))))
    held = jnp.where(lane == step, packed, jnp.where(step == 0, jnp.zeros_like(packed), energy_ref[...]))
    energy_ref[...] = held
    for out in outs:
        out[pl.ds(rows, 16), :] = held


def density_parts(place, levels, vir_energy, chunks, n_pair):
    quad = len(chunks)
    pairs, share, virtual = chunks[0].shape
    rows = virtual // n_pair

    def kernel(place_ref, level_ref, vir_ref, virt_ref, *refs):
        density_kernel(place_ref, level_ref, vir_ref, virt_ref, quad, n_pair, pairs, *refs)

    fixed = lambda shape: pl.BlockSpec(shape, lambda r: (0,) * len(shape))
    return pl.pallas_call(
        kernel,
        grid=(pairs,),
        in_specs=[
            pl.BlockSpec(memory_space=SMEM),
            pl.BlockSpec(memory_space=SMEM),
            fixed((virtual, 1)),
            fixed((1, virtual)),
        ]
        + [pl.BlockSpec((1, share, virtual), lambda r: (r, 0, 0))] * quad,
        out_specs=[fixed((rows, virtual))] + [fixed((rows + 16, virtual))] * (n_pair - 1) + [fixed((16, virtual))],
        out_shape=[jax.ShapeDtypeStruct((rows, virtual), jnp.float32)]
        + [jax.ShapeDtypeStruct((rows + 16, virtual), jnp.bfloat16)] * (n_pair - 1)
        + [jax.ShapeDtypeStruct((16, virtual), jnp.bfloat16)],
        scratch_shapes=[
            VMEM((virtual, virtual), jnp.float32),
            VMEM((virtual, virtual), jnp.bfloat16),
            VMEM((virtual, virtual), jnp.bfloat16),
            VMEM((n_pair, rows, virtual) if pairs > 1 else (1, 8, 128), jnp.float32),
        ],
        compiler_params=pltpu.CompilerParams(vmem_limit_bytes=48 * 1024 * 1024),
        name="density_parts",
    )(place, levels, vir_energy[:, None], vir_energy[None, :], *chunks)


def summed(value, axis, low, bits):
    if bits == 0:
        return value
    if bits == 1:
        other = swapped(value, axis, 1 << low)
        return (value.astype(jnp.float32) + other.astype(jnp.float32)).astype(jnp.bfloat16)
    place = (lax.axis_index(axis) >> low) & 3
    share = value.shape[1] // 4
    parts = [lax.dynamic_slice_in_dim(value, (place ^ d) * share, share, 1) for d in range(4)]
    chunks = scattered(parts, axis, low, bits)
    out = jnp.zeros_like(value)
    for d in range(4):
        out = lax.dynamic_update_slice_in_dim(out, chunks[d], (place ^ d) * share, 1)
    return out


def scattered(parts, axis, low, bits):
    total = parts[0].astype(jnp.float32)
    for d in (3, 2, 1):
        total += swapped(parts[d], axis, d << low).astype(jnp.float32)
    total = summed(total.astype(jnp.bfloat16), axis, low + 2, bits - 2)
    return [total] + [swapped(total, axis, d << low) for d in (1, 2, 3)]


def per_device(
    shell_ints, block_ids, block_count, occ_coef, occ_pick, vir_coef, occ_energy, vir_energy
):
    aux_rows, slots, width, _ = shell_ints.shape
    n_aux = lax.axis_size("aux")
    n_pair = lax.axis_size("pair")
    nocc = occ_coef.shape[2]
    virtual = vir_coef.shape[2]
    n_half = n_aux // 2
    pairs = n_half // n_pair
    aux_at = lax.axis_index("aux")
    pair_at = lax.axis_index("pair")

    live = jnp.arange(slots, dtype=jnp.int32) < block_count[0]
    mu_ids = jnp.where(live, block_ids[:, 0], -1)
    ids = jnp.concatenate([mu_ids] + [swapped(mu_ids, "pair", d) for d in range(1, n_pair)])

    mates = pair_at ^ jnp.arange(n_pair, dtype=jnp.int32)
    order = (mates[:, None] * pairs + jnp.arange(pairs, dtype=jnp.int32)[None, :])[:, :, None]
    order = (order + jnp.array([0, n_half], jnp.int32)[None, None, :]).reshape(n_aux)
    spots = jnp.arange(n_aux, dtype=jnp.int32)
    batch = jnp.sum(jnp.where(order[:, None] == spots[None, :], occ_pick[:n_aux][None, :], 0), axis=1)
    orbitals = jnp.arange(nocc, dtype=jnp.int32)
    chosen = orbitals[:, None] == batch[None, :]
    levels = jnp.sum(jnp.where(chosen[:, : 2 * pairs], occ_energy[:, None], 0.0), axis=0)
    levels = jnp.sum(levels.reshape(pairs, 2), axis=1)

    blocks = jnp.arange(occ_coef.shape[0], dtype=jnp.int32)
    nu_onehot = (block_ids[:, 1][:, None] == blocks[None, :]).astype(jnp.bfloat16)
    occ_rows = jnp.einsum("kt,tno->kno", nu_onehot, occ_coef, preferred_element_type=jnp.float32).astype(jnp.bfloat16)
    occ_sel = jnp.einsum(
        "kno,oi->kni", occ_rows, chosen.astype(jnp.bfloat16), preferred_element_type=jnp.float32
    ).astype(jnp.bfloat16)
    half = jnp.einsum(
        "qkmn,kni->ikmq", shell_ints, occ_sel, preferred_element_type=jnp.float32
    ).astype(jnp.bfloat16)
    half = half.reshape(n_pair, pairs, 2, slots * width, aux_rows)
    sent = [half[d] for d in range(n_pair)]
    got = [sent[0]] + [swapped(sent[d], "pair", d) for d in range(1, n_pair)]

    bits = n_aux.bit_length() - 1
    quad = 4 if bits >= 2 else 1
    place = jnp.stack([aux_at & (quad - 1), pair_at]).astype(jnp.int32)
    parts = coulomb_parts(ids, place, vir_coef, got, quad)
    chunks = scattered(parts, "aux", 0, bits)
    outs = density_parts(place, levels, vir_energy, chunks, n_pair)
    own, sent, energies = outs[0], outs[1:-1], outs[-1]
    rows = virtual // n_pair
    density = own
    energy = [energies]
    for d in range(1, n_pair):
        other = swapped(sent[d - 1], "pair", d)
        density += other[:rows].astype(jnp.float32)
        energy.append(other[rows:])
    found = jnp.stack(energy)[:, :3, :pairs].astype(jnp.float32).sum(axis=1)
    wanted = aux_at % n_half
    mine = mates[:, None] * pairs + jnp.arange(pairs, dtype=jnp.int32)[None, :] == wanted
    return (jnp.sum(jnp.where(mine, found, 0.0)).reshape(1), density)


def solution(mesh):
    placed = (P("aux", "pair", None, None), P("pair", None), P("pair"), P(), P(), P(), P(), P())
    return jax.shard_map(
        per_device,
        mesh=mesh,
        in_specs=placed,
        out_specs=(P("aux"), P("pair", None)),
        check_vma=False,
    )
```

time: 226 us -> 58.3 us (0.26); the launches traced: 223 us -> 57.3 us
  waiting for transfers between devices: 143 us -> 19.9 us
  blocking collectives: 42.4 us -> 0 us
  starting transfers between devices: 2.25 us -> 20.1 us
  between operations: 15.7 us -> 1.46 us
  matrix products: 10.1 us -> 5.48 us
  Pallas kernels: 0 us -> 3.62 us
    psum x2 -> x0, waiting for transfers between devices: 101 us -> none  [the longest x1 69.6 us: per_device(): vir_density = lax.psum(density_rows, 'aux')]
    all_to_all x1 -> x0, blocking collectives: 42.4 us -> none  [per_device(): lax.all_to_all(partial_value, 'aux', split_axis=1, concat_axis=0, tiled=T...]
    reduce_scatter x1 -> x0, waiting for transfers between devices: 28.5 us -> none  [per_device(): lax.psum_scatter(moved.astype(jnp.float32).astype(jnp.bfloat16), 'pair',...]
    ppermute x1 -> x16, starting transfers between devices: 2.13 us -> 20.1 us  [swapped(): lax.ppermute(value, axis, [(source, source ^ mask) for source in range(co...]
    ppermute x1 -> x16, waiting for transfers between devices: 13.8 us -> 19.9 us  [swapped(): lax.ppermute(value, axis, [(source, source ^ mask) for source in range(co...]
    dot_general x6 -> x2, matrix products: 10.1 us -> 5.48 us  [the longest x1 4.8 us: per_device(): jnp.einsum('qkmn,kni->ikmq', shell_ints, occ_sel, preferred_element_type=...]
    pallas_call x0 -> x2, Pallas kernels: none -> 3.62 us  [the longest x1 2.14 us: density_parts(): pl.pallas_call(kernel, grid=(pairs,), in_specs=[pl.BlockSpec(memory_space...]
    slice x1 -> x6, local copies, waits for them, and re-layouts: 0.68 us -> 3.21 us  [the longest x5 2.41 us: per_device(): sent = [half[d] for d in range(n_pair)]]
  transfers between devices with their start and end apart: 4 -> 16, of which waited for: 4 -> 8; matrix products, arithmetic and copies ran while one was open for 1% -> 4% of each run, Pallas kernels for 0% -> 0%
where the time goes in v1:
time: 58.3 us; the launch traced here: 57.3 us
  starting transfers between devices  20.1 us (34%)
  waiting for transfers between devices  19.9 us (34%)
  matrix products  5.48 us (9%)
  local copies, waits for them, and re-layouts  4.12 us (7%)
  Pallas kernels  3.62 us (6%)
  other arithmetic  2.58 us (4%)
  between operations  1.46 us (3%)
    ppermute x16, starting transfers between devices, swapped(): lax.ppermute(value, axis, [(source, source ^ mask) for source in range(co...  20.1 us
    ppermute x16, waiting for transfers between devices, swapped(): lax.ppermute(value, axis, [(source, source ^ mask) for source in range(co...  19.9 us
    dot_general x1, matrix products, per_device(): jnp.einsum('qkmn,kni->ikmq', shell_ints, occ_sel, preferred_element_type=...  4.8 us
    slice x5, local copies, waits for them, and re-layouts, per_device(): sent = [half[d] for d in range(n_pair)]  2.41 us
    pallas_call x1, Pallas kernels, density_parts(): pl.pallas_call(kernel, grid=(pairs,), in_specs=[pl.BlockSpec(memory_space...  2.14 us
    pallas_call x1, Pallas kernels, coulomb_parts(): pl.pallas_call(coulomb_kernel, grid=(pairs,), in_specs=[pl.BlockSpec(memo...  1.49 us
  transfers between devices with their start and end apart: 16, of which 8 were waited for; matrix products, arithmetic and copies ran while one was open for 4% of the time, Pallas kernels for 0%

profile of v1, /device:TPU:1, one launch (start us, length us, event | category | flops | bytes accessed | tf_op | source)
XLA Modules:
  0.0 57.3 jit_solution(16517328909535875293)
XLA Ops:
  0.9 0.8 %slice.49 = s32[8]{0:T(128)S(1)} slice(s32[512]{0:T(512)} %param.13), slice={[0:8]} | slice | bytes 64 | tf_op jit(solution)/shard_map/slice | solution.py:204
  3.2 4.8 %fusion = bf16[8,4,64,256]{3,0,2,1:T(8,128)(2,1)S(1)} fusion(bf16[256,4,64,64]{0,3,2,1:T(8,128)(2,1)} %param.9, bf16[4,64,512]{2,0,1:T(4,128)(2,1)S(1)} %convolution_convert_fusion.1, s32[8]{0:T(128)S(1)} %select_reduce_fusion), kind=kOutput, calls=%fused_computation.1 | convolution fusion | flops 69736448 | bytes 9699360 | tf_op jit(solution)/shard_map/qkmn,kni->ikmq/dot_general | solution.py:216
  8.0 0.9 %fusion.12 = (bf16[2,4,64,256]{3,0,2,1:T(2,128)(2,1)S(1)}, bf16[2,4,64,256]{3,0,2,1:T(2,128)(2,1)S(1)}, bf16[2,4,64,256]{3,0,2,1:T(2,128)(2,1)S(1)}, bf16[2,4,64,256]{3,0,2,1:T(2,128)(2,1)S(1)}) fusion(bf16[8,4,64,256]{3,0,2,1:T(8,128)(2,1)S(1)} %fusion), kind=kLoop, calls=%fused_computation.35 | loop fusion | bytes 2097152 | tf_op jit(solution)/shard_map/slice | solution.py:220
  9.1 0.7 %copy.24 = bf16[2,4,64,256]{3,2,1,0:T(8,128)(2,1)} copy(bf16[2,4,64,256]{3,0,2,1:T(2,128)(2,1)S(1)} %get-tuple-element.21) | data formatting | bytes 524288 | tf_op jit(solution)/shard_map/slice | solution.py:220
  9.8 2.7 %collective-permute-start.4 = (bf16[1,2,256,256]{3,2,1,0:T(8,128)(2,1)}, bf16[1,2,256,256]{3,2,1,0:T(8,128)(2,1)S(1)}, u32[]{:S(2)}, u32[]{:S(2)}) collective-permute-start(bf16[1,2,256,256]{3,2,1,0:T(8,128)(2,1)} %bitcast.13), channel_id=1, source_target_pairs={{0,2},{1,3},{2,0},{3,1},{4,6},{5,7},{6,4},{7,5},{8,10},{9,11},{10,... | collective-permute-start | bytes 786440 | tf_op jit(solution)/shard_map/ppermute | solution.py:16
  12.5 0.7 %copy.25 = bf16[2,4,64,256]{3,2,1,0:T(8,128)(2,1)} copy(bf16[2,4,64,256]{3,0,2,1:T(2,128)(2,1)S(1)} %get-tuple-element.20) | data formatting | bytes 524288 | tf_op jit(solution)/shard_map/slice | solution.py:220
  14.4 1.5 %collective-permute-start.1 = (s32[4]{0:T(128)S(1)}, s32[4]{0:T(128)S(1)}, u32[]{:S(2)}, u32[]{:S(2)}) collective-permute-start(s32[4]{0:T(128)S(1)} %compare_select_fusion), channel_id=1, source_target_pairs={{0,2},{1,3},{2,0},{3,1},{4,6},{5,7},{6,4},{7,5},{8,10},{9,11},{10,... | collective-permute-start | bytes 56 | tf_op jit(solution)/shard_map/ppermute | solution.py:16
  16.0 0.9 %collective-permute-start.2 = (s32[4]{0:T(128)S(1)}, s32[4]{0:T(128)S(1)}, u32[]{:S(2)}, u32[]{:S(2)}) collective-permute-start(s32[4]{0:T(128)S(1)} %compare_select_fusion), channel_id=1, source_target_pairs={{0,3},{1,2},{2,1},{3,0},{4,7},{5,6},{6,5},{7,4},{8,11},{9,10},{10,... | collective-permute-start | bytes 56 | tf_op jit(solution)/shard_map/ppermute | solution.py:16
  16.8 8.1 %collective-permute-done.1 = s32[4]{0:T(128)S(1)} collective-permute-done((s32[4]{0:T(128)S(1)}, s32[4]{0:T(128)S(1)}, u32[]{:S(2)}, u32[]{:S(2)}) %collective-permute-start.1) | collective-permute-done | bytes 48 | tf_op jit(solution)/shard_map/ppermute | solution.py:16
  25.1 1.5 %coulomb_parts.1 = (bf16[1,96,384]{2,1,0:T(8,128)(2,1)S(1)}, bf16[1,96,384]{2,1,0:T(8,128)(2,1)S(1)}, bf16[1,96,384]{2,1,0:T(8,128)(2,1)S(1)}, bf16[1,96,384]{2,1,0:T(8,128)(2,1)S(1)}) custom-call(s32[16]{0:T(128)S(1)} %pad_add_fusion.1.ids_ref, s32[2]{0:T(128)S(1)} %pad_add_fusion.place_ref, bf16[16,64,384]{2,1,0:T(8,128)(2,1)S(1)} %copy-done.1, ...), custom_call_target="tpu_custom_call" | custom-call | tf_op jit(solution)/shard_map/coulomb_parts/pallas_call | solution.py:60
  26.6 2.5 %collective-permute-start.6 = (bf16[1,96,384]{2,1,0:T(8,128)(2,1)S(1)}, bf16[1,96,384]{2,1,0:T(8,128)(2,1)S(1)}, u32[]{:S(2)}, u32[]{:S(2)}) collective-permute-start(bf16[1,96,384]{2,1,0:T(8,128)(2,1)S(1)} %get-tuple-element.12), channel_id=1, source_target_pairs={{0,12},{4,8},{8,4},{12,0},{16,28},{20,24},{24,20},{28,16},{1,13},{... | collective-permute-start | bytes 221192 | tf_op jit(solution)/shard_map/ppermute | solution.py:16
  29.4 1.4 %collective-permute-done.6 = bf16[1,96,384]{2,1,0:T(8,128)(2,1)S(1)} collective-permute-done((bf16[1,96,384]{2,1,0:T(8,128)(2,1)S(1)}, bf16[1,96,384]{2,1,0:T(8,128)(2,1)S(1)}, u32[]{:S(2)}, u32[]{:S(2)}) %collective-permute-start.6) | collective-permute-done | bytes 73760 | tf_op jit(solution)/shard_map/ppermute | solution.py:16
  30.8 2.0 %collective-permute-done.7 = bf16[1,96,384]{2,1,0:T(8,128)(2,1)S(1)} collective-permute-done((bf16[1,96,384]{2,1,0:T(8,128)(2,1)S(1)}, bf16[1,96,384]{2,1,0:T(8,128)(2,1)S(1)}, u32[]{:S(2)}, u32[]{:S(2)}) %collective-permute-start.7) | collective-permute-done | bytes 73760 | tf_op jit(solution)/shard_map/ppermute | solution.py:16
  32.9 2.7 %collective-permute-start.9 = (bf16[1,96,384]{2,1,0:T(8,128)(2,1)S(1)}, bf16[1,96,384]{2,1,0:T(8,128)(2,1)S(1)}, u32[]{:S(2)}, u32[]{:S(2)}) collective-permute-start(bf16[1,96,384]{2,1,0:T(8,128)(2,1)S(1)} %add_convert_fusion.1), channel_id=1, source_target_pairs={{0,16},{4,20},{8,24},{12,28},{16,0},{20,4},{24,8},{28,12},{1,17},{... | collective-permute-start | bytes 221192 | tf_op jit(solution)/shard_map/ppermute | solution.py:16
  35.8 1.5 %collective-permute-done.9 = bf16[1,96,384]{2,1,0:T(8,128)(2,1)S(1)} collective-permute-done((bf16[1,96,384]{2,1,0:T(8,128)(2,1)S(1)}, bf16[1,96,384]{2,1,0:T(8,128)(2,1)S(1)}, u32[]{:S(2)}, u32[]{:S(2)}) %collective-permute-start.9) | collective-permute-done | bytes 73760 | tf_op jit(solution)/shard_map/ppermute | solution.py:16
  37.4 2.2 %collective-permute-start.10 = (bf16[1,96,384]{2,1,0:T(8,128)(2,1)S(1)}, bf16[1,96,384]{2,1,0:T(8,128)(2,1)S(1)}, u32[]{:S(2)}, u32[]{:S(2)}) collective-permute-start(bf16[1,96,384]{2,1,0:T(8,128)(2,1)S(1)} %add_convert_fusion.refs_0_), channel_id=1, source_target_pairs={{0,4},{4,0},{8,12},{12,8},{16,20},{20,16},{24,28},{28,24},{1,5},{5... | collective-permute-start | bytes 221192 | tf_op jit(solution)/shard_map/ppermute | solution.py:16
  39.6 1.2 %collective-permute-start.12 = (bf16[1,96,384]{2,1,0:T(8,128)(2,1)S(1)}, bf16[1,96,384]{2,1,0:T(8,128)(2,1)S(1)}, u32[]{:S(2)}, u32[]{:S(2)}) collective-permute-start(bf16[1,96,384]{2,1,0:T(8,128)(2,1)S(1)} %add_convert_fusion.refs_0_), channel_id=1, source_target_pairs={{0,12},{4,8},{8,4},{12,0},{16,28},{20,24},{24,20},{28,16},{1,13},{... | collective-permute-start | bytes 221192 | tf_op jit(solution)/shard_map/ppermute | solution.py:16
  41.5 1.3 %collective-permute-done.11.refs_2_ = bf16[1,96,384]{2,1,0:T(8,128)(2,1)S(1)} collective-permute-done((bf16[1,96,384]{2,1,0:T(8,128)(2,1)S(1)}, bf16[1,96,384]{2,1,0:T(8,128)(2,1)S(1)}, u32[]{:S(2)}, u32[]{:S(2)}) %collective-permute-start.11) | collective-permute-done | bytes 73760 | tf_op jit(solution)/shard_map/ppermute | solution.py:16
  42.8 1.0 %collective-permute-done.12.refs_3_ = bf16[1,96,384]{2,1,0:T(8,128)(2,1)S(1)} collective-permute-done((bf16[1,96,384]{2,1,0:T(8,128)(2,1)S(1)}, bf16[1,96,384]{2,1,0:T(8,128)(2,1)S(1)}, u32[]{:S(2)}, u32[]{:S(2)}) %collective-permute-start.12) | collective-permute-done | bytes 73760 | tf_op jit(solution)/shard_map/ppermute | solution.py:16
  43.8 2.1 %density_parts.1 = (f32[96,384]{1,0:T(8,128)S(1)}, bf16[112,384]{1,0:T(8,128)(2,1)S(1)}, bf16[112,384]{1,0:T(8,128)(2,1)S(1)}, bf16[112,384]{1,0:T(8,128)(2,1)S(1)}, bf16[16,384]{1,0:T(8,128)(2,1)S(1)}) custom-call(s32[2]{0:T(128)S(1)} %pad_add_fusion.place_ref, f32[1]{0:T(128)} %bitcast.2.level_ref, f32[384,1]{1,0:T(8,128)S(1)} %broadcast_in_dim.54.vir_ref, ...), custom_call_target="tpu_custom_call" | custom-call | tf_op jit(solution)/shard_map/density_parts/pallas_call | solution.py:134
  46.0 5.1 %collective-permute-start.15 = (bf16[112,384]{1,0:T(8,128)(2,1)S(1)}, bf16[112,384]{1,0:T(8,128)(2,1)S(1)}, u32[]{:S(2)}, u32[]{:S(2)}) collective-permute-start(bf16[112,384]{1,0:T(8,128)(2,1)S(1)} %get-tuple-element.18), channel_id=1, source_target_pairs={{0,3},{1,2},{2,1},{3,0},{4,7},{5,6},{6,5},{7,4},{8,11},{9,10},{10,... | collective-permute-start | bytes 258056 | tf_op jit(solution)/shard_map/ppermute | solution.py:16
  51.3 3.0 %collective-permute-done.15 = bf16[112,384]{1,0:T(8,128)(2,1)S(1)} collective-permute-done((bf16[112,384]{1,0:T(8,128)(2,1)S(1)}, bf16[112,384]{1,0:T(8,128)(2,1)S(1)}, u32[]{:S(2)}, u32[]{:S(2)}) %collective-permute-start.15) | collective-permute-done | bytes 86048 | tf_op jit(solution)/shard_map/ppermute | solution.py:16
  54.4 1.5 %collective-permute-done.14 = bf16[112,384]{1,0:T(8,128)(2,1)S(1)} collective-permute-done((bf16[112,384]{1,0:T(8,128)(2,1)S(1)}, bf16[112,384]{1,0:T(8,128)(2,1)S(1)}, u32[]{:S(2)}, u32[]{:S(2)}) %collective-permute-start.14) | collective-permute-done | bytes 86048 | tf_op jit(solution)/shard_map/ppermute | solution.py:16
  56.6 0.7 %convert_add_fusion = f32[96,384]{1,0:T(8,128)} fusion(f32[96,384]{1,0:T(8,128)S(1)} %get-tuple-element.19, bf16[112,384]{1,0:T(8,128)(2,1)S(1)} %collective-permute-done.15, bf16[112,384]{1,0:T(8,128)(2,1)S(1)} %collective-permute-done.14, bf16[112,384]{1,0:T(8,128)(2,1)S(1)} %collective-permute-done.13), kind=kLoop, calls=%fused_computation.7 | loop fusion | flops 221184 | bytes 516096 | tf_op jit(solution)/shard_map/add | solution.py:235
  (49 shorter events, 4.8 us)
Async XLA Ops:
  0.6 1.9 %copy-start = (bf16[16,64,512]{2,1,0:T(8,128)(2,1)S(1)}, bf16[16,64,512]{2,1,0:T(8,128)(2,1)}, u32[]{:S(2)}) copy-start(bf16[16,64,512]{2,1,0:T(8,128)(2,1)} %param.12) | copy-start | bytes 3145732
  0.6 13.2 %copy-start.4 = (s32[4,2]{0,1:T(2,128)S(1)}, s32[4,2]{0,1:T(2,128)}, u32[]{:S(2)}) copy-start(s32[4,2]{0,1:T(2,128)} %param.10) | copy-start | bytes 100
  0.7 24.4 %copy-start.1 = (bf16[16,64,384]{2,1,0:T(8,128)(2,1)S(1)}, bf16[16,64,384]{2,1,0:T(8,128)(2,1)}, u32[]{:S(2)}) copy-start(bf16[16,64,384]{2,1,0:T(8,128)(2,1)} %vir_ref.1) | copy-start | bytes 2359300
  3.2 32.5 %copy-start.2 = (f32[384]{0:T(512)S(1)}, f32[384]{0:T(512)}, u32[]{:S(2)}) copy-start(f32[384]{0:T(512)} %param.16) | copy-start | bytes 4612
  3.2 37.6 %copy-start.3 = (f32[512]{0:T(512)S(1)}, f32[512]{0:T(512)}, u32[]{:S(2)}) copy-start(f32[512]{0:T(512)} %param.15) | copy-start | bytes 6148
  8.9 16.1 %collective-permute-start.3 = (bf16[1,2,256,256]{3,2,1,0:T(8,128)(2,1)S(1)}, bf16[1,2,256,256]{3,2,1,0:T(8,128)(2,1)S(1)}, u32[]{:S(2)}, u32[]{:S(2)}) collective-permute-start(bf16[1,2,256,256]{3,2,1,0:T(8,128)(2,1)S(1)} %bitcast.41), channel_id=1, source_target_pairs={{0,1},{1,0},{2,3},{3,2},{4,5},{5,4},{6,7},{7,6},{8,9},{9,8},{10,11... | collective-permute-start | bytes 786440 | tf_op jit(solution)/shard_map/ppermute | solution.py:16
  9.8 15.3 %collective-permute-start.4 = (bf16[1,2,256,256]{3,2,1,0:T(8,128)(2,1)}, bf16[1,2,256,256]{3,2,1,0:T(8,128)(2,1)S(1)}, u32[]{:S(2)}, u32[]{:S(2)}) collective-permute-start(bf16[1,2,256,256]{3,2,1,0:T(8,128)(2,1)} %bitcast.13), channel_id=1, source_target_pairs={{0,2},{1,3},{2,0},{3,1},{4,6},{5,7},{6,4},{7,5},{8,10},{9,11},{10,... | collective-permute-start | bytes 786440 | tf_op jit(solution)/shard_map/ppermute | solution.py:16
  13.2 11.8 %collective-permute-start.5 = (bf16[1,2,256,256]{3,2,1,0:T(8,128)(2,1)}, bf16[1,2,256,256]{3,2,1,0:T(8,128)(2,1)S(1)}, u32[]{:S(2)}, u32[]{:S(2)}) collective-permute-start(bf16[1,2,256,256]{3,2,1,0:T(8,128)(2,1)} %bitcast.14), channel_id=1, source_target_pairs={{0,3},{1,2},{2,1},{3,0},{4,7},{5,6},{6,5},{7,4},{8,11},{9,10},{10,... | collective-permute-start | bytes 786440 | tf_op jit(solution)/shard_map/ppermute | solution.py:16
  13.9 2.0 %collective-permute-start = (s32[4]{0:T(128)S(1)}, s32[4]{0:T(128)S(1)}, u32[]{:S(2)}, u32[]{:S(2)}) collective-permute-start(s32[4]{0:T(128)S(1)} %compare_select_fusion), channel_id=1, source_target_pairs={{0,1},{1,0},{2,3},{3,2},{4,5},{5,4},{6,7},{7,6},{8,9},{9,8},{10,11... | collective-permute-start | bytes 56 | tf_op jit(solution)/shard_map/ppermute | solution.py:16
  14.4 10.6 %collective-permute-start.1 = (s32[4]{0:T(128)S(1)}, s32[4]{0:T(128)S(1)}, u32[]{:S(2)}, u32[]{:S(2)}) collective-permute-start(s32[4]{0:T(128)S(1)} %compare_select_fusion), channel_id=1, source_target_pairs={{0,2},{1,3},{2,0},{3,1},{4,6},{5,7},{6,4},{7,5},{8,10},{9,11},{10,... | collective-permute-start | bytes 56 | tf_op jit(solution)/shard_map/ppermute | solution.py:16
  16.0 9.0 %collective-permute-start.2 = (s32[4]{0:T(128)S(1)}, s32[4]{0:T(128)S(1)}, u32[]{:S(2)}, u32[]{:S(2)}) collective-permute-start(s32[4]{0:T(128)S(1)} %compare_select_fusion), channel_id=1, source_target_pairs={{0,3},{1,2},{2,1},{3,0},{4,7},{5,6},{6,5},{7,4},{8,11},{9,10},{10,... | collective-permute-start | bytes 56 | tf_op jit(solution)/shard_map/ppermute | solution.py:16
  26.6 4.2 %collective-permute-start.6 = (bf16[1,96,384]{2,1,0:T(8,128)(2,1)S(1)}, bf16[1,96,384]{2,1,0:T(8,128)(2,1)S(1)}, u32[]{:S(2)}, u32[]{:S(2)}) collective-permute-start(bf16[1,96,384]{2,1,0:T(8,128)(2,1)S(1)} %get-tuple-element.12), channel_id=1, source_target_pairs={{0,12},{4,8},{8,4},{12,0},{16,28},{20,24},{24,20},{28,16},{1,13},{... | collective-permute-start | bytes 221192 | tf_op jit(solution)/shard_map/ppermute | solution.py:16
  29.1 3.7 %collective-permute-start.7 = (bf16[1,96,384]{2,1,0:T(8,128)(2,1)S(1)}, bf16[1,96,384]{2,1,0:T(8,128)(2,1)S(1)}, u32[]{:S(2)}, u32[]{:S(2)}) collective-permute-start(bf16[1,96,384]{2,1,0:T(8,128)(2,1)S(1)} %get-tuple-element.13), channel_id=1, source_target_pairs={{0,8},{4,12},{8,0},{12,4},{16,24},{20,28},{24,16},{28,20},{1,9},{5... | collective-permute-start | bytes 221192 | tf_op jit(solution)/shard_map/ppermute | solution.py:16
  29.2 3.6 %collective-permute-start.8 = (bf16[1,96,384]{2,1,0:T(8,128)(2,1)S(1)}, bf16[1,96,384]{2,1,0:T(8,128)(2,1)S(1)}, u32[]{:S(2)}, u32[]{:S(2)}) collective-permute-start(bf16[1,96,384]{2,1,0:T(8,128)(2,1)S(1)} %get-tuple-element.14), channel_id=1, source_target_pairs={{0,4},{4,0},{8,12},{12,8},{16,20},{20,16},{24,28},{28,24},{1,5},{5... | collective-permute-start | bytes 221192 | tf_op jit(solution)/shard_map/ppermute | solution.py:16
  32.9 4.5 %collective-permute-start.9 = (bf16[1,96,384]{2,1,0:T(8,128)(2,1)S(1)}, bf16[1,96,384]{2,1,0:T(8,128)(2,1)S(1)}, u32[]{:S(2)}, u32[]{:S(2)}) collective-permute-start(bf16[1,96,384]{2,1,0:T(8,128)(2,1)S(1)} %add_convert_fusion.1), channel_id=1, source_target_pairs={{0,16},{4,20},{8,24},{12,28},{16,0},{20,4},{24,8},{28,12},{1,17},{... | collective-permute-start | bytes 221192 | tf_op jit(solution)/shard_map/ppermute | solution.py:16
  37.4 4.1 %collective-permute-start.10 = (bf16[1,96,384]{2,1,0:T(8,128)(2,1)S(1)}, bf16[1,96,384]{2,1,0:T(8,128)(2,1)S(1)}, u32[]{:S(2)}, u32[]{:S(2)}) collective-permute-start(bf16[1,96,384]{2,1,0:T(8,128)(2,1)S(1)} %add_convert_fusion.refs_0_), channel_id=1, source_target_pairs={{0,4},{4,0},{8,12},{12,8},{16,20},{20,16},{24,28},{28,24},{1,5},{5... | collective-permute-start | bytes 221192 | tf_op jit(solution)/shard_map/ppermute | solution.py:16
  39.6 3.2 %collective-permute-start.11 = (bf16[1,96,384]{2,1,0:T(8,128)(2,1)S(1)}, bf16[1,96,384]{2,1,0:T(8,128)(2,1)S(1)}, u32[]{:S(2)}, u32[]{:S(2)}) collective-permute-start(bf16[1,96,384]{2,1,0:T(8,128)(2,1)S(1)} %add_convert_fusion.refs_0_), channel_id=1, source_target_pairs={{0,8},{4,12},{8,0},{12,4},{16,24},{20,28},{24,16},{28,20},{1,9},{5... | collective-permute-start | bytes 221192 | tf_op jit(solution)/shard_map/ppermute | solution.py:16
  39.6 4.2 %collective-permute-start.12 = (bf16[1,96,384]{2,1,0:T(8,128)(2,1)S(1)}, bf16[1,96,384]{2,1,0:T(8,128)(2,1)S(1)}, u32[]{:S(2)}, u32[]{:S(2)}) collective-permute-start(bf16[1,96,384]{2,1,0:T(8,128)(2,1)S(1)} %add_convert_fusion.refs_0_), channel_id=1, source_target_pairs={{0,12},{4,8},{8,4},{12,0},{16,28},{20,24},{24,20},{28,16},{1,13},{... | collective-permute-start | bytes 221192 | tf_op jit(solution)/shard_map/ppermute | solution.py:16
  46.0 8.4 %collective-permute-start.15 = (bf16[112,384]{1,0:T(8,128)(2,1)S(1)}, bf16[112,384]{1,0:T(8,128)(2,1)S(1)}, u32[]{:S(2)}, u32[]{:S(2)}) collective-permute-start(bf16[112,384]{1,0:T(8,128)(2,1)S(1)} %get-tuple-element.18), channel_id=1, source_target_pairs={{0,3},{1,2},{2,1},{3,0},{4,7},{5,6},{6,5},{7,4},{8,11},{9,10},{10,... | collective-permute-start | bytes 258056 | tf_op jit(solution)/shard_map/ppermute | solution.py:16
  51.1 4.7 %collective-permute-start.13 = (bf16[112,384]{1,0:T(8,128)(2,1)S(1)}, bf16[112,384]{1,0:T(8,128)(2,1)S(1)}, u32[]{:S(2)}, u32[]{:S(2)}) collective-permute-start(bf16[112,384]{1,0:T(8,128)(2,1)S(1)} %get-tuple-element.16), channel_id=1, source_target_pairs={{0,1},{1,0},{2,3},{3,2},{4,5},{5,4},{6,7},{7,6},{8,9},{9,8},{10,11... | collective-permute-start | bytes 258056 | tf_op jit(solution)/shard_map/ppermute | solution.py:16
  51.1 4.7 %collective-permute-start.14 = (bf16[112,384]{1,0:T(8,128)(2,1)S(1)}, bf16[112,384]{1,0:T(8,128)(2,1)S(1)}, u32[]{:S(2)}, u32[]{:S(2)}) collective-permute-start(bf16[112,384]{1,0:T(8,128)(2,1)S(1)} %get-tuple-element.17), channel_id=1, source_target_pairs={{0,2},{1,3},{2,0},{3,1},{4,6},{5,7},{6,4},{7,5},{8,10},{9,11},{10,... | collective-permute-start | bytes 258056 | tf_op jit(solution)/shard_map/ppermute | solution.py:16

commit v2 on v0

v2 whole, which is shorter than its diff:
```python
import jax
import jax.numpy as jnp
from jax import lax
from jax.experimental import pallas as pl
from jax.experimental.pallas import tpu as pltpu
from jax.sharding import PartitionSpec as P

VMEM = pltpu.VMEM
SMEM = pltpu.SMEM
TILE = 16
PARAMS = pltpu.CompilerParams(vmem_limit_bytes=48 * 1024 * 1024)


def swapped(value, axis, mask):
    count = lax.axis_size(axis)
    return lax.ppermute(value, axis, [(source, source ^ mask) for source in range(count)])


def whole(count):
    return [pl.BlockSpec(memory_space=VMEM)] * count


def half_blocks(ints, block_ids, block_count, occ_pick, occ_coef, first, count, n_aux, n_pair):
    slots, width, _, aux_rows = ints.shape
    nocc = occ_coef.shape[2]
    n_half = n_aux // 2
    pairs = n_half // n_pair
    steps = width // TILE
    depth = TILE * width
    rows = 2 * pairs * count * width

    def kernel(ids_hbm, count_hbm, pick_hbm, occ_ref, ints_hbm, *refs):
        outs, (ids_ref, count_ref, pick_ref, held, small, large) = refs[:n_pair], refs[n_pair:]
        copies = []
        for at in range(count * steps):
            copy = pltpu.make_async_copy(
                ints_hbm.at[pl.ds((first * steps + at) * depth, depth), :],
                held.at[pl.ds(at * depth, depth), :],
                large.at[at],
            )
            copy.start()
            copies.append(copy)
        tables = [
            pltpu.make_async_copy(source, target, small.at[at])
            for at, (source, target) in enumerate(
                ((ids_hbm, ids_ref), (count_hbm, count_ref), (pick_hbm, pick_ref))
            )
        ]
        for copy in tables:
            copy.start()
        for copy in tables:
            copy.wait()
        pair_at = lax.axis_index("pair")
        lane = lax.broadcasted_iota(jnp.int32, (TILE, nocc), 1)
        chosen = []
        for mate in range(n_pair):
            for pair in range(pairs):
                for side in range(2):
                    orbital = pick_ref[(pair_at ^ mate) * pairs + pair + side * n_half]
                    chosen.append(jnp.where(lane == orbital, 1.0, 0.0))
        chosen = jnp.concatenate(chosen, axis=0).astype(jnp.bfloat16)
        shape = (n_aux * TILE, depth)
        diagonal = lax.broadcasted_iota(jnp.int32, shape, 0) % TILE == lax.broadcasted_iota(jnp.int32, shape, 1) // width
        row = lax.broadcasted_iota(jnp.int32, (TILE, aux_rows), 0)
        blocks = jnp.full((TILE, aux_rows), -1.0, jnp.float32)
        for slot in range(slots):
            block = jnp.where(slot < count_ref[0], ids_ref[0, slot], -1).astype(jnp.float32)
            blocks = jnp.where(row == slot, block, blocks)
        for out in outs:
            out[pl.ds(rows, TILE), :] = blocks.astype(jnp.bfloat16)
        for slot in range(count):
            table = occ_ref[ids_ref[1, first + slot]]
            table = jnp.concatenate([table] * (128 // width), axis=0)
            spread = lax.dot_general(chosen, table, (((1,), (1,)), ((), ())), preferred_element_type=jnp.float32)
            spread = jnp.concatenate([spread] * (depth // 128), axis=1)
            weights = jnp.where(diagonal, spread, 0.0).astype(jnp.bfloat16)
            for step in range(steps):
                at = slot * steps + step
                copies[at].wait()
                made = jnp.dot(weights, held[pl.ds(at * depth, depth), :], preferred_element_type=jnp.float32)
                made = made.astype(jnp.bfloat16)
                for mate in range(n_pair):
                    for orbital in range(2 * pairs):
                        source = (mate * 2 * pairs + orbital) * TILE
                        target = orbital * count * width + at * TILE
                        outs[mate][pl.ds(target, TILE), :] = made[source : source + TILE]

    anywhere = pl.BlockSpec(memory_space=pl.ANY)
    return pl.pallas_call(
        kernel,
        in_specs=[anywhere, anywhere, anywhere, pl.BlockSpec(memory_space=VMEM), anywhere],
        out_specs=whole(n_pair),
        out_shape=[jax.ShapeDtypeStruct((rows + TILE, aux_rows), jnp.bfloat16)] * n_pair,
        scratch_shapes=[
            SMEM((2, slots), jnp.int32),
            SMEM((1,), jnp.int32),
            SMEM((nocc,), jnp.int32),
            VMEM((count * width * width, aux_rows), jnp.bfloat16),
            pltpu.SemaphoreType.DMA((3,)),
            pltpu.SemaphoreType.DMA((count * steps,)),
        ],
        compiler_params=PARAMS,
        cost_estimate=pl.CostEstimate(
            flops=2 * n_aux * width * width * count * aux_rows,
            bytes_accessed=2 * count * width * width * aux_rows,
            transcendentals=0,
        ),
        name="half_blocks",
    )(block_ids.T, block_count, occ_pick, occ_coef, ints.reshape(-1, aux_rows))


def fitted_first(vir_coef, parts, pairs, counts):
    n_pair = len(parts)
    aux_rows = parts[0].shape[1]
    width, virtual = vir_coef.shape[1], vir_coef.shape[2]
    span = counts[0] * width

    def kernel(vir_ref, *refs):
        held, (fitted_ref, rest_ref, own_ref) = refs[:n_pair], refs[n_pair:]
        rows, later = [], []
        for part in held:
            tail = part[pl.ds(2 * pairs * span, TILE), :][:, :128].astype(jnp.float32)
            for slot in range(sum(counts)):
                block = tail[slot, 0].astype(jnp.int32)
                row = vir_ref[jnp.maximum(block, 0)]
                row = jnp.where(block >= 0, row, jnp.zeros_like(row))
                (rows if slot < counts[0] else later).append(row)
        own_ref[...] = jnp.concatenate(rows, axis=0).T
        rest_ref[...] = jnp.concatenate(later, axis=0).T
        for orbital in range(2 * pairs):
            blocks = jnp.concatenate([part[pl.ds(orbital * span, span), :] for part in held], axis=0)
            fitted_ref[orbital] = jnp.dot(own_ref[...], blocks, preferred_element_type=jnp.float32)

    return pl.pallas_call(
        kernel,
        in_specs=whole(1 + n_pair),
        out_specs=whole(2),
        out_shape=[
            jax.ShapeDtypeStruct((2 * pairs, virtual, aux_rows), jnp.float32),
            jax.ShapeDtypeStruct((virtual, n_pair * counts[1] * width), jnp.bfloat16),
        ],
        scratch_shapes=[VMEM((virtual, n_pair * span), jnp.bfloat16)],
        compiler_params=PARAMS,
        name="fitted_first",
    )(vir_coef, *parts)


def coulomb_parts(fitted, rest, parts, pairs, span, quad):
    n_pair = len(parts)
    virtual, aux_rows = fitted.shape[1:]
    share = virtual // quad

    def kernel(fitted_ref, rest_ref, *refs):
        held, outs, left_ref = refs[:n_pair], refs[n_pair:-1], refs[-1]
        place = lax.axis_index("aux") % quad
        for pair in range(pairs):
            sides = []
            for orbital in (2 * pair, 2 * pair + 1):
                blocks = jnp.concatenate([part[pl.ds(orbital * span, span), :] for part in held], axis=0)
                total = jnp.dot(rest_ref[...], blocks, preferred_element_type=jnp.float32)
                sides.append((fitted_ref[orbital] + total).astype(jnp.bfloat16))
            left_ref[...] = sides[0]
            for part, out in enumerate(outs):
                at = pl.multiple_of((place ^ part) * share, share)
                out[pair] = lax.dot_general(
                    left_ref[pl.ds(at, share), :],
                    sides[1],
                    (((1,), (1,)), ((), ())),
                    preferred_element_type=jnp.float32,
                ).astype(jnp.bfloat16)

    return pl.pallas_call(
        kernel,
        in_specs=whole(2 + n_pair),
        out_specs=whole(quad),
        out_shape=[jax.ShapeDtypeStruct((pairs, share, virtual), jnp.bfloat16)] * quad,
        scratch_shapes=[VMEM((virtual, aux_rows), jnp.bfloat16)],
        compiler_params=PARAMS,
        name="coulomb_parts",
    )(fitted, rest, *parts)


def density_parts(inverse, chunks, n_pair):
    quad = len(chunks)
    pairs, share, virtual = chunks[0].shape
    rows = virtual // n_pair

    def kernel(inverse_ref, *refs):
        held, own_ref, outs = refs[:quad], refs[quad], refs[quad + 1 : quad + n_pair]
        energy_ref, block_ref, even_ref, odd_ref = refs[quad + n_pair :]
        place = lax.axis_index("aux") % quad
        pair_at = lax.axis_index("pair")
        kind = lax.broadcasted_iota(jnp.int32, (TILE, virtual), 0)
        lane = lax.broadcasted_iota(jnp.int32, (TILE, virtual), 1)
        energies = jnp.zeros((TILE, virtual), jnp.float32)
        totals = [None] * n_pair
        for pair in range(pairs):
            for part in range(quad):
                at = pl.multiple_of((place ^ part) * share, share)
                block_ref[pl.ds(at, share), :] = held[part][pair].astype(jnp.float32)
            block = block_ref[...]
            flipped = block.T
            inverse = inverse_ref[pair]
            energy = jnp.sum(block * (2.0 * block - flipped) * inverse)
            even = ((block + flipped) * inverse).astype(jnp.bfloat16)
            odd = ((block - flipped) * inverse).astype(jnp.bfloat16)
            even_ref[...] = even
            odd_ref[...] = odd
            for part in range(n_pair):
                at = pl.multiple_of((pair_at ^ part) * rows, rows)
                term = 0.5 * jnp.dot(even_ref[pl.ds(at, rows), :], even, preferred_element_type=jnp.float32)
                term -= 1.5 * jnp.dot(odd_ref[pl.ds(at, rows), :], odd, preferred_element_type=jnp.float32)
                totals[part] = term if pair == 0 else totals[part] + term
            energies = jnp.where(lane == pair, energy, energies)
        own_ref[...] = totals[0]
        high = energies.astype(jnp.bfloat16)
        rest = energies - high.astype(jnp.float32)
        middle = rest.astype(jnp.bfloat16)
        low = (rest - middle.astype(jnp.float32)).astype(jnp.bfloat16)
        zero = jnp.zeros_like(high)
        packed = jnp.where(kind == 0, high, jnp.where(kind == 1, middle, jnp.where(kind == 2, low, zero)))
        energy_ref[...] = packed
        for part in range(1, n_pair):
            outs[part - 1][pl.ds(0, rows), :] = totals[part].astype(jnp.bfloat16)
            outs[part - 1][pl.ds(rows, TILE), :] = packed

    return pl.pallas_call(
        kernel,
        in_specs=whole(1 + quad),
        out_specs=whole(n_pair + 1),
        out_shape=[jax.ShapeDtypeStruct((rows, virtual), jnp.float32)]
        + [jax.ShapeDtypeStruct((rows + TILE, virtual), jnp.bfloat16)] * (n_pair - 1)
        + [jax.ShapeDtypeStruct((TILE, virtual), jnp.bfloat16)],
        scratch_shapes=[
            VMEM((virtual, virtual), jnp.float32),
            VMEM((virtual, virtual), jnp.bfloat16),
            VMEM((virtual, virtual), jnp.bfloat16),
        ],
        compiler_params=PARAMS,
        name="density_parts",
    )(inverse, *chunks)


def closing(own, energies, others, pairs, n_half):
    rows, virtual = own.shape

    def kernel(own_ref, energy_ref, *refs):
        held, (density_ref, value_ref) = refs[: len(others)], refs[len(others) :]
        wanted = lax.axis_index("aux") % n_half
        pair_at = lax.axis_index("pair")
        lane = lax.broadcasted_iota(jnp.int32, (TILE, virtual), 1)
        tails = [energy_ref[...]] + [ref[pl.ds(rows, TILE), :] for ref in held]
        found = jnp.zeros((TILE, virtual), jnp.float32)
        for mate, tail in enumerate(tails):
            at = wanted - (pair_at ^ mate) * pairs
            at = jnp.where((at >= 0) & (at < pairs), at, -1)
            found += jnp.where(lane == at, tail.astype(jnp.float32), 0.0)
        value_ref[0] = jnp.sum(found)
        total = own_ref[...]
        for ref in held:
            total += ref[pl.ds(0, rows), :].astype(jnp.float32)
        density_ref[...] = total

    return pl.pallas_call(
        kernel,
        in_specs=whole(2 + len(others)),
        out_specs=[pl.BlockSpec(memory_space=VMEM), pl.BlockSpec(memory_space=SMEM)],
        out_shape=[jax.ShapeDtypeStruct((rows, virtual), jnp.float32), jax.ShapeDtypeStruct((1,), jnp.float32)],
        compiler_params=PARAMS,
        name="closing",
    )(own, energies, *others)


def summed(value, axis, low, bits):
    if bits == 0:
        return value
    if bits == 1:
        other = swapped(value, axis, 1 << low)
        return (value.astype(jnp.float32) + other.astype(jnp.float32)).astype(jnp.bfloat16)
    place = (lax.axis_index(axis) >> low) & 3
    share = value.shape[1] // 4
    parts = [lax.dynamic_slice_in_dim(value, (place ^ d) * share, share, 1) for d in range(4)]
    chunks = scattered(parts, axis, low, bits)
    out = jnp.zeros_like(value)
    for d in range(4):
        out = lax.dynamic_update_slice_in_dim(out, chunks[d], (place ^ d) * share, 1)
    return out


def scattered(parts, axis, low, bits):
    total = parts[0].astype(jnp.float32)
    for d in range(1, len(parts)):
        total += swapped(parts[d], axis, d << low).astype(jnp.float32)
    total = summed(total.astype(jnp.bfloat16), axis, low + 2, bits - 2)
    return [total] + [swapped(total, axis, d << low) for d in range(1, len(parts))]


def per_device(
    shell_ints, block_ids, block_count, occ_coef, occ_pick, vir_coef, occ_energy, vir_energy
):
    _, slots, width, _ = shell_ints.shape
    n_aux = lax.axis_size("aux")
    n_pair = lax.axis_size("pair")
    n_half = n_aux // 2
    pairs = n_half // n_pair
    bits = n_aux.bit_length() - 1

    ints = jnp.transpose(shell_ints, (1, 2, 3, 0))
    counts = (slots // 2, slots - slots // 2)
    sent, got = [], []
    for first, count in ((0, counts[0]), (counts[0], counts[1])):
        made = half_blocks(ints, block_ids, block_count, occ_pick, occ_coef, first, count, n_aux, n_pair)
        sent.append(made)
        got.append([made[0]] + [swapped(made[d], "pair", d) for d in range(1, n_pair)])

    fitted, rest = fitted_first(vir_coef, got[0], pairs, counts)
    parts = coulomb_parts(fitted, rest, got[1], pairs, counts[1] * width, 4)

    occ_pick, occ_energy, vir_energy, _ = lax.optimization_barrier((occ_pick, occ_energy, vir_energy, sent[1][0]))
    own_pairs = lax.axis_index("pair") * pairs + jnp.arange(pairs, dtype=jnp.int32)
    spots = jnp.arange(n_aux, dtype=jnp.int32)
    batch = occ_pick[:n_aux]
    orbitals = jnp.arange(occ_energy.shape[0], dtype=jnp.int32)
    energies = jnp.sum(jnp.where(batch[:, None] == orbitals[None, :], occ_energy[None, :], 0.0), axis=1)
    levels = jnp.sum(jnp.where(own_pairs[:, None] == spots[None, :] % n_half, energies[None, :], 0.0), axis=1)
    inverse = 1.0 / (levels[:, None, None] - vir_energy[None, :, None] - vir_energy[None, None, :])

    chunks = scattered(parts, "aux", 0, bits)
    outs = density_parts(inverse, chunks, n_pair)
    others = [swapped(outs[d], "pair", d) for d in range(1, n_pair)]
    density, energy = closing(outs[0], outs[-1], others, pairs, n_half)
    return (energy, density)


def solution(mesh):
    placed = (P("aux", "pair", None, None), P("pair", None), P("pair"), P(), P(), P(), P(), P())
    return jax.shard_map(
        per_device,
        mesh=mesh,
        in_specs=placed,
        out_specs=(P("aux"), P("pair", None)),
        check_vma=False,
    )
```

time: 226 us -> 53.8 us (0.24); the launches traced: 223 us -> 53.3 us
  waiting for transfers between devices: 143 us -> 18.7 us
  blocking collectives: 42.4 us -> 0 us
  starting transfers between devices: 2.25 us -> 19.3 us
  between operations: 15.7 us -> 1.38 us
  matrix products: 10.1 us -> 0 us
  Pallas kernels: 0 us -> 9.77 us
  local copies, waits for them, and re-layouts: 5.05 us -> 2.59 us
    psum x2 -> x0, waiting for transfers between devices: 101 us -> none  [the longest x1 69.6 us: per_device(): vir_density = lax.psum(density_rows, 'aux')]
    all_to_all x1 -> x0, blocking collectives: 42.4 us -> none  [per_device(): lax.all_to_all(partial_value, 'aux', split_axis=1, concat_axis=0, tiled=T...]
    reduce_scatter x1 -> x0, waiting for transfers between devices: 28.5 us -> none  [per_device(): lax.psum_scatter(moved.astype(jnp.float32).astype(jnp.bfloat16), 'pair',...]
    ppermute x1 -> x16, starting transfers between devices: 2.13 us -> 19.3 us  [swapped(): lax.ppermute(value, axis, [(source, source ^ mask) for source in range(co...]
    dot_general x6 -> x0, matrix products: 10.1 us -> none  [the longest x1 4.81 us: per_device(): jnp.einsum('qkmn,kni->qikm', shell_ints, occ_sel, preferred_element_type=...]
    pallas_call x0 -> x6, Pallas kernels: none -> 9.77 us  [the longest x2 6.98 us: half_blocks(): pl.pallas_call(kernel, in_specs=[anywhere, anywhere, anywhere, pl.BlockSp...]
    ppermute x1 -> x16, waiting for transfers between devices: 13.8 us -> 18.7 us  [swapped(): lax.ppermute(value, axis, [(source, source ^ mask) for source in range(co...]
  transfers between devices with their start and end apart: 4 -> 16, of which waited for: 4 -> 11; matrix products, arithmetic and copies ran while one was open for 1% -> 3% of each run, Pallas kernels for 0% -> 7%
where the time goes in v2:
time: 53.8 us; the launch traced here: 53.3 us
  starting transfers between devices  19.3 us (36%)
  waiting for transfers between devices  18.7 us (35%)
  Pallas kernels  9.77 us (18%)
  local copies, waits for them, and re-layouts  2.59 us (5%)
  other arithmetic  1.64 us (3%)
  between operations  1.38 us (3%)
    ppermute x16, starting transfers between devices, swapped(): lax.ppermute(value, axis, [(source, source ^ mask) for source in range(co...  19.3 us
    ppermute x16, waiting for transfers between devices, swapped(): lax.ppermute(value, axis, [(source, source ^ mask) for source in range(co...  18.7 us
    pallas_call x2, Pallas kernels, half_blocks(): pl.pallas_call(kernel, in_specs=[anywhere, anywhere, anywhere, pl.BlockSp...  6.98 us
    unnamed x12, local copies, waits for them, and re-layouts  2.59 us
  transfers between devices with their start and end apart: 16, of which 11 were waited for; matrix products, arithmetic and copies ran while one was open for 3% of the time, Pallas kernels for 7%

profile of v2, /device:TPU:1, one launch (start us, length us, event | category | flops | bytes accessed | tf_op | source)
XLA Modules:
  0.0 53.3 jit_solution(6355658009132628489)
XLA Ops:
  1.3 1.2 %copy-done = bf16[16,64,512]{2,1,0:T(8,128)(2,1)S(1)} copy-done((bf16[16,64,512]{2,1,0:T(8,128)(2,1)S(1)}, bf16[16,64,512]{2,1,0:T(8,128)(2,1)}, u32[]{:S(2)}) %copy-start) | copy-done | bytes 1048600
  3.9 3.5 %half_blocks.3 = (bf16[272,256]{1,0:T(8,128)(2,1)S(1)}, bf16[272,256]{1,0:T(8,128)(2,1)S(1)}, bf16[272,256]{1,0:T(8,128)(2,1)S(1)}, bf16[272,256]{1,0:T(8,128)(2,1)S(1)}) custom-call(s32[2,4]{1,0:T(2,128)S(1)} %bitcast.4, s32[1]{0:T(128)S(6)} %copy.10.count_hbm, s32[512]{0:T(512)S(1)} %copy-done.2, bf16[16,64,512]{2,1,0:T(8,128)(2,1)S(1)} %copy-done, ...), custom_call_target="tpu_custom_call" | custom-call | flops 33554432 | bytes 4194304 | tf_op jit(solution)/shard_map/half_blocks/pallas_call | solution.py:89
  7.5 2.7 %collective-permute-start.1 = (bf16[272,256]{1,0:T(8,128)(2,1)S(1)}, bf16[272,256]{1,0:T(8,128)(2,1)S(1)}, u32[]{:S(2)}, u32[]{:S(2)}) collective-permute-start(bf16[272,256]{1,0:T(8,128)(2,1)S(1)} %get-tuple-element.32), channel_id=1, source_target_pairs={{0,2},{1,3},{2,0},{3,1},{4,6},{5,7},{6,4},{7,5},{8,10},{9,11},{10,... | collective-permute-start | bytes 417800 | tf_op jit(solution)/shard_map/ppermute | solution.py:16
  10.3 3.5 %half_blocks.2 = (bf16[272,256]{1,0:T(8,128)(2,1)S(1)}, bf16[272,256]{1,0:T(8,128)(2,1)S(1)}, bf16[272,256]{1,0:T(8,128)(2,1)S(1)}, bf16[272,256]{1,0:T(8,128)(2,1)S(1)}) custom-call(s32[2,4]{1,0:T(2,128)S(1)} %bitcast.5, s32[1]{0:T(128)S(6)} %copy.10.count_hbm, s32[512]{0:T(512)S(1)} %copy-done.2, bf16[16,64,512]{2,1,0:T(8,128)(2,1)S(1)} %copy-done, ...), custom_call_target="tpu_custom_call" | custom-call | flops 33554432 | bytes 4194304 | tf_op jit(solution)/shard_map/half_blocks/pallas_call | solution.py:89
  14.2 1.4 %collective-permute-start.4 = (bf16[272,256]{1,0:T(8,128)(2,1)S(1)}, bf16[272,256]{1,0:T(8,128)(2,1)S(1)}, u32[]{:S(2)}, u32[]{:S(2)}) collective-permute-start(bf16[272,256]{1,0:T(8,128)(2,1)S(1)} %get-tuple-element.37), channel_id=1, source_target_pairs={{0,2},{1,3},{2,0},{3,1},{4,6},{5,7},{6,4},{7,5},{8,10},{9,11},{10,... | collective-permute-start | bytes 417800 | tf_op jit(solution)/shard_map/ppermute | solution.py:16
  16.2 1.2 %collective-permute-done.2.refs_3_ = bf16[272,256]{1,0:T(8,128)(2,1)S(1)} collective-permute-done((bf16[272,256]{1,0:T(8,128)(2,1)S(1)}, bf16[272,256]{1,0:T(8,128)(2,1)S(1)}, u32[]{:S(2)}, u32[]{:S(2)}) %collective-permute-start.2) | collective-permute-done | bytes 139296 | tf_op jit(solution)/shard_map/ppermute | solution.py:16
  17.9 2.3 %collective-permute-done.4.refs_2_ = bf16[272,256]{1,0:T(8,128)(2,1)S(1)} collective-permute-done((bf16[272,256]{1,0:T(8,128)(2,1)S(1)}, bf16[272,256]{1,0:T(8,128)(2,1)S(1)}, u32[]{:S(2)}, u32[]{:S(2)}) %collective-permute-start.4) | collective-permute-done | bytes 139296 | tf_op jit(solution)/shard_map/ppermute | solution.py:16
  20.2 3.0 %collective-permute-done.5.refs_3_ = bf16[272,256]{1,0:T(8,128)(2,1)S(1)} collective-permute-done((bf16[272,256]{1,0:T(8,128)(2,1)S(1)}, bf16[272,256]{1,0:T(8,128)(2,1)S(1)}, u32[]{:S(2)}, u32[]{:S(2)}) %collective-permute-start.5) | collective-permute-done | bytes 139296 | tf_op jit(solution)/shard_map/ppermute | solution.py:16
  23.8 1.5 %collective-permute-start.6 = (bf16[1,96,384]{2,1,0:T(8,128)(2,1)S(1)}, bf16[1,96,384]{2,1,0:T(8,128)(2,1)S(1)}, u32[]{:S(2)}, u32[]{:S(2)}) collective-permute-start(bf16[1,96,384]{2,1,0:T(8,128)(2,1)S(1)} %get-tuple-element.40), channel_id=1, source_target_pairs={{0,4},{4,0},{8,12},{12,8},{16,20},{20,16},{24,28},{28,24},{1,5},{5... | collective-permute-start | bytes 221192 | tf_op jit(solution)/shard_map/ppermute | solution.py:16
  25.3 1.3 %collective-permute-start.7 = (bf16[1,96,384]{2,1,0:T(8,128)(2,1)S(1)}, bf16[1,96,384]{2,1,0:T(8,128)(2,1)S(1)}, u32[]{:S(2)}, u32[]{:S(2)}) collective-permute-start(bf16[1,96,384]{2,1,0:T(8,128)(2,1)S(1)} %get-tuple-element.41), channel_id=1, source_target_pairs={{0,8},{4,12},{8,0},{12,4},{16,24},{20,28},{24,16},{28,20},{1,9},{5... | collective-permute-start | bytes 221192 | tf_op jit(solution)/shard_map/ppermute | solution.py:16
  27.2 1.3 %collective-permute-done.7 = bf16[1,96,384]{2,1,0:T(8,128)(2,1)S(1)} collective-permute-done((bf16[1,96,384]{2,1,0:T(8,128)(2,1)S(1)}, bf16[1,96,384]{2,1,0:T(8,128)(2,1)S(1)}, u32[]{:S(2)}, u32[]{:S(2)}) %collective-permute-start.7) | collective-permute-done | bytes 73760 | tf_op jit(solution)/shard_map/ppermute | solution.py:16
  28.5 2.2 %collective-permute-done.8 = bf16[1,96,384]{2,1,0:T(8,128)(2,1)S(1)} collective-permute-done((bf16[1,96,384]{2,1,0:T(8,128)(2,1)S(1)}, bf16[1,96,384]{2,1,0:T(8,128)(2,1)S(1)}, u32[]{:S(2)}, u32[]{:S(2)}) %collective-permute-start.8) | collective-permute-done | bytes 73760 | tf_op jit(solution)/shard_map/ppermute | solution.py:16
  30.8 2.4 %collective-permute-start.9 = (bf16[1,96,384]{2,1,0:T(8,128)(2,1)S(1)}, bf16[1,96,384]{2,1,0:T(8,128)(2,1)S(1)}, u32[]{:S(2)}, u32[]{:S(2)}) collective-permute-start(bf16[1,96,384]{2,1,0:T(8,128)(2,1)S(1)} %add_convert_fusion.1), channel_id=1, source_target_pairs={{0,16},{4,20},{8,24},{12,28},{16,0},{20,4},{24,8},{28,12},{1,17},{... | collective-permute-start | bytes 221192 | tf_op jit(solution)/shard_map/ppermute | solution.py:16
  33.8 1.1 %collective-permute-done.9 = bf16[1,96,384]{2,1,0:T(8,128)(2,1)S(1)} collective-permute-done((bf16[1,96,384]{2,1,0:T(8,128)(2,1)S(1)}, bf16[1,96,384]{2,1,0:T(8,128)(2,1)S(1)}, u32[]{:S(2)}, u32[]{:S(2)}) %collective-permute-start.9) | collective-permute-done | bytes 73760 | tf_op jit(solution)/shard_map/ppermute | solution.py:16
  35.0 1.6 %collective-permute-start.10 = (bf16[1,96,384]{2,1,0:T(8,128)(2,1)S(1)}, bf16[1,96,384]{2,1,0:T(8,128)(2,1)S(1)}, u32[]{:S(2)}, u32[]{:S(2)}) collective-permute-start(bf16[1,96,384]{2,1,0:T(8,128)(2,1)S(1)} %add_convert_fusion.refs_0_), channel_id=1, source_target_pairs={{0,4},{4,0},{8,12},{12,8},{16,20},{20,16},{24,28},{28,24},{1,5},{5... | collective-permute-start | bytes 221192 | tf_op jit(solution)/shard_map/ppermute | solution.py:16
  37.0 0.8 %collective-permute-start.12 = (bf16[1,96,384]{2,1,0:T(8,128)(2,1)S(1)}, bf16[1,96,384]{2,1,0:T(8,128)(2,1)S(1)}, u32[]{:S(2)}, u32[]{:S(2)}) collective-permute-start(bf16[1,96,384]{2,1,0:T(8,128)(2,1)S(1)} %add_convert_fusion.refs_0_), channel_id=1, source_target_pairs={{0,12},{4,8},{8,4},{12,0},{16,28},{20,24},{24,20},{28,16},{1,13},{... | collective-permute-start | bytes 221192 | tf_op jit(solution)/shard_map/ppermute | solution.py:16
  38.4 1.4 %collective-permute-done.11.refs_2_ = bf16[1,96,384]{2,1,0:T(8,128)(2,1)S(1)} collective-permute-done((bf16[1,96,384]{2,1,0:T(8,128)(2,1)S(1)}, bf16[1,96,384]{2,1,0:T(8,128)(2,1)S(1)}, u32[]{:S(2)}, u32[]{:S(2)}) %collective-permute-start.11) | collective-permute-done | bytes 73760 | tf_op jit(solution)/shard_map/ppermute | solution.py:16
  39.8 1.3 %collective-permute-done.12.refs_3_ = bf16[1,96,384]{2,1,0:T(8,128)(2,1)S(1)} collective-permute-done((bf16[1,96,384]{2,1,0:T(8,128)(2,1)S(1)}, bf16[1,96,384]{2,1,0:T(8,128)(2,1)S(1)}, u32[]{:S(2)}, u32[]{:S(2)}) %collective-permute-start.12) | collective-permute-done | bytes 73760 | tf_op jit(solution)/shard_map/ppermute | solution.py:16
  41.1 0.9 %density_parts.1 = (f32[96,384]{1,0:T(8,128)S(1)}, bf16[112,384]{1,0:T(8,128)(2,1)S(1)}, bf16[112,384]{1,0:T(8,128)(2,1)S(1)}, bf16[112,384]{1,0:T(8,128)(2,1)S(1)}, bf16[16,384]{1,0:T(8,128)(2,1)S(1)}) custom-call(f32[1,384,384]{2,1,0:T(8,128)S(1)} %subtract_divide_fusion.inverse_ref, bf16[1,96,384]{2,1,0:T(8,128)(2,1)S(1)} %add_convert_fusion.refs_0_, ...), custom_call_target="tpu_custom_call" | custom-call | tf_op jit(solution)/shard_map/density_parts/pallas_call | solution.py:227
  42.0 4.5 %collective-permute-start.13 = (bf16[112,384]{1,0:T(8,128)(2,1)S(1)}, bf16[112,384]{1,0:T(8,128)(2,1)S(1)}, u32[]{:S(2)}, u32[]{:S(2)}) collective-permute-start(bf16[112,384]{1,0:T(8,128)(2,1)S(1)} %get-tuple-element.45), channel_id=1, source_target_pairs={{0,1},{1,0},{2,3},{3,2},{4,5},{5,4},{6,7},{7,6},{8,9},{9,8},{10,11... | collective-permute-start | bytes 258056 | tf_op jit(solution)/shard_map/ppermute | solution.py:16
  46.5 1.3 %collective-permute-start.14 = (bf16[112,384]{1,0:T(8,128)(2,1)S(1)}, bf16[112,384]{1,0:T(8,128)(2,1)S(1)}, u32[]{:S(2)}, u32[]{:S(2)}) collective-permute-start(bf16[112,384]{1,0:T(8,128)(2,1)S(1)} %get-tuple-element.46), channel_id=1, source_target_pairs={{0,2},{1,3},{2,0},{3,1},{4,6},{5,7},{6,4},{7,5},{8,10},{9,11},{10,... | collective-permute-start | bytes 258056 | tf_op jit(solution)/shard_map/ppermute | solution.py:16
  48.2 2.4 %collective-permute-done.14.refs_1_ = bf16[112,384]{1,0:T(8,128)(2,1)S(1)} collective-permute-done((bf16[112,384]{1,0:T(8,128)(2,1)S(1)}, bf16[112,384]{1,0:T(8,128)(2,1)S(1)}, u32[]{:S(2)}, u32[]{:S(2)}) %collective-permute-start.14) | collective-permute-done | bytes 86048 | tf_op jit(solution)/shard_map/ppermute | solution.py:16
  50.6 2.0 %collective-permute-done.15.refs_2_ = bf16[112,384]{1,0:T(8,128)(2,1)S(1)} collective-permute-done((bf16[112,384]{1,0:T(8,128)(2,1)S(1)}, bf16[112,384]{1,0:T(8,128)(2,1)S(1)}, u32[]{:S(2)}, u32[]{:S(2)}) %collective-permute-start.15) | collective-permute-done | bytes 86048 | tf_op jit(solution)/shard_map/ppermute | solution.py:16
  52.6 0.7 %closing.1 = (f32[96,384]{1,0:T(8,128)}, f32[1]{0:T(128)}) custom-call(f32[96,384]{1,0:T(8,128)S(1)} %get-tuple-element.43.own_ref, bf16[16,384]{1,0:T(8,128)(2,1)S(1)} %get-tuple-element.44.energy_ref, bf16[112,384]{1,0:T(8,128)(2,1)S(1)} %collective-permute-done.13.refs_0_, bf16[112,384]{1,0:T(8,128)(2,1)S(1)} %collective-permute-done.14.refs_1_, ...), custom_call_target="tpu_custom_call" | custom-call | tf_op jit(solution)/shard_map/closing/pallas_call | solution.py:264
  (34 shorter events, 6.4 us)
Async XLA Ops:
  1.3 1.2 %copy-start = (bf16[16,64,512]{2,1,0:T(8,128)(2,1)S(1)}, bf16[16,64,512]{2,1,0:T(8,128)(2,1)}, u32[]{:S(2)}) copy-start(bf16[16,64,512]{2,1,0:T(8,128)(2,1)} %occ_ref.3) | copy-start | bytes 3145732
  2.5 0.7 %copy-start.2 = (s32[512]{0:T(512)S(1)}, s32[512]{0:T(512)}, u32[]{:S(2)}) copy-start(s32[512]{0:T(512)} %pick_hbm.3) | copy-start | bytes 6148
  3.2 0.7 %copy-start.3 = (s32[4,2]{0,1:T(2,128)S(1)}, s32[4,2]{0,1:T(2,128)}, u32[]{:S(2)}) copy-start(s32[4,2]{0,1:T(2,128)} %param.9) | copy-start | bytes 100
  3.9 12.1 %slice-start = ((s32[512]{0:T(512)}), s32[8]{0:T(128)S(1)}, s32[]{:S(2)}) async-start(s32[512]{0:T(512)} %pick_hbm.3), calls=%async_computation | async-start | bytes 1024 | tf_op jit(solution)/shard_map/slice | solution.py:322
  3.9 12.1 %copy-start.5 = (f32[512]{0:T(512)S(1)}, f32[512]{0:T(512)}, u32[]{:S(2)}) copy-start(f32[512]{0:T(512)} %param.14) | copy-start | bytes 6148
  3.9 13.5 %copy-start.1 = (bf16[16,64,384]{2,1,0:T(8,128)(2,1)S(1)}, bf16[16,64,384]{2,1,0:T(8,128)(2,1)}, u32[]{:S(2)}) copy-start(bf16[16,64,384]{2,1,0:T(8,128)(2,1)} %vir_ref.1) | copy-start | bytes 2359300
  7.4 25.7 %copy-start.4 = (f32[384]{0:T(512)S(1)}, f32[384]{0:T(512)}, u32[]{:S(2)}) copy-start(f32[384]{0:T(512)} %param.15) | copy-start | bytes 4612
  7.4 8.2 %collective-permute-start = (bf16[272,256]{1,0:T(8,128)(2,1)S(1)}, bf16[272,256]{1,0:T(8,128)(2,1)S(1)}, u32[]{:S(2)}, u32[]{:S(2)}) collective-permute-start(bf16[272,256]{1,0:T(8,128)(2,1)S(1)} %get-tuple-element.31), channel_id=1, source_target_pairs={{0,1},{1,0},{2,3},{3,2},{4,5},{5,4},{6,7},{7,6},{8,9},{9,8},{10,11... | collective-permute-start | bytes 417800 | tf_op jit(solution)/shard_map/ppermute | solution.py:16
  7.5 8.6 %collective-permute-start.1 = (bf16[272,256]{1,0:T(8,128)(2,1)S(1)}, bf16[272,256]{1,0:T(8,128)(2,1)S(1)}, u32[]{:S(2)}, u32[]{:S(2)}) collective-permute-start(bf16[272,256]{1,0:T(8,128)(2,1)S(1)} %get-tuple-element.32), channel_id=1, source_target_pairs={{0,2},{1,3},{2,0},{3,1},{4,6},{5,7},{6,4},{7,5},{8,10},{9,11},{10,... | collective-permute-start | bytes 417800 | tf_op jit(solution)/shard_map/ppermute | solution.py:16
  10.2 7.2 %collective-permute-start.2 = (bf16[272,256]{1,0:T(8,128)(2,1)S(1)}, bf16[272,256]{1,0:T(8,128)(2,1)S(1)}, u32[]{:S(2)}, u32[]{:S(2)}) collective-permute-start(bf16[272,256]{1,0:T(8,128)(2,1)S(1)} %get-tuple-element.33), channel_id=1, source_target_pairs={{0,3},{1,2},{2,1},{3,0},{4,7},{5,6},{6,5},{7,4},{8,11},{9,10},{10,... | collective-permute-start | bytes 417800 | tf_op jit(solution)/shard_map/ppermute | solution.py:16
  13.7 4.1 %collective-permute-start.3 = (bf16[272,256]{1,0:T(8,128)(2,1)S(1)}, bf16[272,256]{1,0:T(8,128)(2,1)S(1)}, u32[]{:S(2)}, u32[]{:S(2)}) collective-permute-start(bf16[272,256]{1,0:T(8,128)(2,1)S(1)} %get-tuple-element.36), channel_id=1, source_target_pairs={{0,1},{1,0},{2,3},{3,2},{4,5},{5,4},{6,7},{7,6},{8,9},{9,8},{10,11... | collective-permute-start | bytes 417800 | tf_op jit(solution)/shard_map/ppermute | solution.py:16
  14.2 6.0 %collective-permute-start.4 = (bf16[272,256]{1,0:T(8,128)(2,1)S(1)}, bf16[272,256]{1,0:T(8,128)(2,1)S(1)}, u32[]{:S(2)}, u32[]{:S(2)}) collective-permute-start(bf16[272,256]{1,0:T(8,128)(2,1)S(1)} %get-tuple-element.37), channel_id=1, source_target_pairs={{0,2},{1,3},{2,0},{3,1},{4,6},{5,7},{6,4},{7,5},{8,10},{9,11},{10,... | collective-permute-start | bytes 417800 | tf_op jit(solution)/shard_map/ppermute | solution.py:16
  15.6 7.5 %collective-permute-start.5 = (bf16[272,256]{1,0:T(8,128)(2,1)S(1)}, bf16[272,256]{1,0:T(8,128)(2,1)S(1)}, u32[]{:S(2)}, u32[]{:S(2)}) collective-permute-start(bf16[272,256]{1,0:T(8,128)(2,1)S(1)} %get-tuple-element.38), channel_id=1, source_target_pairs={{0,3},{1,2},{2,1},{3,0},{4,7},{5,6},{6,5},{7,4},{8,11},{9,10},{10,... | collective-permute-start | bytes 417800 | tf_op jit(solution)/shard_map/ppermute | solution.py:16
  23.8 3.4 %collective-permute-start.6 = (bf16[1,96,384]{2,1,0:T(8,128)(2,1)S(1)}, bf16[1,96,384]{2,1,0:T(8,128)(2,1)S(1)}, u32[]{:S(2)}, u32[]{:S(2)}) collective-permute-start(bf16[1,96,384]{2,1,0:T(8,128)(2,1)S(1)} %get-tuple-element.40), channel_id=1, source_target_pairs={{0,4},{4,0},{8,12},{12,8},{16,20},{20,16},{24,28},{28,24},{1,5},{5... | collective-permute-start | bytes 221192 | tf_op jit(solution)/shard_map/ppermute | solution.py:16
  25.3 3.2 %collective-permute-start.7 = (bf16[1,96,384]{2,1,0:T(8,128)(2,1)S(1)}, bf16[1,96,384]{2,1,0:T(8,128)(2,1)S(1)}, u32[]{:S(2)}, u32[]{:S(2)}) collective-permute-start(bf16[1,96,384]{2,1,0:T(8,128)(2,1)S(1)} %get-tuple-element.41), channel_id=1, source_target_pairs={{0,8},{4,12},{8,0},{12,4},{16,24},{20,28},{24,16},{28,20},{1,9},{5... | collective-permute-start | bytes 221192 | tf_op jit(solution)/shard_map/ppermute | solution.py:16
  26.6 4.1 %collective-permute-start.8 = (bf16[1,96,384]{2,1,0:T(8,128)(2,1)S(1)}, bf16[1,96,384]{2,1,0:T(8,128)(2,1)S(1)}, u32[]{:S(2)}, u32[]{:S(2)}) collective-permute-start(bf16[1,96,384]{2,1,0:T(8,128)(2,1)S(1)} %get-tuple-element.42), channel_id=1, source_target_pairs={{0,12},{4,8},{8,4},{12,0},{16,28},{20,24},{24,20},{28,16},{1,13},{... | collective-permute-start | bytes 221192 | tf_op jit(solution)/shard_map/ppermute | solution.py:16
  30.8 4.2 %collective-permute-start.9 = (bf16[1,96,384]{2,1,0:T(8,128)(2,1)S(1)}, bf16[1,96,384]{2,1,0:T(8,128)(2,1)S(1)}, u32[]{:S(2)}, u32[]{:S(2)}) collective-permute-start(bf16[1,96,384]{2,1,0:T(8,128)(2,1)S(1)} %add_convert_fusion.1), channel_id=1, source_target_pairs={{0,16},{4,20},{8,24},{12,28},{16,0},{20,4},{24,8},{28,12},{1,17},{... | collective-permute-start | bytes 221192 | tf_op jit(solution)/shard_map/ppermute | solution.py:16
  35.0 3.5 %collective-permute-start.10 = (bf16[1,96,384]{2,1,0:T(8,128)(2,1)S(1)}, bf16[1,96,384]{2,1,0:T(8,128)(2,1)S(1)}, u32[]{:S(2)}, u32[]{:S(2)}) collective-permute-start(bf16[1,96,384]{2,1,0:T(8,128)(2,1)S(1)} %add_convert_fusion.refs_0_), channel_id=1, source_target_pairs={{0,4},{4,0},{8,12},{12,8},{16,20},{20,16},{24,28},{28,24},{1,5},{5... | collective-permute-start | bytes 221192 | tf_op jit(solution)/shard_map/ppermute | solution.py:16
  36.6 3.2 %collective-permute-start.11 = (bf16[1,96,384]{2,1,0:T(8,128)(2,1)S(1)}, bf16[1,96,384]{2,1,0:T(8,128)(2,1)S(1)}, u32[]{:S(2)}, u32[]{:S(2)}) collective-permute-start(bf16[1,96,384]{2,1,0:T(8,128)(2,1)S(1)} %add_convert_fusion.refs_0_), channel_id=1, source_target_pairs={{0,8},{4,12},{8,0},{12,4},{16,24},{20,28},{24,16},{28,20},{1,9},{5... | collective-permute-start | bytes 221192 | tf_op jit(solution)/shard_map/ppermute | solution.py:16
  37.0 4.1 %collective-permute-start.12 = (bf16[1,96,384]{2,1,0:T(8,128)(2,1)S(1)}, bf16[1,96,384]{2,1,0:T(8,128)(2,1)S(1)}, u32[]{:S(2)}, u32[]{:S(2)}) collective-permute-start(bf16[1,96,384]{2,1,0:T(8,128)(2,1)S(1)} %add_convert_fusion.refs_0_), channel_id=1, source_target_pairs={{0,12},{4,8},{8,4},{12,0},{16,28},{20,24},{24,20},{28,16},{1,13},{... | collective-permute-start | bytes 221192 | tf_op jit(solution)/shard_map/ppermute | solution.py:16
  42.0 6.2 %collective-permute-start.13 = (bf16[112,384]{1,0:T(8,128)(2,1)S(1)}, bf16[112,384]{1,0:T(8,128)(2,1)S(1)}, u32[]{:S(2)}, u32[]{:S(2)}) collective-permute-start(bf16[112,384]{1,0:T(8,128)(2,1)S(1)} %get-tuple-element.45), channel_id=1, source_target_pairs={{0,1},{1,0},{2,3},{3,2},{4,5},{5,4},{6,7},{7,6},{8,9},{9,8},{10,11... | collective-permute-start | bytes 258056 | tf_op jit(solution)/shard_map/ppermute | solution.py:16
  46.5 4.1 %collective-permute-start.14 = (bf16[112,384]{1,0:T(8,128)(2,1)S(1)}, bf16[112,384]{1,0:T(8,128)(2,1)S(1)}, u32[]{:S(2)}, u32[]{:S(2)}) collective-permute-start(bf16[112,384]{1,0:T(8,128)(2,1)S(1)} %get-tuple-element.46), channel_id=1, source_target_pairs={{0,2},{1,3},{2,0},{3,1},{4,6},{5,7},{6,4},{7,5},{8,10},{9,11},{10,... | collective-permute-start | bytes 258056 | tf_op jit(solution)/shard_map/ppermute | solution.py:16
  47.8 4.9 %collective-permute-start.15 = (bf16[112,384]{1,0:T(8,128)(2,1)S(1)}, bf16[112,384]{1,0:T(8,128)(2,1)S(1)}, u32[]{:S(2)}, u32[]{:S(2)}) collective-permute-start(bf16[112,384]{1,0:T(8,128)(2,1)S(1)} %get-tuple-element.47), channel_id=1, source_target_pairs={{0,3},{1,2},{2,1},{3,0},{4,7},{5,6},{6,5},{7,4},{8,11},{9,10},{10,... | collective-permute-start | bytes 258056 | tf_op jit(solution)/shard_map/ppermute | solution.py:16

commit v3 on v2

v3 whole, which is shorter than its diff:
```python
import jax
import jax.numpy as jnp
from jax import lax
from jax.experimental import pallas as pl
from jax.experimental.pallas import tpu as pltpu
from jax.sharding import PartitionSpec as P

VMEM = pltpu.VMEM
SMEM = pltpu.SMEM
TILE = 16
SUB = 8
PARAMS = pltpu.CompilerParams(vmem_limit_bytes=48 * 1024 * 1024)


def order(count):
    return sorted(range(1, count), reverse=True)


def swapped(value, axis, mask):
    count = lax.axis_size(axis)
    return lax.ppermute(value, axis, [(source, source ^ mask) for source in range(count)])


def in_hbm(*values):
    return [pltpu.with_memory_space_constraint(value, pltpu.HBM) for value in values]


def whole(count):
    return [pl.BlockSpec(memory_space=VMEM)] * count


def half_blocks(ints, block_ids, block_count, occ_pick, occ_coef, n_aux, n_pair):
    slots, width, _, aux_rows = ints.shape
    nocc = occ_coef.shape[2]
    n_half = n_aux // 2
    pairs = n_half // n_pair
    rows = 2 * pairs * slots * width

    def kernel(count_ref, ids_hbm, pick_hbm, occ_hbm, ints_hbm, *refs):
        outs, (ids_ref, pick_ref, occ_ref, held, small, large) = refs[:n_pair], refs[n_pair:]
        tables = [
            pltpu.make_async_copy(source, target, small.at[at])
            for at, (source, target) in enumerate(((ids_hbm, ids_ref), (pick_hbm, pick_ref), (occ_hbm, occ_ref)))
        ]
        for copy in tables:
            copy.start()
        copies = started(ints_hbm, held, large, slots, width * width)
        for copy in tables:
            copy.wait()
        pair_at = lax.axis_index("pair")
        lane = lax.broadcasted_iota(jnp.int32, (SUB, nocc), 1)
        chosen = []
        for mate in range(n_pair):
            for pair in range(pairs):
                for side in range(2):
                    orbital = pick_ref[(pair_at ^ mate) * pairs + pair + side * n_half]
                    chosen.append(jnp.where(lane == orbital, 1.0, 0.0))
        chosen = jnp.concatenate(chosen, axis=0).astype(jnp.bfloat16)
        row = lax.broadcasted_iota(jnp.int32, (TILE, aux_rows), 0)
        blocks = jnp.full((TILE, aux_rows), -1.0, jnp.float32)
        for slot in range(slots):
            block = jnp.where(slot < count_ref[0], ids_ref[0, slot], -1).astype(jnp.float32)
            blocks = jnp.where(row == slot, block, blocks)
        for out in outs:
            out[pl.ds(rows, TILE), :] = blocks.astype(jnp.bfloat16)
        weights = [slot_weights(chosen, occ_ref[ids_ref[1, slot]]) for slot in range(slots)]
        for slot in range(slots):
            copies[slot].wait()
            halves(weights[slot], held, outs, slot, slots, width, pairs)

    return pl.pallas_call(
        kernel,
        in_specs=[pl.BlockSpec(memory_space=SMEM)] + [pl.BlockSpec(memory_space=pltpu.HBM)] * 4,
        out_specs=whole(n_pair),
        out_shape=[jax.ShapeDtypeStruct((rows + TILE, aux_rows), jnp.bfloat16)] * n_pair,
        scratch_shapes=[
            SMEM((2, slots), jnp.int32),
            SMEM((nocc,), jnp.int32),
            VMEM(occ_coef.shape, jnp.bfloat16),
            VMEM((slots * width * width, aux_rows), jnp.bfloat16),
            pltpu.SemaphoreType.DMA((3,)),
            pltpu.SemaphoreType.DMA((slots,)),
        ],
        compiler_params=PARAMS,
        name="half_blocks",
    )(block_count, *in_hbm(block_ids.T, occ_pick, occ_coef, ints.reshape(-1, aux_rows)))


def started(ints_hbm, held, sems, count, rows):
    copies = []
    for slot in range(count):
        span = pl.ds(slot * rows, rows)
        copies.append(pltpu.make_async_copy(ints_hbm.at[span, :], held.at[span, :], sems.at[slot]))
        copies[-1].start()
    return copies


def slot_weights(chosen, table):
    width = table.shape[0]
    table = jnp.concatenate([table] * (128 // width), axis=0)
    spread = lax.dot_general(chosen, table, (((1,), (1,)), ((), ())), preferred_element_type=jnp.float32)
    spread = jnp.concatenate([spread] * (SUB * width // 128), axis=1)
    row = lax.broadcasted_iota(jnp.int32, spread.shape, 0)
    column = lax.broadcasted_iota(jnp.int32, spread.shape, 1)
    return jnp.where(row % SUB == column // width, spread, 0.0).astype(jnp.bfloat16)


def halves(weights, ints, outs, slot, count, width, pairs):
    depth = SUB * width
    for step in range(width // TILE):
        at = slot * (width // TILE) + step
        made = [
            jnp.dot(weights, ints[pl.ds((2 * at + part) * depth, depth), :], preferred_element_type=jnp.float32)
            for part in range(2)
        ]
        for mate, out in enumerate(outs):
            for orbital in range(2 * pairs):
                source = (mate * 2 * pairs + orbital) * SUB
                both = jnp.concatenate([part[source : source + SUB] for part in made], axis=0)
                out[pl.ds(orbital * count * width + at * TILE, TILE), :] = both.astype(jnp.bfloat16)


def virtual_rows(vir_ref, parts, slots, span):
    rows = []
    for part in parts:
        tail = part[pl.ds(span, TILE), :][:, :128].astype(jnp.float32)
        for slot in range(slots):
            block = tail[slot, 0].astype(jnp.int32)
            row = vir_ref[jnp.maximum(block, 0)]
            rows.append(jnp.where(block >= 0, row, jnp.zeros_like(row)))
    return jnp.concatenate(rows, axis=0).T


def fitted_rows(virtuals, parts, orbital, span):
    blocks = jnp.concatenate([part[pl.ds(orbital * span, span), :] for part in parts], axis=0)
    return jnp.dot(virtuals, blocks, preferred_element_type=jnp.float32)


def fitted_first(vir_coef, parts, pairs, slots):
    aux_rows = parts[0].shape[1]
    width, virtual = vir_coef.shape[1], vir_coef.shape[2]
    span = slots * width

    def kernel(vir_ref, *refs):
        held, fitted_ref, rows_ref = refs[:-2], refs[-2], refs[-1]
        rows_ref[...] = virtual_rows(vir_ref, held, slots, 2 * pairs * span)
        for orbital in range(2 * pairs):
            fitted_ref[orbital] = fitted_rows(rows_ref[...], held, orbital, span)

    return pl.pallas_call(
        kernel,
        in_specs=whole(1 + len(parts)),
        out_specs=pl.BlockSpec(memory_space=VMEM),
        out_shape=jax.ShapeDtypeStruct((2 * pairs, virtual, aux_rows), jnp.float32),
        scratch_shapes=[VMEM((virtual, len(parts) * span), jnp.bfloat16)],
        compiler_params=PARAMS,
        name="fitted_first",
    )(vir_coef, *parts)


def coulomb_parts(fitted, vir_coef, parts, slots, quad):
    pairs = fitted.shape[0] // 2
    virtual, aux_rows = fitted.shape[1:]
    span = slots * vir_coef.shape[1]
    share = virtual // quad

    def kernel(fitted_ref, vir_ref, *refs):
        held, outs, (left_ref, rows_ref) = refs[: len(parts)], refs[len(parts) : -2], refs[-2:]
        place = lax.axis_index("aux") % quad
        rows_ref[...] = virtual_rows(vir_ref, held, slots, 2 * pairs * span)
        for pair in range(pairs):
            sides = []
            for orbital in (2 * pair, 2 * pair + 1):
                total = fitted_ref[orbital] + fitted_rows(rows_ref[...], held, orbital, span)
                sides.append(total.astype(jnp.bfloat16))
            left_ref[...] = sides[0]
            for part, out in enumerate(outs):
                at = pl.multiple_of((place ^ part) * share, share)
                out[pair] = lax.dot_general(
                    left_ref[pl.ds(at, share), :],
                    sides[1],
                    (((1,), (1,)), ((), ())),
                    preferred_element_type=jnp.float32,
                ).astype(jnp.bfloat16)

    return pl.pallas_call(
        kernel,
        in_specs=whole(2 + len(parts)),
        out_specs=whole(quad),
        out_shape=[jax.ShapeDtypeStruct((pairs, share, virtual), jnp.bfloat16)] * quad,
        scratch_shapes=[
            VMEM((virtual, aux_rows), jnp.bfloat16),
            VMEM((virtual, len(parts) * span), jnp.bfloat16),
        ],
        compiler_params=PARAMS,
        name="coulomb_parts",
    )(fitted, vir_coef, *parts)


def density_parts(inverse, chunks, n_pair):
    quad = len(chunks)
    pairs, share, virtual = chunks[0].shape
    rows = virtual // n_pair

    def kernel(inverse_ref, *refs):
        held, own_ref, outs = refs[:quad], refs[quad], refs[quad + 1 : quad + n_pair]
        energy_ref, block_ref, even_ref, odd_ref = refs[quad + n_pair :]
        place = lax.axis_index("aux") % quad
        pair_at = lax.axis_index("pair")
        kind = lax.broadcasted_iota(jnp.int32, (TILE, virtual), 0)
        lane = lax.broadcasted_iota(jnp.int32, (TILE, virtual), 1)
        energies = jnp.zeros((TILE, virtual), jnp.float32)
        totals = [None] * n_pair
        for pair in range(pairs):
            for part in range(quad):
                at = pl.multiple_of((place ^ part) * share, share)
                block_ref[pl.ds(at, share), :] = held[part][pair].astype(jnp.float32)
            block = block_ref[...]
            flipped = block.T
            inverse = inverse_ref[pair]
            energy = jnp.sum(block * (2.0 * block - flipped) * inverse)
            even = ((block + flipped) * inverse).astype(jnp.bfloat16)
            odd = ((block - flipped) * inverse).astype(jnp.bfloat16)
            even_ref[...] = even
            odd_ref[...] = odd
            for part in range(n_pair):
                at = pl.multiple_of((pair_at ^ part) * rows, rows)
                term = 0.5 * jnp.dot(even_ref[pl.ds(at, rows), :], even, preferred_element_type=jnp.float32)
                term -= 1.5 * jnp.dot(odd_ref[pl.ds(at, rows), :], odd, preferred_element_type=jnp.float32)
                totals[part] = term if pair == 0 else totals[part] + term
            energies = jnp.where(lane == pair, energy, energies)
        own_ref[...] = totals[0]
        high = energies.astype(jnp.bfloat16)
        rest = energies - high.astype(jnp.float32)
        middle = rest.astype(jnp.bfloat16)
        low = (rest - middle.astype(jnp.float32)).astype(jnp.bfloat16)
        zero = jnp.zeros_like(high)
        packed = jnp.where(kind == 0, high, jnp.where(kind == 1, middle, jnp.where(kind == 2, low, zero)))
        energy_ref[...] = packed
        for part in range(1, n_pair):
            outs[part - 1][pl.ds(0, rows), :] = totals[part].astype(jnp.bfloat16)
            outs[part - 1][pl.ds(rows, TILE), :] = packed

    return pl.pallas_call(
        kernel,
        in_specs=whole(1 + quad),
        out_specs=whole(n_pair + 1),
        out_shape=[jax.ShapeDtypeStruct((rows, virtual), jnp.float32)]
        + [jax.ShapeDtypeStruct((rows + TILE, virtual), jnp.bfloat16)] * (n_pair - 1)
        + [jax.ShapeDtypeStruct((TILE, virtual), jnp.bfloat16)],
        scratch_shapes=[
            VMEM((virtual, virtual), jnp.float32),
            VMEM((virtual, virtual), jnp.bfloat16),
            VMEM((virtual, virtual), jnp.bfloat16),
        ],
        compiler_params=PARAMS,
        name="density_parts",
    )(inverse, *chunks)


def closing(own, energies, others, pairs, n_half):
    rows, virtual = own.shape

    def kernel(own_ref, energy_ref, *refs):
        held, (density_ref, value_ref) = refs[: len(others)], refs[len(others) :]
        wanted = lax.axis_index("aux") % n_half
        pair_at = lax.axis_index("pair")
        lane = lax.broadcasted_iota(jnp.int32, (TILE, virtual), 1)
        tails = [energy_ref[...]] + [ref[pl.ds(rows, TILE), :] for ref in held]
        found = jnp.zeros((TILE, virtual), jnp.float32)
        for mate, tail in enumerate(tails):
            at = wanted - (pair_at ^ mate) * pairs
            at = jnp.where((at >= 0) & (at < pairs), at, -1)
            found += jnp.where(lane == at, tail.astype(jnp.float32), 0.0)
        value_ref[0] = jnp.sum(found)
        total = own_ref[...]
        for ref in held:
            total += ref[pl.ds(0, rows), :].astype(jnp.float32)
        density_ref[...] = total

    return pl.pallas_call(
        kernel,
        in_specs=whole(2 + len(others)),
        out_specs=[pl.BlockSpec(memory_space=VMEM), pl.BlockSpec(memory_space=SMEM)],
        out_shape=[jax.ShapeDtypeStruct((rows, virtual), jnp.float32), jax.ShapeDtypeStruct((1,), jnp.float32)],
        compiler_params=PARAMS,
        name="closing",
    )(own, energies, *others)


def exchanged(parts, axis, low=0):
    got = [parts[0]] + [None] * (len(parts) - 1)
    for d in order(len(parts)):
        got[d] = swapped(parts[d], axis, d << low)
    return got


def summed(value, axis, low, bits):
    if bits == 0:
        return value
    if bits == 1:
        other = swapped(value, axis, 1 << low)
        return (value.astype(jnp.float32) + other.astype(jnp.float32)).astype(jnp.bfloat16)
    place = (lax.axis_index(axis) >> low) & 3
    share = value.shape[1] // 4
    parts = [lax.dynamic_slice_in_dim(value, (place ^ d) * share, share, 1) for d in range(4)]
    chunks = scattered(parts, axis, low, bits)
    out = jnp.zeros_like(value)
    for d in range(4):
        out = lax.dynamic_update_slice_in_dim(out, chunks[d], (place ^ d) * share, 1)
    return out


def scattered(parts, axis, low, bits):
    total = sum(part.astype(jnp.float32) for part in exchanged(parts, axis, low))
    total = summed(total.astype(jnp.bfloat16), axis, low + 2, bits - 2)
    return exchanged([total] * len(parts), axis, low)


def per_device(
    shell_ints, block_ids, block_count, occ_coef, occ_pick, vir_coef, occ_energy, vir_energy
):
    slots = shell_ints.shape[1]
    n_aux = lax.axis_size("aux")
    n_pair = lax.axis_size("pair")
    n_half = n_aux // 2
    pairs = n_half // n_pair
    bits = n_aux.bit_length() - 1

    ints = jnp.transpose(shell_ints, (1, 2, 3, 0))
    made = half_blocks(ints, block_ids, block_count, occ_pick, occ_coef, n_aux, n_pair)
    got = exchanged(made, "pair")
    near = n_pair // 2
    fitted = fitted_first(vir_coef, got[:near], pairs, slots)
    parts = coulomb_parts(fitted, vir_coef, got[near:], slots, 4)

    occ_pick, occ_energy, vir_energy, _ = lax.optimization_barrier((occ_pick, occ_energy, vir_energy, made[0]))
    own_pairs = lax.axis_index("pair") * pairs + jnp.arange(pairs, dtype=jnp.int32)
    spots = jnp.arange(n_aux, dtype=jnp.int32)
    batch = occ_pick[:n_aux]
    orbitals = jnp.arange(occ_energy.shape[0], dtype=jnp.int32)
    energies = jnp.sum(jnp.where(batch[:, None] == orbitals[None, :], occ_energy[None, :], 0.0), axis=1)
    levels = jnp.sum(jnp.where(own_pairs[:, None] == spots[None, :] % n_half, energies[None, :], 0.0), axis=1)
    inverse = 1.0 / (levels[:, None, None] - vir_energy[None, :, None] - vir_energy[None, None, :])

    chunks = scattered(parts, "aux", 0, bits)
    outs = density_parts(inverse, chunks, n_pair)
    others = exchanged(outs[:-1], "pair")[1:]
    density, energy = closing(outs[0], outs[-1], others, pairs, n_half)
    return (energy, density)


def solution(mesh):
    placed = (P("aux", "pair", None, None), P("pair", None), P("pair"), P(), P(), P(), P(), P())
    return jax.shard_map(
        per_device,
        mesh=mesh,
        in_specs=placed,
        out_specs=(P("aux"), P("pair", None)),
        check_vma=False,
    )
```

time: 53.8 us -> 52.3 us (0.972)
  waiting for transfers between devices: 18.7 us -> 23.9 us
  starting transfers between devices: 19.3 us -> 16.6 us
  local copies, waits for them, and re-layouts: 2.59 us -> 0.02 us
  Pallas kernels: 9.77 us -> 8.24 us
    ppermute x16 -> x13, waiting for transfers between devices: 18.7 us -> 23.9 us  [swapped(): lax.ppermute(value, axis, [(source, source ^ mask) for source in range(co...]
    ppermute x16 -> x13, starting transfers between devices: 19.3 us -> 16.6 us  [swapped(): lax.ppermute(value, axis, [(source, source ^ mask) for source in range(co...]
    unnamed x12 -> x6, local copies, waits for them, and re-layouts: 2.59 us -> 0.01 us
    pallas_call x4 -> x3, Pallas kernels: 8.15 us -> 6.62 us  [the longest x1 5.38 us: half_blocks(): pl.pallas_call(kernel, in_specs=[pl.BlockSpec(memory_space=SMEM)] + [pl.B...]
  transfers between devices with their start and end apart: 16 -> 13, of which waited for: 11 -> 10; matrix products, arithmetic and copies ran while one was open for 3% -> 3% of each run, Pallas kernels for 7% -> 1%
where the time goes in v3:
time: 52.3 us; the launch traced here: 51.9 us
  waiting for transfers between devices  23.9 us (46%)
  starting transfers between devices  16.6 us (32%)
  Pallas kernels  8.24 us (16%)
  other arithmetic  1.64 us (3%)
  between operations  1.46 us (3%)
    ppermute x13, waiting for transfers between devices, swapped(): lax.ppermute(value, axis, [(source, source ^ mask) for source in range(co...  23.9 us
    ppermute x13, starting transfers between devices, swapped(): lax.ppermute(value, axis, [(source, source ^ mask) for source in range(co...  16.6 us
    pallas_call x1, Pallas kernels, half_blocks(): pl.pallas_call(kernel, in_specs=[pl.BlockSpec(memory_space=SMEM)] + [pl.B...  5.38 us
  transfers between devices with their start and end apart: 13, of which 10 were waited for; matrix products, arithmetic and copies ran while one was open for 3% of the time, Pallas kernels for 1%

profile of v3, /device:TPU:1, one launch (start us, length us, event | category | flops | bytes accessed | tf_op | source)
XLA Modules:
  0.0 51.9 jit_solution(4771905066166812851)
XLA Ops:
  1.4 5.4 %half_blocks.1 = (bf16[528,256]{1,0:T(8,128)(2,1)S(1)}, bf16[528,256]{1,0:T(8,128)(2,1)S(1)}, bf16[528,256]{1,0:T(8,128)(2,1)S(1)}, bf16[528,256]{1,0:T(8,128)(2,1)S(1)}) custom-call(s32[1]{0:T(128)S(6)} %copy.10.count_ref, s32[2,4]{1,0:T(2,128)} %bitcast.5, s32[512]{0:T(512)} %pick_hbm.1, bf16[16,64,512]{2,1,0:T(8,128)(2,1)} %occ_hbm.1, ...), custom_call_target="tpu_custom_call" | custom-call | tf_op jit(solution)/shard_map/half_blocks/pallas_call | solution.py:71
  6.9 2.7 %collective-permute-start.1 = (bf16[528,256]{1,0:T(8,128)(2,1)S(1)}, bf16[528,256]{1,0:T(8,128)(2,1)S(1)}, u32[]{:S(2)}, u32[]{:S(2)}) collective-permute-start(bf16[528,256]{1,0:T(8,128)(2,1)S(1)} %get-tuple-element.25), channel_id=1, source_target_pairs={{0,2},{1,3},{2,0},{3,1},{4,6},{5,7},{6,4},{7,5},{8,10},{9,11},{10,... | collective-permute-start | bytes 811016 | tf_op jit(solution)/shard_map/ppermute | solution.py:21
  10.3 6.1 %collective-permute-done.1.refs_0_ = bf16[528,256]{1,0:T(8,128)(2,1)S(1)} collective-permute-done((bf16[528,256]{1,0:T(8,128)(2,1)S(1)}, bf16[528,256]{1,0:T(8,128)(2,1)S(1)}, u32[]{:S(2)}, u32[]{:S(2)}) %collective-permute-start.1) | collective-permute-done | bytes 270368 | tf_op jit(solution)/shard_map/ppermute | solution.py:21
  16.4 5.8 %collective-permute-done.2.refs_1_ = bf16[528,256]{1,0:T(8,128)(2,1)S(1)} collective-permute-done((bf16[528,256]{1,0:T(8,128)(2,1)S(1)}, bf16[528,256]{1,0:T(8,128)(2,1)S(1)}, u32[]{:S(2)}, u32[]{:S(2)}) %collective-permute-start.2) | collective-permute-done | bytes 270368 | tf_op jit(solution)/shard_map/ppermute | solution.py:21
  22.2 0.8 %coulomb_parts.1 = (bf16[1,96,384]{2,1,0:T(8,128)(2,1)S(1)}, bf16[1,96,384]{2,1,0:T(8,128)(2,1)S(1)}, bf16[1,96,384]{2,1,0:T(8,128)(2,1)S(1)}, bf16[1,96,384]{2,1,0:T(8,128)(2,1)S(1)}) custom-call(f32[2,384,256]{2,1,0:T(8,128)S(1)} %fitted_first.1.fitted_ref, bf16[16,64,384]{2,1,0:T(8,128)(2,1)S(1)} %copy-done, ...), custom_call_target="tpu_custom_call" | custom-call | tf_op jit(solution)/shard_map/coulomb_parts/pallas_call | solution.py:186
  22.9 1.5 %collective-permute-start.3 = (bf16[1,96,384]{2,1,0:T(8,128)(2,1)S(1)}, bf16[1,96,384]{2,1,0:T(8,128)(2,1)S(1)}, u32[]{:S(2)}, u32[]{:S(2)}) collective-permute-start(bf16[1,96,384]{2,1,0:T(8,128)(2,1)S(1)} %get-tuple-element.28), channel_id=1, source_target_pairs={{0,4},{4,0},{8,12},{12,8},{16,20},{20,16},{24,28},{28,24},{1,5},{5... | collective-permute-start | bytes 221192 | tf_op jit(solution)/shard_map/ppermute | solution.py:21
  24.4 1.3 %collective-permute-start.4 = (bf16[1,96,384]{2,1,0:T(8,128)(2,1)S(1)}, bf16[1,96,384]{2,1,0:T(8,128)(2,1)S(1)}, u32[]{:S(2)}, u32[]{:S(2)}) collective-permute-start(bf16[1,96,384]{2,1,0:T(8,128)(2,1)S(1)} %get-tuple-element.29), channel_id=1, source_target_pairs={{0,8},{4,12},{8,0},{12,4},{16,24},{20,28},{24,16},{28,20},{1,9},{5... | collective-permute-start | bytes 221192 | tf_op jit(solution)/shard_map/ppermute | solution.py:21
  25.7 0.6 %fusion = f32[]{:T(128)} fusion(f32[8]{0:T(128)S(1)} %select_reduce_fusion, s32[]{:T(128)S(6)} %axis_index.12), kind=kLoop, calls=%fused_computation.8 | loop fusion | flops 71 | bytes 40 | tf_op jit(solution)/shard_map/reduce_sum | solution.py:343
  26.3 1.3 %collective-permute-done.4 = bf16[1,96,384]{2,1,0:T(8,128)(2,1)S(1)} collective-permute-done((bf16[1,96,384]{2,1,0:T(8,128)(2,1)S(1)}, bf16[1,96,384]{2,1,0:T(8,128)(2,1)S(1)}, u32[]{:S(2)}, u32[]{:S(2)}) %collective-permute-start.4) | collective-permute-done | bytes 73760 | tf_op jit(solution)/shard_map/ppermute | solution.py:21
  27.6 2.2 %collective-permute-done.5 = bf16[1,96,384]{2,1,0:T(8,128)(2,1)S(1)} collective-permute-done((bf16[1,96,384]{2,1,0:T(8,128)(2,1)S(1)}, bf16[1,96,384]{2,1,0:T(8,128)(2,1)S(1)}, u32[]{:S(2)}, u32[]{:S(2)}) %collective-permute-start.5) | collective-permute-done | bytes 73760 | tf_op jit(solution)/shard_map/ppermute | solution.py:21
  29.9 2.4 %collective-permute-start.6 = (bf16[1,96,384]{2,1,0:T(8,128)(2,1)S(1)}, bf16[1,96,384]{2,1,0:T(8,128)(2,1)S(1)}, u32[]{:S(2)}, u32[]{:S(2)}) collective-permute-start(bf16[1,96,384]{2,1,0:T(8,128)(2,1)S(1)} %add_convert_fusion.1), channel_id=1, source_target_pairs={{0,16},{4,20},{8,24},{12,28},{16,0},{20,4},{24,8},{28,12},{1,17},{... | collective-permute-start | bytes 221192 | tf_op jit(solution)/shard_map/ppermute | solution.py:21
  32.3 0.6 %broadcast_subtract_fusion = f32[384]{0:T(512)S(1)} fusion(f32[384]{0:T(512)S(1)} %copy-done.1, f32[]{:T(128)} %fusion), kind=kLoop, calls=%fused_computation.7 | loop fusion | flops 384 | bytes 3076 | tf_op jit(solution)/shard_map/sub | solution.py:344
  32.9 1.1 %collective-permute-done.6 = bf16[1,96,384]{2,1,0:T(8,128)(2,1)S(1)} collective-permute-done((bf16[1,96,384]{2,1,0:T(8,128)(2,1)S(1)}, bf16[1,96,384]{2,1,0:T(8,128)(2,1)S(1)}, u32[]{:S(2)}, u32[]{:S(2)}) %collective-permute-start.6) | collective-permute-done | bytes 73760 | tf_op jit(solution)/shard_map/ppermute | solution.py:21
  34.1 1.8 %collective-permute-start.9 = (bf16[1,96,384]{2,1,0:T(8,128)(2,1)S(1)}, bf16[1,96,384]{2,1,0:T(8,128)(2,1)S(1)}, u32[]{:S(2)}, u32[]{:S(2)}) collective-permute-start(bf16[1,96,384]{2,1,0:T(8,128)(2,1)S(1)} %add_convert_fusion.refs_0_), channel_id=1, source_target_pairs={{0,12},{4,8},{8,4},{12,0},{16,28},{20,24},{24,20},{28,16},{1,13},{... | collective-permute-start | bytes 221192 | tf_op jit(solution)/shard_map/ppermute | solution.py:21
  35.8 1.0 %collective-permute-start.8 = (bf16[1,96,384]{2,1,0:T(8,128)(2,1)S(1)}, bf16[1,96,384]{2,1,0:T(8,128)(2,1)S(1)}, u32[]{:S(2)}, u32[]{:S(2)}) collective-permute-start(bf16[1,96,384]{2,1,0:T(8,128)(2,1)S(1)} %add_convert_fusion.refs_0_), channel_id=1, source_target_pairs={{0,8},{4,12},{8,0},{12,4},{16,24},{20,28},{24,16},{28,20},{1,9},{5... | collective-permute-start | bytes 221192 | tf_op jit(solution)/shard_map/ppermute | solution.py:21
  37.0 1.2 %collective-permute-done.9.refs_3_ = bf16[1,96,384]{2,1,0:T(8,128)(2,1)S(1)} collective-permute-done((bf16[1,96,384]{2,1,0:T(8,128)(2,1)S(1)}, bf16[1,96,384]{2,1,0:T(8,128)(2,1)S(1)}, u32[]{:S(2)}, u32[]{:S(2)}) %collective-permute-start.9) | collective-permute-done | bytes 73760 | tf_op jit(solution)/shard_map/ppermute | solution.py:21
  38.2 1.2 %collective-permute-done.8.refs_2_ = bf16[1,96,384]{2,1,0:T(8,128)(2,1)S(1)} collective-permute-done((bf16[1,96,384]{2,1,0:T(8,128)(2,1)S(1)}, bf16[1,96,384]{2,1,0:T(8,128)(2,1)S(1)}, u32[]{:S(2)}, u32[]{:S(2)}) %collective-permute-start.8) | collective-permute-done | bytes 73760 | tf_op jit(solution)/shard_map/ppermute | solution.py:21
  39.4 0.7 %collective-permute-done.7.refs_1_ = bf16[1,96,384]{2,1,0:T(8,128)(2,1)S(1)} collective-permute-done((bf16[1,96,384]{2,1,0:T(8,128)(2,1)S(1)}, bf16[1,96,384]{2,1,0:T(8,128)(2,1)S(1)}, u32[]{:S(2)}, u32[]{:S(2)}) %collective-permute-start.7) | collective-permute-done | bytes 73760 | tf_op jit(solution)/shard_map/ppermute | solution.py:21
  40.1 0.9 %density_parts.1 = (f32[96,384]{1,0:T(8,128)S(1)}, bf16[112,384]{1,0:T(8,128)(2,1)S(1)}, bf16[112,384]{1,0:T(8,128)(2,1)S(1)}, bf16[112,384]{1,0:T(8,128)(2,1)S(1)}, bf16[16,384]{1,0:T(8,128)(2,1)S(1)}) custom-call(f32[1,384,384]{2,1,0:T(8,128)S(1)} %subtract_divide_fusion.inverse_ref, bf16[1,96,384]{2,1,0:T(8,128)(2,1)S(1)} %add_convert_fusion.refs_0_, ...), custom_call_target="tpu_custom_call" | custom-call | tf_op jit(solution)/shard_map/density_parts/pallas_call | solution.py:244
  41.0 4.0 %collective-permute-start.10 = (bf16[112,384]{1,0:T(8,128)(2,1)S(1)}, bf16[112,384]{1,0:T(8,128)(2,1)S(1)}, u32[]{:S(2)}, u32[]{:S(2)}) collective-permute-start(bf16[112,384]{1,0:T(8,128)(2,1)S(1)} %get-tuple-element.33), channel_id=1, source_target_pairs={{0,1},{1,0},{2,3},{3,2},{4,5},{5,4},{6,7},{7,6},{8,9},{9,8},{10,11... | collective-permute-start | bytes 258056 | tf_op jit(solution)/shard_map/ppermute | solution.py:21
  45.0 1.3 %collective-permute-start.11 = (bf16[112,384]{1,0:T(8,128)(2,1)S(1)}, bf16[112,384]{1,0:T(8,128)(2,1)S(1)}, u32[]{:S(2)}, u32[]{:S(2)}) collective-permute-start(bf16[112,384]{1,0:T(8,128)(2,1)S(1)} %get-tuple-element.34), channel_id=1, source_target_pairs={{0,2},{1,3},{2,0},{3,1},{4,6},{5,7},{6,4},{7,5},{8,10},{9,11},{10,... | collective-permute-start | bytes 258056 | tf_op jit(solution)/shard_map/ppermute | solution.py:21
  46.7 2.4 %collective-permute-done.11.refs_1_ = bf16[112,384]{1,0:T(8,128)(2,1)S(1)} collective-permute-done((bf16[112,384]{1,0:T(8,128)(2,1)S(1)}, bf16[112,384]{1,0:T(8,128)(2,1)S(1)}, u32[]{:S(2)}, u32[]{:S(2)}) %collective-permute-start.11) | collective-permute-done | bytes 86048 | tf_op jit(solution)/shard_map/ppermute | solution.py:21
  49.1 2.0 %collective-permute-done.12.refs_2_ = bf16[112,384]{1,0:T(8,128)(2,1)S(1)} collective-permute-done((bf16[112,384]{1,0:T(8,128)(2,1)S(1)}, bf16[112,384]{1,0:T(8,128)(2,1)S(1)}, u32[]{:S(2)}, u32[]{:S(2)}) %collective-permute-start.12) | collective-permute-done | bytes 86048 | tf_op jit(solution)/shard_map/ppermute | solution.py:21
  51.1 0.7 %closing.1 = (f32[96,384]{1,0:T(8,128)}, f32[1]{0:T(128)}) custom-call(f32[96,384]{1,0:T(8,128)S(1)} %get-tuple-element.31.own_ref, bf16[16,384]{1,0:T(8,128)(2,1)S(1)} %get-tuple-element.32.energy_ref, bf16[112,384]{1,0:T(8,128)(2,1)S(1)} %collective-permute-done.10.refs_0_, bf16[112,384]{1,0:T(8,128)(2,1)S(1)} %collective-permute-done.11.refs_1_, ...), custom_call_target="tpu_custom_call" | custom-call | tf_op jit(solution)/shard_map/closing/pallas_call | solution.py:281
  (21 shorter events, 1.5 us)
Async XLA Ops:
  0.6 9.0 %slice-start = ((s32[512]{0:T(512)}), s32[8]{0:T(128)S(1)}, s32[]{:S(2)}) async-start(s32[512]{0:T(512)} %pick_hbm.1), calls=%async_computation | async-start | bytes 1024 | tf_op jit(solution)/shard_map/slice | solution.py:340
  0.6 31.6 %copy-start.1 = (f32[384]{0:T(512)S(1)}, f32[384]{0:T(512)}, u32[]{:S(2)}) copy-start(f32[384]{0:T(512)} %param.15) | copy-start | bytes 4612
  0.7 9.0 %copy-start.2 = (f32[512]{0:T(512)S(1)}, f32[512]{0:T(512)}, u32[]{:S(2)}) copy-start(f32[512]{0:T(512)} %param.14) | copy-start | bytes 6148
  0.7 9.2 %copy-start = (bf16[16,64,384]{2,1,0:T(8,128)(2,1)S(1)}, bf16[16,64,384]{2,1,0:T(8,128)(2,1)}, u32[]{:S(2)}) copy-start(bf16[16,64,384]{2,1,0:T(8,128)(2,1)} %vir_ref.3) | copy-start | bytes 2359300
  6.8 3.0 %collective-permute-start = (bf16[528,256]{1,0:T(8,128)(2,1)S(1)}, bf16[528,256]{1,0:T(8,128)(2,1)S(1)}, u32[]{:S(2)}, u32[]{:S(2)}) collective-permute-start(bf16[528,256]{1,0:T(8,128)(2,1)S(1)} %get-tuple-element.24), channel_id=1, source_target_pairs={{0,1},{1,0},{2,3},{3,2},{4,5},{5,4},{6,7},{7,6},{8,9},{9,8},{10,11... | collective-permute-start | bytes 811016 | tf_op jit(solution)/shard_map/ppermute | solution.py:21
  6.9 9.5 %collective-permute-start.1 = (bf16[528,256]{1,0:T(8,128)(2,1)S(1)}, bf16[528,256]{1,0:T(8,128)(2,1)S(1)}, u32[]{:S(2)}, u32[]{:S(2)}) collective-permute-start(bf16[528,256]{1,0:T(8,128)(2,1)S(1)} %get-tuple-element.25), channel_id=1, source_target_pairs={{0,2},{1,3},{2,0},{3,1},{4,6},{5,7},{6,4},{7,5},{8,10},{9,11},{10,... | collective-permute-start | bytes 811016 | tf_op jit(solution)/shard_map/ppermute | solution.py:21
  9.6 12.6 %collective-permute-start.2 = (bf16[528,256]{1,0:T(8,128)(2,1)S(1)}, bf16[528,256]{1,0:T(8,128)(2,1)S(1)}, u32[]{:S(2)}, u32[]{:S(2)}) collective-permute-start(bf16[528,256]{1,0:T(8,128)(2,1)S(1)} %get-tuple-element.26), channel_id=1, source_target_pairs={{0,3},{1,2},{2,1},{3,0},{4,7},{5,6},{6,5},{7,4},{8,11},{9,10},{10,... | collective-permute-start | bytes 811016 | tf_op jit(solution)/shard_map/ppermute | solution.py:21
  22.9 3.4 %collective-permute-start.3 = (bf16[1,96,384]{2,1,0:T(8,128)(2,1)S(1)}, bf16[1,96,384]{2,1,0:T(8,128)(2,1)S(1)}, u32[]{:S(2)}, u32[]{:S(2)}) collective-permute-start(bf16[1,96,384]{2,1,0:T(8,128)(2,1)S(1)} %get-tuple-element.28), channel_id=1, source_target_pairs={{0,4},{4,0},{8,12},{12,8},{16,20},{20,16},{24,28},{28,24},{1,5},{5... | collective-permute-start | bytes 221192 | tf_op jit(solution)/shard_map/ppermute | solution.py:21
  24.4 3.2 %collective-permute-start.4 = (bf16[1,96,384]{2,1,0:T(8,128)(2,1)S(1)}, bf16[1,96,384]{2,1,0:T(8,128)(2,1)S(1)}, u32[]{:S(2)}, u32[]{:S(2)}) collective-permute-start(bf16[1,96,384]{2,1,0:T(8,128)(2,1)S(1)} %get-tuple-element.29), channel_id=1, source_target_pairs={{0,8},{4,12},{8,0},{12,4},{16,24},{20,28},{24,16},{28,20},{1,9},{5... | collective-permute-start | bytes 221192 | tf_op jit(solution)/shard_map/ppermute | solution.py:21
  25.7 4.1 %collective-permute-start.5 = (bf16[1,96,384]{2,1,0:T(8,128)(2,1)S(1)}, bf16[1,96,384]{2,1,0:T(8,128)(2,1)S(1)}, u32[]{:S(2)}, u32[]{:S(2)}) collective-permute-start(bf16[1,96,384]{2,1,0:T(8,128)(2,1)S(1)} %get-tuple-element.30), channel_id=1, source_target_pairs={{0,12},{4,8},{8,4},{12,0},{16,28},{20,24},{24,20},{28,16},{1,13},{... | collective-permute-start | bytes 221192 | tf_op jit(solution)/shard_map/ppermute | solution.py:21
  29.9 4.2 %collective-permute-start.6 = (bf16[1,96,384]{2,1,0:T(8,128)(2,1)S(1)}, bf16[1,96,384]{2,1,0:T(8,128)(2,1)S(1)}, u32[]{:S(2)}, u32[]{:S(2)}) collective-permute-start(bf16[1,96,384]{2,1,0:T(8,128)(2,1)S(1)} %add_convert_fusion.1), channel_id=1, source_target_pairs={{0,16},{4,20},{8,24},{12,28},{16,0},{20,4},{24,8},{28,12},{1,17},{... | collective-permute-start | bytes 221192 | tf_op jit(solution)/shard_map/ppermute | solution.py:21
  34.1 4.2 %collective-permute-start.9 = (bf16[1,96,384]{2,1,0:T(8,128)(2,1)S(1)}, bf16[1,96,384]{2,1,0:T(8,128)(2,1)S(1)}, u32[]{:S(2)}, u32[]{:S(2)}) collective-permute-start(bf16[1,96,384]{2,1,0:T(8,128)(2,1)S(1)} %add_convert_fusion.refs_0_), channel_id=1, source_target_pairs={{0,12},{4,8},{8,4},{12,0},{16,28},{20,24},{24,20},{28,16},{1,13},{... | collective-permute-start | bytes 221192 | tf_op jit(solution)/shard_map/ppermute | solution.py:21
  35.8 3.6 %collective-permute-start.8 = (bf16[1,96,384]{2,1,0:T(8,128)(2,1)S(1)}, bf16[1,96,384]{2,1,0:T(8,128)(2,1)S(1)}, u32[]{:S(2)}, u32[]{:S(2)}) collective-permute-start(bf16[1,96,384]{2,1,0:T(8,128)(2,1)S(1)} %add_convert_fusion.refs_0_), channel_id=1, source_target_pairs={{0,8},{4,12},{8,0},{12,4},{16,24},{20,28},{24,16},{28,20},{1,9},{5... | collective-permute-start | bytes 221192 | tf_op jit(solution)/shard_map/ppermute | solution.py:21
  36.9 3.2 %collective-permute-start.7 = (bf16[1,96,384]{2,1,0:T(8,128)(2,1)S(1)}, bf16[1,96,384]{2,1,0:T(8,128)(2,1)S(1)}, u32[]{:S(2)}, u32[]{:S(2)}) collective-permute-start(bf16[1,96,384]{2,1,0:T(8,128)(2,1)S(1)} %add_convert_fusion.refs_0_), channel_id=1, source_target_pairs={{0,4},{4,0},{8,12},{12,8},{16,20},{20,16},{24,28},{28,24},{1,5},{5... | collective-permute-start | bytes 221192 | tf_op jit(solution)/shard_map/ppermute | solution.py:21
  41.0 5.8 %collective-permute-start.10 = (bf16[112,384]{1,0:T(8,128)(2,1)S(1)}, bf16[112,384]{1,0:T(8,128)(2,1)S(1)}, u32[]{:S(2)}, u32[]{:S(2)}) collective-permute-start(bf16[112,384]{1,0:T(8,128)(2,1)S(1)} %get-tuple-element.33), channel_id=1, source_target_pairs={{0,1},{1,0},{2,3},{3,2},{4,5},{5,4},{6,7},{7,6},{8,9},{9,8},{10,11... | collective-permute-start | bytes 258056 | tf_op jit(solution)/shard_map/ppermute | solution.py:21
  45.0 4.1 %collective-permute-start.11 = (bf16[112,384]{1,0:T(8,128)(2,1)S(1)}, bf16[112,384]{1,0:T(8,128)(2,1)S(1)}, u32[]{:S(2)}, u32[]{:S(2)}) collective-permute-start(bf16[112,384]{1,0:T(8,128)(2,1)S(1)} %get-tuple-element.34), channel_id=1, source_target_pairs={{0,2},{1,3},{2,0},{3,1},{4,6},{5,7},{6,4},{7,5},{8,10},{9,11},{10,... | collective-permute-start | bytes 258056 | tf_op jit(solution)/shard_map/ppermute | solution.py:21
  46.3 4.9 %collective-permute-start.12 = (bf16[112,384]{1,0:T(8,128)(2,1)S(1)}, bf16[112,384]{1,0:T(8,128)(2,1)S(1)}, u32[]{:S(2)}, u32[]{:S(2)}) collective-permute-start(bf16[112,384]{1,0:T(8,128)(2,1)S(1)} %get-tuple-element.35), channel_id=1, source_target_pairs={{0,3},{1,2},{2,1},{3,0},{4,7},{5,6},{6,5},{7,4},{8,11},{9,10},{10,... | collective-permute-start | bytes 258056 | tf_op jit(solution)/shard_map/ppermute | solution.py:21

commit v4 on v3

v4 whole, which is shorter than its diff:
```python
import jax
import jax.numpy as jnp
from jax import lax
from jax.experimental import pallas as pl
from jax.experimental.pallas import tpu as pltpu
from jax.sharding import PartitionSpec as P

VMEM = pltpu.VMEM
SMEM = pltpu.SMEM
TILE = 16
SUB = 8
MARK = 128
PARAMS = pltpu.CompilerParams(vmem_limit_bytes=48 * 1024 * 1024)


def order(count):
    return sorted(range(1, count), reverse=True)


def swapped(value, axis, mask):
    count = lax.axis_size(axis)
    return lax.ppermute(value, axis, [(source, source ^ mask) for source in range(count)])


def in_hbm(*values):
    return [pltpu.with_memory_space_constraint(value, pltpu.HBM) for value in values]


def whole(count):
    return [pl.BlockSpec(memory_space=VMEM)] * count


def half_first(ints, block_ids, occ_pick, occ_coef, count, n_aux, n_pair):
    slots, width, _, aux_rows = ints.shape
    blocks, _, nocc = occ_coef.shape
    n_half = n_aux // 2
    pairs = n_half // n_pair
    rows = 2 * pairs * count * width

    def kernel(ids_hbm, pick_hbm, occ_hbm, ints_hbm, *refs):
        outs, chosen_ref, tables_ref = refs[:n_pair], refs[n_pair], refs[n_pair + 1]
        ids_ref, pick_ref, occ_ref, held, small, large = refs[n_pair + 2 :]
        tables = [
            pltpu.make_async_copy(source, target, small.at[at])
            for at, (source, target) in enumerate(((ids_hbm, ids_ref), (pick_hbm, pick_ref), (occ_hbm, occ_ref)))
        ]
        for copy in tables:
            copy.start()
        copies = started(ints_hbm, held, large, 0, count, width * width)
        for copy in tables:
            copy.wait()
        pair_at = lax.axis_index("pair")
        lane = lax.broadcasted_iota(jnp.int32, (SUB, nocc), 1)
        chosen = []
        for mate in range(n_pair):
            for pair in range(pairs):
                for side in range(2):
                    orbital = pick_ref[(pair_at ^ mate) * pairs + pair + side * n_half]
                    chosen.append(jnp.where(lane == orbital, 1.0, 0.0))
        chosen = jnp.concatenate(chosen, axis=0).astype(jnp.bfloat16)
        weights = [slot_weights(chosen, occ_ref[ids_ref[1, slot]]) for slot in range(count)]
        row = lax.broadcasted_iota(jnp.int32, (TILE, aux_rows), 0)
        blocks = jnp.zeros((TILE, aux_rows), jnp.float32)
        for slot in range(slots):
            blocks = jnp.where(row == slot, ids_ref[0, slot].astype(jnp.float32), blocks)
        for out in outs:
            out[pl.ds(rows, TILE), :] = blocks.astype(jnp.bfloat16)
        chosen_ref[...] = chosen
        for slot in range(count, slots):
            tables_ref[slot - count] = occ_ref[ids_ref[1, slot]]
        for slot in range(count):
            copies[slot].wait()
            halves(weights[slot], held, outs, slot, count, width, pairs)

    return pl.pallas_call(
        kernel,
        in_specs=[pl.BlockSpec(memory_space=pltpu.HBM)] * 4,
        out_specs=whole(n_pair + 2),
        out_shape=[jax.ShapeDtypeStruct((rows + TILE, aux_rows), jnp.bfloat16)] * n_pair
        + [
            jax.ShapeDtypeStruct((n_aux * SUB, nocc), jnp.bfloat16),
            jax.ShapeDtypeStruct((slots - count, width, nocc), jnp.bfloat16),
        ],
        scratch_shapes=[
            SMEM((2, slots), jnp.int32),
            SMEM((nocc,), jnp.int32),
            VMEM(occ_coef.shape, jnp.bfloat16),
            VMEM((count * width * width, aux_rows), jnp.bfloat16),
            pltpu.SemaphoreType.DMA((3,)),
            pltpu.SemaphoreType.DMA((count,)),
        ],
        compiler_params=PARAMS,
        name="half_first",
    )(*in_hbm(block_ids.T, occ_pick, occ_coef, ints.reshape(-1, aux_rows)))


def started(ints_hbm, held, sems, first, count, rows):
    copies = []
    for slot in range(count):
        source = ints_hbm.at[pl.ds((first + slot) * rows, rows), :]
        copies.append(pltpu.make_async_copy(source, held.at[pl.ds(slot * rows, rows), :], sems.at[slot]))
        copies[-1].start()
    return copies


def slot_weights(chosen, table):
    width = table.shape[0]
    table = jnp.concatenate([table] * (128 // width), axis=0)
    spread = lax.dot_general(chosen, table, (((1,), (1,)), ((), ())), preferred_element_type=jnp.float32)
    spread = jnp.concatenate([spread] * (SUB * width // 128), axis=1)
    row = lax.broadcasted_iota(jnp.int32, spread.shape, 0)
    column = lax.broadcasted_iota(jnp.int32, spread.shape, 1)
    return jnp.where(row % SUB == column // width, spread, 0.0).astype(jnp.bfloat16)


def halves(weights, ints, outs, slot, count, width, pairs):
    depth = SUB * width
    for step in range(width // TILE):
        at = slot * (width // TILE) + step
        made = [
            jnp.dot(weights, ints[pl.ds((2 * at + part) * depth, depth), :], preferred_element_type=jnp.float32)
            for part in range(2)
        ]
        for mate, out in enumerate(outs):
            for orbital in range(2 * pairs):
                source = (mate * 2 * pairs + orbital) * SUB
                both = jnp.concatenate([part[source : source + SUB] for part in made], axis=0)
                out[pl.ds(orbital * count * width + at * TILE, TILE), :] = both.astype(jnp.bfloat16)


def half_rest(ints, block_count, chosen, tables, n_pair, pairs):
    slots, width, _, aux_rows = ints.shape
    count = tables.shape[0]

    def kernel(count_ref, chosen_ref, tables_ref, ints_hbm, *refs):
        outs, (held, large) = refs[:n_pair], refs[n_pair:]
        copies = started(ints_hbm, held, large, slots - count, count, width * width)
        weights = [slot_weights(chosen_ref[...], tables_ref[slot]) for slot in range(count)]
        for slot in range(count):
            copies[slot].wait()
            halves(weights[slot], held, outs, slot, count, width, pairs)
        live = count_ref[0]
        mark = jnp.full((TILE, aux_rows), (MARK * (live + 1)).astype(jnp.float32), jnp.float32).astype(jnp.bfloat16)
        for out in outs:
            spot = pl.ds((count - 1) * width, TILE)
            out[spot, :] = jnp.where(live < slots, mark, out[spot, :])

    return pl.pallas_call(
        kernel,
        in_specs=[pl.BlockSpec(memory_space=SMEM)] + whole(2) + [pl.BlockSpec(memory_space=pltpu.HBM)],
        out_specs=whole(n_pair),
        out_shape=[jax.ShapeDtypeStruct((2 * pairs * count * width, aux_rows), jnp.bfloat16)] * n_pair,
        scratch_shapes=[
            VMEM((count * width * width, aux_rows), jnp.bfloat16),
            pltpu.SemaphoreType.DMA((count,)),
        ],
        compiler_params=PARAMS,
        name="half_rest",
    )(block_count, chosen, tables, *in_hbm(ints.reshape(-1, aux_rows)))


def fitted_first(vir_coef, parts, pairs, counts):
    aux_rows = parts[0].shape[1]
    width, virtual = vir_coef.shape[1], vir_coef.shape[2]
    span = counts[0] * width

    def kernel(vir_ref, *refs):
        held, (fitted_ref, rest_ref, own_ref) = refs[: len(parts)], refs[len(parts) :]
        first, rest = [], []
        for part in held:
            tail = part[pl.ds(2 * pairs * span, TILE), :][:, :128].astype(jnp.float32)
            found = [vir_ref[tail[slot, 0].astype(jnp.int32)] for slot in range(sum(counts))]
            first.append(found[0])
            rest += found[1:]
        own_ref[...] = jnp.concatenate(first, axis=0).T
        rest_ref[...] = jnp.concatenate(rest, axis=0).T
        for orbital in range(2 * pairs):
            blocks = jnp.concatenate([part[pl.ds(orbital * span, width), :] for part in held], axis=0)
            fitted_ref[orbital] = jnp.dot(own_ref[...], blocks, preferred_element_type=jnp.float32)

    return pl.pallas_call(
        kernel,
        in_specs=whole(1 + len(parts)),
        out_specs=whole(2),
        out_shape=[
            jax.ShapeDtypeStruct((2 * pairs, virtual, aux_rows), jnp.float32),
            jax.ShapeDtypeStruct((virtual, len(parts) * (sum(counts) - 1) * width), jnp.bfloat16),
        ],
        scratch_shapes=[VMEM((virtual, len(parts) * width), jnp.bfloat16)],
        compiler_params=PARAMS,
        name="fitted_first",
    )(vir_coef, *parts)


def coulomb_parts(fitted, rest, first, later, pairs, counts, quad):
    n_pair = len(first)
    slots = sum(counts)
    virtual, aux_rows = fitted.shape[1:]
    width = rest.shape[1] // (n_pair * (slots - 1))
    share = virtual // quad

    def kernel(fitted_ref, rest_ref, *refs):
        held, outs, block_ref = (refs[:n_pair], refs[n_pair : 2 * n_pair]), refs[2 * n_pair : -1], refs[-1]
        place = lax.axis_index("aux") % quad
        live = []
        for part in held[1]:
            mark = part[pl.ds((counts[1] - 1) * width, TILE), :][:, :128].astype(jnp.float32)[0, 0]
            live.append(jnp.where(mark < MARK, slots, (mark * (1.0 / MARK)).astype(jnp.int32) - 1))
        for pair in range(pairs):
            sides = []
            for orbital in (2 * pair, 2 * pair + 1):
                blocks = []
                for group in range(n_pair):
                    for slot in range(1, slots):
                        chunk = int(slot >= counts[0])
                        at = (orbital * counts[chunk] + slot - chunk * counts[0]) * width
                        block = held[chunk][group][pl.ds(at, width), :]
                        blocks.append(jnp.where(slot < live[group], block, jnp.zeros_like(block)))
                total = jnp.dot(rest_ref[...], jnp.concatenate(blocks, axis=0), preferred_element_type=jnp.float32)
                sides.append((fitted_ref[orbital] + total).astype(jnp.bfloat16))
            block = lax.dot_general(*sides, (((1,), (1,)), ((), ())), preferred_element_type=jnp.float32)
            block_ref[...] = block.astype(jnp.bfloat16)
            for part, out in enumerate(outs):
                at = pl.multiple_of((place ^ part) * share, share)
                out[pair] = block_ref[pl.ds(at, share), :]

    return pl.pallas_call(
        kernel,
        in_specs=whole(2 + 2 * n_pair),
        out_specs=whole(quad),
        out_shape=[jax.ShapeDtypeStruct((pairs, share, virtual), jnp.bfloat16)] * quad,
        scratch_shapes=[VMEM((virtual, virtual), jnp.bfloat16)],
        compiler_params=PARAMS,
        name="coulomb_parts",
    )(fitted, rest, *first, *later)


def density_parts(inverse, chunks, n_pair):
    quad = len(chunks)
    pairs, share, virtual = chunks[0].shape
    rows = virtual // n_pair

    def kernel(inverse_ref, *refs):
        held, own_ref, outs = refs[:quad], refs[quad], refs[quad + 1 : quad + n_pair]
        energy_ref, block_ref, total_ref = refs[quad + n_pair :]
        place = lax.axis_index("aux") % quad
        pair_at = lax.axis_index("pair")
        lane = lax.broadcasted_iota(jnp.int32, (1, virtual), 1)
        energies = []
        totals = [None] * n_pair
        for pair in range(pairs):
            for part in range(quad):
                at = pl.multiple_of((place ^ part) * share, share)
                block_ref[pl.ds(at, share), :] = held[part][pair]
            block = block_ref[...].astype(jnp.float32)
            flipped = block_ref[...].T.astype(jnp.float32)
            inverse = inverse_ref[pair]
            energy = jnp.sum(block * (2.0 * block - flipped) * inverse)
            even = ((block + flipped) * inverse).astype(jnp.bfloat16)
            odd = ((block - flipped) * inverse).astype(jnp.bfloat16)
            term = 0.5 * jnp.dot(even, even, preferred_element_type=jnp.float32)
            term -= 1.5 * jnp.dot(odd, odd, preferred_element_type=jnp.float32)
            total_ref[...] = term if pair == 0 else total_ref[...] + term
        for part in range(n_pair):
            totals[part] = total_ref[pl.ds(pl.multiple_of((pair_at ^ part) * rows, rows), rows), :]
            energies.append(energy)
        own_ref[...] = totals[0]
        energy_ref[...] = jnp.zeros_like(energy_ref)
        for pair, energy in enumerate(energies):
            energy_ref[...] = jnp.where(lane == pair, energy, energy_ref[...])
        for part in range(1, n_pair):
            outs[part - 1][...] = totals[part].astype(jnp.bfloat16)
            first = (pair_at ^ part) * rows
            last = totals[part][rows - TILE :]
            row = lax.broadcasted_iota(jnp.int32, (TILE, virtual), 0)
            corner = jnp.zeros((1, virtual), jnp.float32)
            for pair, energy in enumerate(energies):
                rest = jnp.full((1, virtual), energy, jnp.float32)
                for at in range(3):
                    piece = rest.astype(jnp.bfloat16).astype(jnp.float32)
                    corner = jnp.where(lane == first + 3 * pair + at, piece, corner)
                    rest = rest - piece
            inside = (lane >= first) & (lane < first + 3 * pairs) & (row == TILE - 1)
            outs[part - 1][pl.ds(rows - TILE, TILE), :] = jnp.where(inside, corner, last).astype(jnp.bfloat16)

    return pl.pallas_call(
        kernel,
        in_specs=whole(1 + quad),
        out_specs=whole(n_pair + 1),
        out_shape=[jax.ShapeDtypeStruct((rows, virtual), jnp.float32)]
        + [jax.ShapeDtypeStruct((rows, virtual), jnp.bfloat16)] * (n_pair - 1)
        + [jax.ShapeDtypeStruct((1, virtual), jnp.float32)],
        scratch_shapes=[
            VMEM((virtual, virtual), jnp.bfloat16),
            VMEM((virtual, virtual), jnp.float32),
        ],
        compiler_params=PARAMS,
        name="density_parts",
    )(inverse, *chunks)


def closing(own, energies, others, pairs, n_half):
    rows, virtual = own.shape

    def kernel(own_ref, energy_ref, *refs):
        held, (density_ref, value_ref) = refs[: len(others)], refs[len(others) :]
        wanted = lax.axis_index("aux") % n_half
        pair_at = lax.axis_index("pair")
        lane = lax.broadcasted_iota(jnp.int32, (1, virtual), 1)
        first = pair_at * rows
        found = jnp.zeros((1, virtual), jnp.float32)
        total = own_ref[...]
        for mate in range(len(held) + 1):
            at = wanted - (pair_at ^ mate) * pairs
            here = (at >= 0) & (at < pairs)
            if mate == 0:
                found += jnp.where(here & (lane == at), energy_ref[...], 0.0)
            else:
                part = held[mate - 1][...].astype(jnp.float32)
                spot = lane - first - 3 * at
                found += jnp.where(here & (spot >= 0) & (spot < 3), part[rows - 1 :], 0.0)
                total += part
        value_ref[0] = jnp.sum(found)
        density_ref[...] = total
        head = -(-3 * pairs // TILE) * TILE
        top = total[:head]
        wide = lax.broadcasted_iota(jnp.int32, (head, virtual), 1)
        row = lax.broadcasted_iota(jnp.int32, (head, virtual), 0)
        column = jnp.sum(jnp.where(wide == first + rows - 1, top, 0.0), axis=1, keepdims=True)
        turned = jnp.sum(jnp.where(wide == first + row, column, 0.0), axis=0, keepdims=True)
        last = total[rows - SUB :]
        inside = (lane >= first) & (lane < first + 3 * pairs)
        inside = inside & (lax.broadcasted_iota(jnp.int32, (SUB, virtual), 0) == SUB - 1)
        density_ref[pl.ds(rows - SUB, SUB), :] = jnp.where(inside, turned, last)

    return pl.pallas_call(
        kernel,
        in_specs=whole(2 + len(others)),
        out_specs=[pl.BlockSpec(memory_space=VMEM), pl.BlockSpec(memory_space=SMEM)],
        out_shape=[jax.ShapeDtypeStruct((rows, virtual), jnp.float32), jax.ShapeDtypeStruct((1,), jnp.float32)],
        compiler_params=PARAMS,
        name="closing",
    )(own, energies, *others)


def exchanged(parts, axis, low=0):
    got = [parts[0]] + [None] * (len(parts) - 1)
    for d in order(len(parts)):
        if parts[d] is not None:
            got[d] = swapped(parts[d], axis, d << low)
    return got


def summed(value, axis, low, bits):
    if bits == 0:
        return value
    if bits == 1:
        other = swapped(value, axis, 1 << low)
        return (value.astype(jnp.float32) + other.astype(jnp.float32)).astype(jnp.bfloat16)
    place = (lax.axis_index(axis) >> low) & 3
    share = value.shape[1] // 4
    parts = [lax.dynamic_slice_in_dim(value, (place ^ d) * share, share, 1) for d in range(4)]
    chunks = scattered(parts, axis, low, bits)
    out = jnp.zeros_like(value)
    for d in range(4):
        out = lax.dynamic_update_slice_in_dim(out, chunks[d], (place ^ d) * share, 1)
    return out


def scattered(parts, axis, low, bits):
    total = sum(part.astype(jnp.float32) for part in exchanged(parts, axis, low))
    total = summed(total.astype(jnp.bfloat16), axis, low + 2, bits - 2)
    return exchanged([total] * len(parts), axis, low)


def per_device(
    shell_ints, block_ids, block_count, occ_coef, occ_pick, vir_coef, occ_energy, vir_energy
):
    _, slots, width, _ = shell_ints.shape
    n_aux = lax.axis_size("aux")
    n_pair = lax.axis_size("pair")
    n_half = n_aux // 2
    pairs = n_half // n_pair
    bits = n_aux.bit_length() - 1

    ints = jnp.transpose(shell_ints, (1, 2, 3, 0))
    counts = (slots // 2, slots - slots // 2)
    *first, chosen, tables = half_first(
        ints, block_ids, occ_pick, occ_coef, counts[0], n_aux, n_pair
    )
    block_count, _ = lax.optimization_barrier((block_count, first[0]))
    later = list(half_rest(ints, block_count, chosen, tables, n_pair, pairs))
    got = [exchanged(first, "pair"), exchanged(later, "pair")]

    fitted, rest = fitted_first(vir_coef, got[0], pairs, counts)
    parts = coulomb_parts(fitted, rest, got[0], got[1], pairs, counts, 4)

    occ_pick, occ_energy, vir_energy, _ = lax.optimization_barrier((occ_pick, occ_energy, vir_energy, later[0]))
    own_pairs = lax.axis_index("pair") * pairs + jnp.arange(pairs, dtype=jnp.int32)
    spots = jnp.arange(n_aux, dtype=jnp.int32)
    batch = occ_pick[:n_aux]
    orbitals = jnp.arange(occ_energy.shape[0], dtype=jnp.int32)
    energies = jnp.sum(jnp.where(batch[:, None] == orbitals[None, :], occ_energy[None, :], 0.0), axis=1)
    levels = jnp.sum(jnp.where(own_pairs[:, None] == spots[None, :] % n_half, energies[None, :], 0.0), axis=1)
    inverse = 1.0 / (levels[:, None, None] - vir_energy[None, :, None] - vir_energy[None, None, :])

    chunks = scattered(parts, "aux", 0, bits)
    outs = density_parts(inverse, chunks, n_pair)
    others = exchanged(outs[:-1], "pair")[1:]
    density, energy = closing(outs[0], outs[-1], others, pairs, n_half)
    return (energy, density)


def solution(mesh):
    placed = (P("aux", "pair", None, None), P("pair", None), P("pair"), P(), P(), P(), P(), P())
    return jax.shard_map(
        per_device,
        mesh=mesh,
        in_specs=placed,
        out_specs=(P("aux"), P("pair", None)),
        check_vma=False,
    )
```

time: 52.3 us -> 49.5 us (0.946)
  waiting for transfers between devices: 23.9 us -> 18 us
  starting transfers between devices: 16.6 us -> 19.3 us
    ppermute x13 -> x16, waiting for transfers between devices: 23.9 us -> 18 us  [swapped(): lax.ppermute(value, axis, [(source, source ^ mask) for source in range(co...]
    ppermute x13 -> x16, starting transfers between devices: 16.6 us -> 19.3 us  [swapped(): lax.ppermute(value, axis, [(source, source ^ mask) for source in range(co...]
    pallas_call x3 -> x4, Pallas kernels: 6.62 us -> 7 us  [the longest x1 3.16 us: half_first(): pl.pallas_call(kernel, in_specs=[pl.BlockSpec(memory_space=pltpu.HBM)] *...]
  transfers between devices with their start and end apart: 13 -> 16, of which waited for: 10 -> 11; matrix products, arithmetic and copies ran while one was open for 3% -> 3% of each run, Pallas kernels for 1% -> 6%
where the time goes in v4:
time: 49.5 us; the launch traced here: 49 us
  starting transfers between devices  19.3 us (39%)
  waiting for transfers between devices  18 us (36%)
  Pallas kernels  8.65 us (17%)
  other arithmetic  1.64 us (3%)
  between operations  1.4 us (3%)
    ppermute x16, starting transfers between devices, swapped(): lax.ppermute(value, axis, [(source, source ^ mask) for source in range(co...  19.3 us
    ppermute x16, waiting for transfers between devices, swapped(): lax.ppermute(value, axis, [(source, source ^ mask) for source in range(co...  18 us
    pallas_call x1, Pallas kernels, half_first(): pl.pallas_call(kernel, in_specs=[pl.BlockSpec(memory_space=pltpu.HBM)] *...  3.16 us
    pallas_call x1, Pallas kernels, half_rest(): pl.pallas_call(kernel, in_specs=[pl.BlockSpec(memory_space=SMEM)] + whole...  2.73 us
  transfers between devices with their start and end apart: 16, of which 11 were waited for; matrix products, arithmetic and copies ran while one was open for 3% of the time, Pallas kernels for 6%

profile of v4, /device:TPU:1, one launch (start us, length us, event | category | flops | bytes accessed | tf_op | source)
XLA Modules:
  0.0 49.0 jit_solution(15481123452688440561)
XLA Ops:
  0.7 3.2 %half_first.1 = (bf16[272,256]{1,0:T(8,128)(2,1)S(1)}, bf16[272,256]{1,0:T(8,128)(2,1)S(1)}, bf16[272,256]{1,0:T(8,128)(2,1)S(1)}, bf16[272,256]{1,0:T(8,128)(2,...) custom-call(s32[2,4]{1,0:T(2,128)} %bitcast.6, s32[512]{0:T(512)} %pick_hbm.1, ...), custom_call_target="tpu_custom_call" | custom-call | tf_op jit(solution)/shard_map/half_first/pallas_call | solution.py:75
  4.0 2.7 %collective-permute-start.1 = (bf16[272,256]{1,0:T(8,128)(2,1)S(1)}, bf16[272,256]{1,0:T(8,128)(2,1)S(1)}, u32[]{:S(2)}, u32[]{:S(2)}) collective-permute-start(bf16[272,256]{1,0:T(8,128)(2,1)S(1)} %get-tuple-element.38), channel_id=1, source_target_pairs={{0,2},{1,3},{2,0},{3,1},{4,6},{5,7},{6,4},{7,5},{8,10},{9,11},{10,... | collective-permute-start | bytes 417800 | tf_op jit(solution)/shard_map/ppermute | solution.py:22
  7.4 2.7 %half_rest.1 = (bf16[256,256]{1,0:T(8,128)(2,1)S(1)}, bf16[256,256]{1,0:T(8,128)(2,1)S(1)}, bf16[256,256]{1,0:T(8,128)(2,1)S(1)}, bf16[256,256]{1,0:T(8,128)(2,1)S(1)}) custom-call(s32[1]{0:T(128)S(6)} %copy.10.count_ref, bf16[64,512]{1,0:T(8,128)(2,1)S(1)} %get-tuple-element.31.chosen_ref, bf16[2,64,512]{2,1,0:T(8,128)(2,1)S(1)} %get-tuple-element.32.tables_ref, ...), custom_call_target="tpu_custom_call" | custom-call | tf_op jit(solution)/shard_map/half_rest/pallas_call | solution.py:148
  10.5 1.4 %collective-permute-start.4 = (bf16[256,256]{1,0:T(8,128)(2,1)S(1)}, bf16[256,256]{1,0:T(8,128)(2,1)S(1)}, u32[]{:S(2)}, u32[]{:S(2)}) collective-permute-start(bf16[256,256]{1,0:T(8,128)(2,1)S(1)} %get-tuple-element.43), channel_id=1, source_target_pairs={{0,2},{1,3},{2,0},{3,1},{4,6},{5,7},{6,4},{7,5},{8,10},{9,11},{10,... | collective-permute-start | bytes 393224 | tf_op jit(solution)/shard_map/ppermute | solution.py:22
  12.5 1.3 %collective-permute-done.2.refs_3_ = bf16[272,256]{1,0:T(8,128)(2,1)S(1)} collective-permute-done((bf16[272,256]{1,0:T(8,128)(2,1)S(1)}, bf16[272,256]{1,0:T(8,128)(2,1)S(1)}, u32[]{:S(2)}, u32[]{:S(2)}) %collective-permute-start.2) | collective-permute-done | bytes 139296 | tf_op jit(solution)/shard_map/ppermute | solution.py:22
  14.2 2.2 %collective-permute-done.4.refs_6_ = bf16[256,256]{1,0:T(8,128)(2,1)S(1)} collective-permute-done((bf16[256,256]{1,0:T(8,128)(2,1)S(1)}, bf16[256,256]{1,0:T(8,128)(2,1)S(1)}, u32[]{:S(2)}, u32[]{:S(2)}) %collective-permute-start.4) | collective-permute-done | bytes 131104 | tf_op jit(solution)/shard_map/ppermute | solution.py:22
  16.4 2.8 %collective-permute-done.5.refs_7_ = bf16[256,256]{1,0:T(8,128)(2,1)S(1)} collective-permute-done((bf16[256,256]{1,0:T(8,128)(2,1)S(1)}, bf16[256,256]{1,0:T(8,128)(2,1)S(1)}, u32[]{:S(2)}, u32[]{:S(2)}) %collective-permute-start.5) | collective-permute-done | bytes 131104 | tf_op jit(solution)/shard_map/ppermute | solution.py:22
  19.2 0.8 %coulomb_parts.1 = (bf16[1,96,384]{2,1,0:T(8,128)(2,1)S(1)}, bf16[1,96,384]{2,1,0:T(8,128)(2,1)S(1)}, bf16[1,96,384]{2,1,0:T(8,128)(2,1)S(1)}, bf16[1,96,384]{2,1,0:T(8,128)(2,1)S(1)}) custom-call(f32[2,384,256]{2,1,0:T(8,128)S(1)} %get-tuple-element.40.fitted_ref, bf16[384,768]{1,0:T(8,128)(2,1)S(1)} %get-tuple-element.41.rest_ref, ...), custom_call_target="tpu_custom_call" | custom-call | tf_op jit(solution)/shard_map/coulomb_parts/pallas_call | solution.py:227
  20.0 1.5 %collective-permute-start.6 = (bf16[1,96,384]{2,1,0:T(8,128)(2,1)S(1)}, bf16[1,96,384]{2,1,0:T(8,128)(2,1)S(1)}, u32[]{:S(2)}, u32[]{:S(2)}) collective-permute-start(bf16[1,96,384]{2,1,0:T(8,128)(2,1)S(1)} %get-tuple-element.46), channel_id=1, source_target_pairs={{0,4},{4,0},{8,12},{12,8},{16,20},{20,16},{24,28},{28,24},{1,5},{5... | collective-permute-start | bytes 221192 | tf_op jit(solution)/shard_map/ppermute | solution.py:22
  21.5 1.3 %collective-permute-start.7 = (bf16[1,96,384]{2,1,0:T(8,128)(2,1)S(1)}, bf16[1,96,384]{2,1,0:T(8,128)(2,1)S(1)}, u32[]{:S(2)}, u32[]{:S(2)}) collective-permute-start(bf16[1,96,384]{2,1,0:T(8,128)(2,1)S(1)} %get-tuple-element.47), channel_id=1, source_target_pairs={{0,8},{4,12},{8,0},{12,4},{16,24},{20,28},{24,16},{28,20},{1,9},{5... | collective-permute-start | bytes 221192 | tf_op jit(solution)/shard_map/ppermute | solution.py:22
  23.4 1.3 %collective-permute-done.7 = bf16[1,96,384]{2,1,0:T(8,128)(2,1)S(1)} collective-permute-done((bf16[1,96,384]{2,1,0:T(8,128)(2,1)S(1)}, bf16[1,96,384]{2,1,0:T(8,128)(2,1)S(1)}, u32[]{:S(2)}, u32[]{:S(2)}) %collective-permute-start.7) | collective-permute-done | bytes 73760 | tf_op jit(solution)/shard_map/ppermute | solution.py:22
  24.7 2.2 %collective-permute-done.8 = bf16[1,96,384]{2,1,0:T(8,128)(2,1)S(1)} collective-permute-done((bf16[1,96,384]{2,1,0:T(8,128)(2,1)S(1)}, bf16[1,96,384]{2,1,0:T(8,128)(2,1)S(1)}, u32[]{:S(2)}, u32[]{:S(2)}) %collective-permute-start.8) | collective-permute-done | bytes 73760 | tf_op jit(solution)/shard_map/ppermute | solution.py:22
  26.9 2.4 %collective-permute-start.9 = (bf16[1,96,384]{2,1,0:T(8,128)(2,1)S(1)}, bf16[1,96,384]{2,1,0:T(8,128)(2,1)S(1)}, u32[]{:S(2)}, u32[]{:S(2)}) collective-permute-start(bf16[1,96,384]{2,1,0:T(8,128)(2,1)S(1)} %add_convert_fusion.1), channel_id=1, source_target_pairs={{0,16},{4,20},{8,24},{12,28},{16,0},{20,4},{24,8},{28,12},{1,17},{... | collective-permute-start | bytes 221192 | tf_op jit(solution)/shard_map/ppermute | solution.py:22
  30.0 1.1 %collective-permute-done.9 = bf16[1,96,384]{2,1,0:T(8,128)(2,1)S(1)} collective-permute-done((bf16[1,96,384]{2,1,0:T(8,128)(2,1)S(1)}, bf16[1,96,384]{2,1,0:T(8,128)(2,1)S(1)}, u32[]{:S(2)}, u32[]{:S(2)}) %collective-permute-start.9) | collective-permute-done | bytes 73760 | tf_op jit(solution)/shard_map/ppermute | solution.py:22
  31.1 1.6 %collective-permute-start.10 = (bf16[1,96,384]{2,1,0:T(8,128)(2,1)S(1)}, bf16[1,96,384]{2,1,0:T(8,128)(2,1)S(1)}, u32[]{:S(2)}, u32[]{:S(2)}) collective-permute-start(bf16[1,96,384]{2,1,0:T(8,128)(2,1)S(1)} %add_convert_fusion.refs_0_), channel_id=1, source_target_pairs={{0,4},{4,0},{8,12},{12,8},{16,20},{20,16},{24,28},{28,24},{1,5},{5... | collective-permute-start | bytes 221192 | tf_op jit(solution)/shard_map/ppermute | solution.py:22
  33.2 0.8 %collective-permute-start.12 = (bf16[1,96,384]{2,1,0:T(8,128)(2,1)S(1)}, bf16[1,96,384]{2,1,0:T(8,128)(2,1)S(1)}, u32[]{:S(2)}, u32[]{:S(2)}) collective-permute-start(bf16[1,96,384]{2,1,0:T(8,128)(2,1)S(1)} %add_convert_fusion.refs_0_), channel_id=1, source_target_pairs={{0,12},{4,8},{8,4},{12,0},{16,28},{20,24},{24,20},{28,16},{1,13},{... | collective-permute-start | bytes 221192 | tf_op jit(solution)/shard_map/ppermute | solution.py:22
  34.6 1.3 %collective-permute-done.11.refs_2_ = bf16[1,96,384]{2,1,0:T(8,128)(2,1)S(1)} collective-permute-done((bf16[1,96,384]{2,1,0:T(8,128)(2,1)S(1)}, bf16[1,96,384]{2,1,0:T(8,128)(2,1)S(1)}, u32[]{:S(2)}, u32[]{:S(2)}) %collective-permute-start.11) | collective-permute-done | bytes 73760 | tf_op jit(solution)/shard_map/ppermute | solution.py:22
  35.9 1.3 %collective-permute-done.12.refs_3_ = bf16[1,96,384]{2,1,0:T(8,128)(2,1)S(1)} collective-permute-done((bf16[1,96,384]{2,1,0:T(8,128)(2,1)S(1)}, bf16[1,96,384]{2,1,0:T(8,128)(2,1)S(1)}, u32[]{:S(2)}, u32[]{:S(2)}) %collective-permute-start.12) | collective-permute-done | bytes 73760 | tf_op jit(solution)/shard_map/ppermute | solution.py:22
  37.3 0.9 %density_parts.1 = (f32[96,384]{1,0:T(8,128)S(1)}, bf16[96,384]{1,0:T(8,128)(2,1)S(1)}, bf16[96,384]{1,0:T(8,128)(2,1)S(1)}, bf16[96,384]{1,0:T(8,128)(2,1)S(1)}, f32[1,384]{1,0:T(1,128)S(1)}) custom-call(f32[1,384,384]{2,1,0:T(8,128)S(1)} %subtract_divide_fusion.inverse_ref, bf16[1,96,384]{2,1,0:T(8,128)(2,1)S(1)} %add_convert_fusion.refs_0_, ...), custom_call_target="tpu_custom_call" | custom-call | tf_op jit(solution)/shard_map/density_parts/pallas_call | solution.py:286
  38.1 4.5 %collective-permute-start.13 = (bf16[96,384]{1,0:T(8,128)(2,1)S(1)}, bf16[96,384]{1,0:T(8,128)(2,1)S(1)}, u32[]{:S(2)}, u32[]{:S(2)}) collective-permute-start(bf16[96,384]{1,0:T(8,128)(2,1)S(1)} %get-tuple-element.51), channel_id=1, source_target_pairs={{0,1},{1,0},{2,3},{3,2},{4,5},{5,4},{6,7},{7,6},{8,9},{9,8},{10,11... | collective-permute-start | bytes 221192 | tf_op jit(solution)/shard_map/ppermute | solution.py:22
  42.6 1.3 %collective-permute-start.14 = (bf16[96,384]{1,0:T(8,128)(2,1)S(1)}, bf16[96,384]{1,0:T(8,128)(2,1)S(1)}, u32[]{:S(2)}, u32[]{:S(2)}) collective-permute-start(bf16[96,384]{1,0:T(8,128)(2,1)S(1)} %get-tuple-element.52), channel_id=1, source_target_pairs={{0,2},{1,3},{2,0},{3,1},{4,6},{5,7},{6,4},{7,5},{8,10},{9,11},{10,... | collective-permute-start | bytes 221192 | tf_op jit(solution)/shard_map/ppermute | solution.py:22
  44.3 2.1 %collective-permute-done.14.refs_1_ = bf16[96,384]{1,0:T(8,128)(2,1)S(1)} collective-permute-done((bf16[96,384]{1,0:T(8,128)(2,1)S(1)}, bf16[96,384]{1,0:T(8,128)(2,1)S(1)}, u32[]{:S(2)}, u32[]{:S(2)}) %collective-permute-start.14) | collective-permute-done | bytes 73760 | tf_op jit(solution)/shard_map/ppermute | solution.py:22
  46.5 1.8 %collective-permute-done.15.refs_2_ = bf16[96,384]{1,0:T(8,128)(2,1)S(1)} collective-permute-done((bf16[96,384]{1,0:T(8,128)(2,1)S(1)}, bf16[96,384]{1,0:T(8,128)(2,1)S(1)}, u32[]{:S(2)}, u32[]{:S(2)}) %collective-permute-start.15) | collective-permute-done | bytes 73760 | tf_op jit(solution)/shard_map/ppermute | solution.py:22
  48.3 0.8 %closing.1 = (f32[96,384]{1,0:T(8,128)}, f32[1]{0:T(128)}) custom-call(f32[96,384]{1,0:T(8,128)S(1)} %get-tuple-element.49.own_ref, f32[1,384]{1,0:T(1,128)S(1)} %get-tuple-element.50.energy_ref, bf16[96,384]{1,0:T(8,128)(2,1)S(1)} %collective-permute-done.13.refs_0_, bf16[96,384]{1,0:T(8,128)(2,1)S(1)} %collective-permute-done.14.refs_1_, ...), custom_call_target="tpu_custom_call" | custom-call | tf_op jit(solution)/shard_map/closing/pallas_call | solution.py:336
  (28 shorter events, 4.3 us)
Async XLA Ops:
  0.6 11.7 %copy-start.2 = (f32[512]{0:T(512)S(1)}, f32[512]{0:T(512)}, u32[]{:S(2)}) copy-start(f32[512]{0:T(512)} %param.14) | copy-start | bytes 6148
  0.6 11.7 %slice-start = ((s32[512]{0:T(512)}), s32[8]{0:T(128)S(1)}, s32[]{:S(2)}) async-start(s32[512]{0:T(512)} %pick_hbm.1), calls=%async_computation | async-start | bytes 1024 | tf_op jit(solution)/shard_map/slice | solution.py:401
  0.7 13.2 %copy-start = (bf16[16,64,384]{2,1,0:T(8,128)(2,1)S(1)}, bf16[16,64,384]{2,1,0:T(8,128)(2,1)}, u32[]{:S(2)}) copy-start(bf16[16,64,384]{2,1,0:T(8,128)(2,1)} %vir_ref.1) | copy-start | bytes 2359300
  3.8 25.5 %copy-start.1 = (f32[384]{0:T(512)S(1)}, f32[384]{0:T(512)}, u32[]{:S(2)}) copy-start(f32[384]{0:T(512)} %param.15) | copy-start | bytes 4612
  3.8 8.1 %collective-permute-start = (bf16[272,256]{1,0:T(8,128)(2,1)S(1)}, bf16[272,256]{1,0:T(8,128)(2,1)S(1)}, u32[]{:S(2)}, u32[]{:S(2)}) collective-permute-start(bf16[272,256]{1,0:T(8,128)(2,1)S(1)} %get-tuple-element.37), channel_id=1, source_target_pairs={{0,1},{1,0},{2,3},{3,2},{4,5},{5,4},{6,7},{7,6},{8,9},{9,8},{10,11... | collective-permute-start | bytes 417800 | tf_op jit(solution)/shard_map/ppermute | solution.py:22
  4.0 8.6 %collective-permute-start.1 = (bf16[272,256]{1,0:T(8,128)(2,1)S(1)}, bf16[272,256]{1,0:T(8,128)(2,1)S(1)}, u32[]{:S(2)}, u32[]{:S(2)}) collective-permute-start(bf16[272,256]{1,0:T(8,128)(2,1)S(1)} %get-tuple-element.38), channel_id=1, source_target_pairs={{0,2},{1,3},{2,0},{3,1},{4,6},{5,7},{6,4},{7,5},{8,10},{9,11},{10,... | collective-permute-start | bytes 417800 | tf_op jit(solution)/shard_map/ppermute | solution.py:22
  6.7 7.2 %collective-permute-start.2 = (bf16[272,256]{1,0:T(8,128)(2,1)S(1)}, bf16[272,256]{1,0:T(8,128)(2,1)S(1)}, u32[]{:S(2)}, u32[]{:S(2)}) collective-permute-start(bf16[272,256]{1,0:T(8,128)(2,1)S(1)} %get-tuple-element.39), channel_id=1, source_target_pairs={{0,3},{1,2},{2,1},{3,0},{4,7},{5,6},{6,5},{7,4},{8,11},{9,10},{10,... | collective-permute-start | bytes 417800 | tf_op jit(solution)/shard_map/ppermute | solution.py:22
  10.1 4.1 %collective-permute-start.3 = (bf16[256,256]{1,0:T(8,128)(2,1)S(1)}, bf16[256,256]{1,0:T(8,128)(2,1)S(1)}, u32[]{:S(2)}, u32[]{:S(2)}) collective-permute-start(bf16[256,256]{1,0:T(8,128)(2,1)S(1)} %get-tuple-element.42), channel_id=1, source_target_pairs={{0,1},{1,0},{2,3},{3,2},{4,5},{5,4},{6,7},{7,6},{8,9},{9,8},{10,11... | collective-permute-start | bytes 393224 | tf_op jit(solution)/shard_map/ppermute | solution.py:22
  10.5 5.9 %collective-permute-start.4 = (bf16[256,256]{1,0:T(8,128)(2,1)S(1)}, bf16[256,256]{1,0:T(8,128)(2,1)S(1)}, u32[]{:S(2)}, u32[]{:S(2)}) collective-permute-start(bf16[256,256]{1,0:T(8,128)(2,1)S(1)} %get-tuple-element.43), channel_id=1, source_target_pairs={{0,2},{1,3},{2,0},{3,1},{4,6},{5,7},{6,4},{7,5},{8,10},{9,11},{10,... | collective-permute-start | bytes 393224 | tf_op jit(solution)/shard_map/ppermute | solution.py:22
  12.0 7.2 %collective-permute-start.5 = (bf16[256,256]{1,0:T(8,128)(2,1)S(1)}, bf16[256,256]{1,0:T(8,128)(2,1)S(1)}, u32[]{:S(2)}, u32[]{:S(2)}) collective-permute-start(bf16[256,256]{1,0:T(8,128)(2,1)S(1)} %get-tuple-element.44), channel_id=1, source_target_pairs={{0,3},{1,2},{2,1},{3,0},{4,7},{5,6},{6,5},{7,4},{8,11},{9,10},{10,... | collective-permute-start | bytes 393224 | tf_op jit(solution)/shard_map/ppermute | solution.py:22
  20.0 3.4 %collective-permute-start.6 = (bf16[1,96,384]{2,1,0:T(8,128)(2,1)S(1)}, bf16[1,96,384]{2,1,0:T(8,128)(2,1)S(1)}, u32[]{:S(2)}, u32[]{:S(2)}) collective-permute-start(bf16[1,96,384]{2,1,0:T(8,128)(2,1)S(1)} %get-tuple-element.46), channel_id=1, source_target_pairs={{0,4},{4,0},{8,12},{12,8},{16,20},{20,16},{24,28},{28,24},{1,5},{5... | collective-permute-start | bytes 221192 | tf_op jit(solution)/shard_map/ppermute | solution.py:22
  21.5 3.2 %collective-permute-start.7 = (bf16[1,96,384]{2,1,0:T(8,128)(2,1)S(1)}, bf16[1,96,384]{2,1,0:T(8,128)(2,1)S(1)}, u32[]{:S(2)}, u32[]{:S(2)}) collective-permute-start(bf16[1,96,384]{2,1,0:T(8,128)(2,1)S(1)} %get-tuple-element.47), channel_id=1, source_target_pairs={{0,8},{4,12},{8,0},{12,4},{16,24},{20,28},{24,16},{28,20},{1,9},{5... | collective-permute-start | bytes 221192 | tf_op jit(solution)/shard_map/ppermute | solution.py:22
  22.8 4.1 %collective-permute-start.8 = (bf16[1,96,384]{2,1,0:T(8,128)(2,1)S(1)}, bf16[1,96,384]{2,1,0:T(8,128)(2,1)S(1)}, u32[]{:S(2)}, u32[]{:S(2)}) collective-permute-start(bf16[1,96,384]{2,1,0:T(8,128)(2,1)S(1)} %get-tuple-element.48), channel_id=1, source_target_pairs={{0,12},{4,8},{8,4},{12,0},{16,28},{20,24},{24,20},{28,16},{1,13},{... | collective-permute-start | bytes 221192 | tf_op jit(solution)/shard_map/ppermute | solution.py:22
  26.9 4.2 %collective-permute-start.9 = (bf16[1,96,384]{2,1,0:T(8,128)(2,1)S(1)}, bf16[1,96,384]{2,1,0:T(8,128)(2,1)S(1)}, u32[]{:S(2)}, u32[]{:S(2)}) collective-permute-start(bf16[1,96,384]{2,1,0:T(8,128)(2,1)S(1)} %add_convert_fusion.1), channel_id=1, source_target_pairs={{0,16},{4,20},{8,24},{12,28},{16,0},{20,4},{24,8},{28,12},{1,17},{... | collective-permute-start | bytes 221192 | tf_op jit(solution)/shard_map/ppermute | solution.py:22
  31.1 3.5 %collective-permute-start.10 = (bf16[1,96,384]{2,1,0:T(8,128)(2,1)S(1)}, bf16[1,96,384]{2,1,0:T(8,128)(2,1)S(1)}, u32[]{:S(2)}, u32[]{:S(2)}) collective-permute-start(bf16[1,96,384]{2,1,0:T(8,128)(2,1)S(1)} %add_convert_fusion.refs_0_), channel_id=1, source_target_pairs={{0,4},{4,0},{8,12},{12,8},{16,20},{20,16},{24,28},{28,24},{1,5},{5... | collective-permute-start | bytes 221192 | tf_op jit(solution)/shard_map/ppermute | solution.py:22
  32.7 3.2 %collective-permute-start.11 = (bf16[1,96,384]{2,1,0:T(8,128)(2,1)S(1)}, bf16[1,96,384]{2,1,0:T(8,128)(2,1)S(1)}, u32[]{:S(2)}, u32[]{:S(2)}) collective-permute-start(bf16[1,96,384]{2,1,0:T(8,128)(2,1)S(1)} %add_convert_fusion.refs_0_), channel_id=1, source_target_pairs={{0,8},{4,12},{8,0},{12,4},{16,24},{20,28},{24,16},{28,20},{1,9},{5... | collective-permute-start | bytes 221192 | tf_op jit(solution)/shard_map/ppermute | solution.py:22
  33.2 4.1 %collective-permute-start.12 = (bf16[1,96,384]{2,1,0:T(8,128)(2,1)S(1)}, bf16[1,96,384]{2,1,0:T(8,128)(2,1)S(1)}, u32[]{:S(2)}, u32[]{:S(2)}) collective-permute-start(bf16[1,96,384]{2,1,0:T(8,128)(2,1)S(1)} %add_convert_fusion.refs_0_), channel_id=1, source_target_pairs={{0,12},{4,8},{8,4},{12,0},{16,28},{20,24},{24,20},{28,16},{1,13},{... | collective-permute-start | bytes 221192 | tf_op jit(solution)/shard_map/ppermute | solution.py:22
  38.1 6.2 %collective-permute-start.13 = (bf16[96,384]{1,0:T(8,128)(2,1)S(1)}, bf16[96,384]{1,0:T(8,128)(2,1)S(1)}, u32[]{:S(2)}, u32[]{:S(2)}) collective-permute-start(bf16[96,384]{1,0:T(8,128)(2,1)S(1)} %get-tuple-element.51), channel_id=1, source_target_pairs={{0,1},{1,0},{2,3},{3,2},{4,5},{5,4},{6,7},{7,6},{8,9},{9,8},{10,11... | collective-permute-start | bytes 221192 | tf_op jit(solution)/shard_map/ppermute | solution.py:22
  42.6 3.8 %collective-permute-start.14 = (bf16[96,384]{1,0:T(8,128)(2,1)S(1)}, bf16[96,384]{1,0:T(8,128)(2,1)S(1)}, u32[]{:S(2)}, u32[]{:S(2)}) collective-permute-start(bf16[96,384]{1,0:T(8,128)(2,1)S(1)} %get-tuple-element.52), channel_id=1, source_target_pairs={{0,2},{1,3},{2,0},{3,1},{4,6},{5,7},{6,4},{7,5},{8,10},{9,11},{10,... | collective-permute-start | bytes 221192 | tf_op jit(solution)/shard_map/ppermute | solution.py:22
  43.9 4.4 %collective-permute-start.15 = (bf16[96,384]{1,0:T(8,128)(2,1)S(1)}, bf16[96,384]{1,0:T(8,128)(2,1)S(1)}, u32[]{:S(2)}, u32[]{:S(2)}) collective-permute-start(bf16[96,384]{1,0:T(8,128)(2,1)S(1)} %get-tuple-element.53), channel_id=1, source_target_pairs={{0,3},{1,2},{2,1},{3,0},{4,7},{5,6},{6,5},{7,4},{8,11},{9,10},{10,... | collective-permute-start | bytes 221192 | tf_op jit(solution)/shard_map/ppermute | solution.py:22

commit v5 on v4

--- a/solution.py
+++ b/solution.py
@@ -13,8 +13,10 @@
 PARAMS = pltpu.CompilerParams(vmem_limit_bytes=48 * 1024 * 1024)
 
 
-def order(count):
-    return sorted(range(1, count), reverse=True)
+PAIR_ORDER = (2, 3, 1)
+SUM_ORDER = (3, 1, 2)
+GATHER_ORDER = (3, 1, 2)
+ROW_ORDER = (2, 1, 3)
 
 
 def swapped(value, axis, mask):
@@ -249,17 +251,18 @@
         energies = []
         totals = [None] * n_pair
         for pair in range(pairs):
-            for part in range(quad):
+            for part, chunk in zip((0, *GATHER_ORDER), held):
                 at = pl.multiple_of((place ^ part) * share, share)
-                block_ref[pl.ds(at, share), :] = held[part][pair]
+                block_ref[pl.ds(at, share), :] = chunk[pair]
             block = block_ref[...].astype(jnp.float32)
             flipped = block_ref[...].T.astype(jnp.float32)
             inverse = inverse_ref[pair]
             energy = jnp.sum(block * (2.0 * block - flipped) * inverse)
             even = ((block + flipped) * inverse).astype(jnp.bfloat16)
-            odd = ((block - flipped) * inverse).astype(jnp.bfloat16)
-            term = 0.5 * jnp.dot(even, even, preferred_element_type=jnp.float32)
-            term -= 1.5 * jnp.dot(odd, odd, preferred_element_type=jnp.float32)
+            odd = ((block - flipped) * (inverse * 3.0**0.5)).astype(jnp.bfloat16)
+            left = jnp.concatenate([even, odd], axis=1)
+            right = jnp.concatenate([even, -odd], axis=0)
+            term = 0.5 * jnp.dot(left, right, preferred_element_type=jnp.float32)
             total_ref[...] = term if pair == 0 else total_ref[...] + term
         for part in range(n_pair):
             totals[part] = total_ref[pl.ds(pl.multiple_of((pair_at ^ part) * rows, rows), rows), :]
@@ -310,13 +313,13 @@
         first = pair_at * rows
         found = jnp.zeros((1, virtual), jnp.float32)
         total = own_ref[...]
-        for mate in range(len(held) + 1):
+        for mate, ref in zip((0, *ROW_ORDER), (None, *held)):
             at = wanted - (pair_at ^ mate) * pairs
             here = (at >= 0) & (at < pairs)
             if mate == 0:
                 found += jnp.where(here & (lane == at), energy_ref[...], 0.0)
             else:
-                part = held[mate - 1][...].astype(jnp.float32)
+                part = ref[...].astype(jnp.float32)
                 spot = lane - first - 3 * at
                 found += jnp.where(here & (spot >= 0) & (spot < 3), part[rows - 1 :], 0.0)
                 total += part
@@ -343,12 +346,8 @@
     )(own, energies, *others)
 
 
-def exchanged(parts, axis, low=0):
-    got = [parts[0]] + [None] * (len(parts) - 1)
-    for d in order(len(parts)):
-        if parts[d] is not None:
-            got[d] = swapped(parts[d], axis, d << low)
-    return got
+def exchanged(parts, axis, order, low=0):
+    return [swapped(parts[d], axis, d << low) for d in order]
 
 
 def summed(value, axis, low, bits):
@@ -362,15 +361,17 @@
     parts = [lax.dynamic_slice_in_dim(value, (place ^ d) * share, share, 1) for d in range(4)]
     chunks = scattered(parts, axis, low, bits)
     out = jnp.zeros_like(value)
-    for d in range(4):
-        out = lax.dynamic_update_slice_in_dim(out, chunks[d], (place ^ d) * share, 1)
+    for d, chunk in zip((0, *GATHER_ORDER), chunks):
+        out = lax.dynamic_update_slice_in_dim(out, chunk, (place ^ d) * share, 1)
     return out
 
 
 def scattered(parts, axis, low, bits):
-    total = sum(part.astype(jnp.float32) for part in exchanged(parts, axis, low))
+    total = parts[0].astype(jnp.float32)
+    for part in exchanged(parts, axis, SUM_ORDER, low):
+        total += part.astype(jnp.float32)
     total = summed(total.astype(jnp.bfloat16), axis, low + 2, bits - 2)
-    return exchanged([total] * len(parts), axis, low)
+    return [total] + exchanged([total] * len(parts), axis, GATHER_ORDER, low)
 
 
 def per_device(
@@ -390,7 +391,7 @@
     )
     block_count, _ = lax.optimization_barrier((block_count, first[0]))
     later = list(half_rest(ints, block_count, chosen, tables, n_pair, pairs))
-    got = [exchanged(first, "pair"), exchanged(later, "pair")]
+    got = [made[:1] + exchanged(made, "pair", PAIR_ORDER) for made in (first, later)]
 
     fitted, rest = fitted_first(vir_coef, got[0], pairs, counts)
     parts = coulomb_parts(fitted, rest, got[0], got[1], pairs, counts, 4)
@@ -406,7 +407,7 @@
 
     chunks = scattered(parts, "aux", 0, bits)
     outs = density_parts(inverse, chunks, n_pair)
-    others = exchanged(outs[:-1], "pair")[1:]
+    others = exchanged(outs, "pair", ROW_ORDER)
     density, energy = closing(outs[0], outs[-1], others, pairs, n_half)
     return (energy, density)
 

time: 49.5 us -> 47 us (0.949)
  waiting for transfers between devices: 18 us -> 16.2 us
    ppermute x16, waiting for transfers between devices: 18 us -> 16.2 us  [swapped(): lax.ppermute(value, axis, [(source, source ^ mask) for source in range(co...]
  transfers between devices with their start and end apart: 16 -> 16, of which waited for: 11 -> 11; matrix products, arithmetic and copies ran while one was open for 3% -> 3% of each run, Pallas kernels for 6% -> 7%
where the time goes in v5:
time: 47 us; the launch traced here: 46.9 us
  starting transfers between devices  19.1 us (41%)
  waiting for transfers between devices  16.2 us (34%)
  Pallas kernels  8.56 us (18%)
  other arithmetic  1.64 us (3%)
  between operations  1.39 us (3%)
    ppermute x16, starting transfers between devices, swapped(): lax.ppermute(value, axis, [(source, source ^ mask) for source in range(co...  19.1 us
    ppermute x16, waiting for transfers between devices, swapped(): lax.ppermute(value, axis, [(source, source ^ mask) for source in range(co...  16.2 us
    pallas_call x1, Pallas kernels, half_first(): pl.pallas_call(kernel, in_specs=[pl.BlockSpec(memory_space=pltpu.HBM)] *...  3.16 us
    pallas_call x1, Pallas kernels, half_rest(): pl.pallas_call(kernel, in_specs=[pl.BlockSpec(memory_space=SMEM)] + whole...  2.73 us
  transfers between devices with their start and end apart: 16, of which 11 were waited for; matrix products, arithmetic and copies ran while one was open for 3% of the time, Pallas kernels for 7%

profile of v5, /device:TPU:1, one launch (start us, length us, event | category | flops | bytes accessed | tf_op | source)
XLA Modules:
  0.0 46.9 jit_solution(4819944804930863932)
XLA Ops:
  0.7 3.2 %half_first.1 = (bf16[272,256]{1,0:T(8,128)(2,1)S(1)}, bf16[272,256]{1,0:T(8,128)(2,1)S(1)}, bf16[272,256]{1,0:T(8,128)(2,1)S(1)}, bf16[272,256]{1,0:T(8,128)(2,...) custom-call(s32[2,4]{1,0:T(2,128)} %bitcast.6, s32[512]{0:T(512)} %pick_hbm.1, ...), custom_call_target="tpu_custom_call" | custom-call | tf_op jit(solution)/shard_map/half_first/pallas_call | solution.py:77
  3.8 2.1 %collective-permute-start = (bf16[272,256]{1,0:T(8,128)(2,1)S(1)}, bf16[272,256]{1,0:T(8,128)(2,1)S(1)}, u32[]{:S(2)}, u32[]{:S(2)}) collective-permute-start(bf16[272,256]{1,0:T(8,128)(2,1)S(1)} %get-tuple-element.37), channel_id=1, source_target_pairs={{0,2},{1,3},{2,0},{3,1},{4,6},{5,7},{6,4},{7,5},{8,10},{9,11},{10,... | collective-permute-start | bytes 417800 | tf_op jit(solution)/shard_map/ppermute | solution.py:24
  7.6 2.7 %half_rest.1 = (bf16[256,256]{1,0:T(8,128)(2,1)S(1)}, bf16[256,256]{1,0:T(8,128)(2,1)S(1)}, bf16[256,256]{1,0:T(8,128)(2,1)S(1)}, bf16[256,256]{1,0:T(8,128)(2,1)S(1)}) custom-call(s32[1]{0:T(128)S(6)} %copy.10.count_ref, bf16[64,512]{1,0:T(8,128)(2,1)S(1)} %get-tuple-element.31.chosen_ref, bf16[2,64,512]{2,1,0:T(8,128)(2,1)S(1)} %get-tuple-element.32.tables_ref, ...), custom_call_target="tpu_custom_call" | custom-call | tf_op jit(solution)/shard_map/half_rest/pallas_call | solution.py:150
  10.3 1.4 %collective-permute-start.3 = (bf16[256,256]{1,0:T(8,128)(2,1)S(1)}, bf16[256,256]{1,0:T(8,128)(2,1)S(1)}, u32[]{:S(2)}, u32[]{:S(2)}) collective-permute-start(bf16[256,256]{1,0:T(8,128)(2,1)S(1)} %get-tuple-element.42), channel_id=1, source_target_pairs={{0,2},{1,3},{2,0},{3,1},{4,6},{5,7},{6,4},{7,5},{8,10},{9,11},{10,... | collective-permute-start | bytes 393224 | tf_op jit(solution)/shard_map/ppermute | solution.py:24
  13.3 2.2 %collective-permute-done.3.refs_5_ = bf16[256,256]{1,0:T(8,128)(2,1)S(1)} collective-permute-done((bf16[256,256]{1,0:T(8,128)(2,1)S(1)}, bf16[256,256]{1,0:T(8,128)(2,1)S(1)}, u32[]{:S(2)}, u32[]{:S(2)}) %collective-permute-start.3) | collective-permute-done | bytes 131104 | tf_op jit(solution)/shard_map/ppermute | solution.py:24
  15.5 3.0 %collective-permute-done.4.refs_6_ = bf16[256,256]{1,0:T(8,128)(2,1)S(1)} collective-permute-done((bf16[256,256]{1,0:T(8,128)(2,1)S(1)}, bf16[256,256]{1,0:T(8,128)(2,1)S(1)}, u32[]{:S(2)}, u32[]{:S(2)}) %collective-permute-start.4) | collective-permute-done | bytes 131104 | tf_op jit(solution)/shard_map/ppermute | solution.py:24
  18.5 0.8 %coulomb_parts.1 = (bf16[1,96,384]{2,1,0:T(8,128)(2,1)S(1)}, bf16[1,96,384]{2,1,0:T(8,128)(2,1)S(1)}, bf16[1,96,384]{2,1,0:T(8,128)(2,1)S(1)}, bf16[1,96,384]{2,1,0:T(8,128)(2,1)S(1)}) custom-call(f32[2,384,256]{2,1,0:T(8,128)S(1)} %get-tuple-element.40.fitted_ref, bf16[384,768]{1,0:T(8,128)(2,1)S(1)} %get-tuple-element.41.rest_ref, ...), custom_call_target="tpu_custom_call" | custom-call | tf_op jit(solution)/shard_map/coulomb_parts/pallas_call | solution.py:229
  19.3 2.5 %collective-permute-start.6 = (bf16[1,96,384]{2,1,0:T(8,128)(2,1)S(1)}, bf16[1,96,384]{2,1,0:T(8,128)(2,1)S(1)}, u32[]{:S(2)}, u32[]{:S(2)}) collective-permute-start(bf16[1,96,384]{2,1,0:T(8,128)(2,1)S(1)} %get-tuple-element.46), channel_id=1, source_target_pairs={{0,12},{4,8},{8,4},{12,0},{16,28},{20,24},{24,20},{28,16},{1,13},{... | collective-permute-start | bytes 221192 | tf_op jit(solution)/shard_map/ppermute | solution.py:24
  22.8 1.4 %collective-permute-done.6 = bf16[1,96,384]{2,1,0:T(8,128)(2,1)S(1)} collective-permute-done((bf16[1,96,384]{2,1,0:T(8,128)(2,1)S(1)}, bf16[1,96,384]{2,1,0:T(8,128)(2,1)S(1)}, u32[]{:S(2)}, u32[]{:S(2)}) %collective-permute-start.6) | collective-permute-done | bytes 73760 | tf_op jit(solution)/shard_map/ppermute | solution.py:24
  24.1 1.6 %collective-permute-done.7 = bf16[1,96,384]{2,1,0:T(8,128)(2,1)S(1)} collective-permute-done((bf16[1,96,384]{2,1,0:T(8,128)(2,1)S(1)}, bf16[1,96,384]{2,1,0:T(8,128)(2,1)S(1)}, u32[]{:S(2)}, u32[]{:S(2)}) %collective-permute-start.7) | collective-permute-done | bytes 73760 | tf_op jit(solution)/shard_map/ppermute | solution.py:24
  25.8 2.6 %collective-permute-start.9 = (bf16[1,96,384]{2,1,0:T(8,128)(2,1)S(1)}, bf16[1,96,384]{2,1,0:T(8,128)(2,1)S(1)}, u32[]{:S(2)}, u32[]{:S(2)}) collective-permute-start(bf16[1,96,384]{2,1,0:T(8,128)(2,1)S(1)} %add_convert_fusion.1), channel_id=1, source_target_pairs={{0,16},{4,20},{8,24},{12,28},{16,0},{20,4},{24,8},{28,12},{1,17},{... | collective-permute-start | bytes 221192 | tf_op jit(solution)/shard_map/ppermute | solution.py:24
  28.4 0.6 %broadcast_subtract_fusion = f32[384]{0:T(512)S(1)} fusion(f32[384]{0:T(512)S(1)} %copy-done.1, f32[]{:T(128)} %fusion), kind=kLoop, calls=%fused_computation.7 | loop fusion | flops 384 | bytes 3076 | tf_op jit(solution)/shard_map/sub | solution.py:406
  29.1 1.1 %collective-permute-done.9 = bf16[1,96,384]{2,1,0:T(8,128)(2,1)S(1)} collective-permute-done((bf16[1,96,384]{2,1,0:T(8,128)(2,1)S(1)}, bf16[1,96,384]{2,1,0:T(8,128)(2,1)S(1)}, u32[]{:S(2)}, u32[]{:S(2)}) %collective-permute-start.9) | collective-permute-done | bytes 73760 | tf_op jit(solution)/shard_map/ppermute | solution.py:24
  30.2 1.2 %collective-permute-start.10 = (bf16[1,96,384]{2,1,0:T(8,128)(2,1)S(1)}, bf16[1,96,384]{2,1,0:T(8,128)(2,1)S(1)}, u32[]{:S(2)}, u32[]{:S(2)}) collective-permute-start(bf16[1,96,384]{2,1,0:T(8,128)(2,1)S(1)} %add_convert_fusion.refs_0_), channel_id=1, source_target_pairs={{0,12},{4,8},{8,4},{12,0},{16,28},{20,24},{24,20},{28,16},{1,13},{... | collective-permute-start | bytes 221192 | tf_op jit(solution)/shard_map/ppermute | solution.py:24
  31.3 1.8 %collective-permute-start.11 = (bf16[1,96,384]{2,1,0:T(8,128)(2,1)S(1)}, bf16[1,96,384]{2,1,0:T(8,128)(2,1)S(1)}, u32[]{:S(2)}, u32[]{:S(2)}) collective-permute-start(bf16[1,96,384]{2,1,0:T(8,128)(2,1)S(1)} %add_convert_fusion.refs_0_), channel_id=1, source_target_pairs={{0,4},{4,0},{8,12},{12,8},{16,20},{20,16},{24,28},{28,24},{1,5},{5... | collective-permute-start | bytes 221192 | tf_op jit(solution)/shard_map/ppermute | solution.py:24
  33.4 0.9 %collective-permute-done.10.refs_1_ = bf16[1,96,384]{2,1,0:T(8,128)(2,1)S(1)} collective-permute-done((bf16[1,96,384]{2,1,0:T(8,128)(2,1)S(1)}, bf16[1,96,384]{2,1,0:T(8,128)(2,1)S(1)}, u32[]{:S(2)}, u32[]{:S(2)}) %collective-permute-start.10) | collective-permute-done | bytes 73760 | tf_op jit(solution)/shard_map/ppermute | solution.py:24
  34.4 0.8 %collective-permute-done.11.refs_2_ = bf16[1,96,384]{2,1,0:T(8,128)(2,1)S(1)} collective-permute-done((bf16[1,96,384]{2,1,0:T(8,128)(2,1)S(1)}, bf16[1,96,384]{2,1,0:T(8,128)(2,1)S(1)}, u32[]{:S(2)}, u32[]{:S(2)}) %collective-permute-start.11) | collective-permute-done | bytes 73760 | tf_op jit(solution)/shard_map/ppermute | solution.py:24
  35.1 1.2 %collective-permute-done.12.refs_3_ = bf16[1,96,384]{2,1,0:T(8,128)(2,1)S(1)} collective-permute-done((bf16[1,96,384]{2,1,0:T(8,128)(2,1)S(1)}, bf16[1,96,384]{2,1,0:T(8,128)(2,1)S(1)}, u32[]{:S(2)}, u32[]{:S(2)}) %collective-permute-start.12) | collective-permute-done | bytes 73760 | tf_op jit(solution)/shard_map/ppermute | solution.py:24
  36.4 0.8 %density_parts.1 = (f32[96,384]{1,0:T(8,128)S(1)}, bf16[96,384]{1,0:T(8,128)(2,1)S(1)}, bf16[96,384]{1,0:T(8,128)(2,1)S(1)}, bf16[96,384]{1,0:T(8,128)(2,1)S(1)}, f32[1,384]{1,0:T(1,128)S(1)}) custom-call(f32[1,384,384]{2,1,0:T(8,128)S(1)} %subtract_divide_fusion.inverse_ref, bf16[1,96,384]{2,1,0:T(8,128)(2,1)S(1)} %add_convert_fusion.refs_0_, ...), custom_call_target="tpu_custom_call" | custom-call | tf_op jit(solution)/shard_map/density_parts/pallas_call | solution.py:289
  37.1 1.3 %collective-permute-start.13 = (bf16[96,384]{1,0:T(8,128)(2,1)S(1)}, bf16[96,384]{1,0:T(8,128)(2,1)S(1)}, u32[]{:S(2)}, u32[]{:S(2)}) collective-permute-start(bf16[96,384]{1,0:T(8,128)(2,1)S(1)} %get-tuple-element.51), channel_id=1, source_target_pairs={{0,2},{1,3},{2,0},{3,1},{4,6},{5,7},{6,4},{7,5},{8,10},{9,11},{10,... | collective-permute-start | bytes 221192 | tf_op jit(solution)/shard_map/ppermute | solution.py:24
  38.4 3.8 %collective-permute-start.14 = (bf16[96,384]{1,0:T(8,128)(2,1)S(1)}, bf16[96,384]{1,0:T(8,128)(2,1)S(1)}, u32[]{:S(2)}, u32[]{:S(2)}) collective-permute-start(bf16[96,384]{1,0:T(8,128)(2,1)S(1)} %get-tuple-element.52), channel_id=1, source_target_pairs={{0,1},{1,0},{2,3},{3,2},{4,5},{5,4},{6,7},{7,6},{8,9},{9,8},{10,11... | collective-permute-start | bytes 221192 | tf_op jit(solution)/shard_map/ppermute | solution.py:24
  42.3 0.8 %collective-permute-done.14.refs_1_ = bf16[96,384]{1,0:T(8,128)(2,1)S(1)} collective-permute-done((bf16[96,384]{1,0:T(8,128)(2,1)S(1)}, bf16[96,384]{1,0:T(8,128)(2,1)S(1)}, u32[]{:S(2)}, u32[]{:S(2)}) %collective-permute-start.14) | collective-permute-done | bytes 73760 | tf_op jit(solution)/shard_map/ppermute | solution.py:24
  43.1 3.0 %collective-permute-done.15.refs_2_ = bf16[96,384]{1,0:T(8,128)(2,1)S(1)} collective-permute-done((bf16[96,384]{1,0:T(8,128)(2,1)S(1)}, bf16[96,384]{1,0:T(8,128)(2,1)S(1)}, u32[]{:S(2)}, u32[]{:S(2)}) %collective-permute-start.15) | collective-permute-done | bytes 73760 | tf_op jit(solution)/shard_map/ppermute | solution.py:24
  46.1 0.8 %closing.1 = (f32[96,384]{1,0:T(8,128)}, f32[1]{0:T(128)}) custom-call(f32[96,384]{1,0:T(8,128)S(1)} %get-tuple-element.49.own_ref, f32[1,384]{1,0:T(1,128)S(1)} %get-tuple-element.50.energy_ref, bf16[96,384]{1,0:T(8,128)(2,1)S(1)} %collective-permute-done.13.refs_0_, bf16[96,384]{1,0:T(8,128)(2,1)S(1)} %collective-permute-done.14.refs_1_, ...), custom_call_target="tpu_custom_call" | custom-call | tf_op jit(solution)/shard_map/closing/pallas_call | solution.py:339
  (28 shorter events, 3.9 us)
Async XLA Ops:
  0.6 11.9 %copy-start.2 = (f32[512]{0:T(512)S(1)}, f32[512]{0:T(512)}, u32[]{:S(2)}) copy-start(f32[512]{0:T(512)} %param.14) | copy-start | bytes 6148
  0.6 11.9 %slice-start = ((s32[512]{0:T(512)}), s32[8]{0:T(128)S(1)}, s32[]{:S(2)}) async-start(s32[512]{0:T(512)} %pick_hbm.1), calls=%async_computation | async-start | bytes 1024 | tf_op jit(solution)/shard_map/slice | solution.py:402
  0.7 12.3 %copy-start = (bf16[16,64,384]{2,1,0:T(8,128)(2,1)S(1)}, bf16[16,64,384]{2,1,0:T(8,128)(2,1)}, u32[]{:S(2)}) copy-start(bf16[16,64,384]{2,1,0:T(8,128)(2,1)} %vir_ref.1) | copy-start | bytes 2359300
  3.8 24.6 %copy-start.1 = (f32[384]{0:T(512)S(1)}, f32[384]{0:T(512)}, u32[]{:S(2)}) copy-start(f32[384]{0:T(512)} %param.15) | copy-start | bytes 4612
  3.8 8.4 %collective-permute-start = (bf16[272,256]{1,0:T(8,128)(2,1)S(1)}, bf16[272,256]{1,0:T(8,128)(2,1)S(1)}, u32[]{:S(2)}, u32[]{:S(2)}) collective-permute-start(bf16[272,256]{1,0:T(8,128)(2,1)S(1)} %get-tuple-element.37), channel_id=1, source_target_pairs={{0,2},{1,3},{2,0},{3,1},{4,6},{5,7},{6,4},{7,5},{8,10},{9,11},{10,... | collective-permute-start | bytes 417800 | tf_op jit(solution)/shard_map/ppermute | solution.py:24
  6.0 6.9 %collective-permute-start.1 = (bf16[272,256]{1,0:T(8,128)(2,1)S(1)}, bf16[272,256]{1,0:T(8,128)(2,1)S(1)}, u32[]{:S(2)}, u32[]{:S(2)}) collective-permute-start(bf16[272,256]{1,0:T(8,128)(2,1)S(1)} %get-tuple-element.38), channel_id=1, source_target_pairs={{0,3},{1,2},{2,1},{3,0},{4,7},{5,6},{6,5},{7,4},{8,11},{9,10},{10,... | collective-permute-start | bytes 417800 | tf_op jit(solution)/shard_map/ppermute | solution.py:24
  6.6 6.3 %collective-permute-start.2 = (bf16[272,256]{1,0:T(8,128)(2,1)S(1)}, bf16[272,256]{1,0:T(8,128)(2,1)S(1)}, u32[]{:S(2)}, u32[]{:S(2)}) collective-permute-start(bf16[272,256]{1,0:T(8,128)(2,1)S(1)} %get-tuple-element.39), channel_id=1, source_target_pairs={{0,1},{1,0},{2,3},{3,2},{4,5},{5,4},{6,7},{7,6},{8,9},{9,8},{10,11... | collective-permute-start | bytes 417800 | tf_op jit(solution)/shard_map/ppermute | solution.py:24
  10.3 5.2 %collective-permute-start.3 = (bf16[256,256]{1,0:T(8,128)(2,1)S(1)}, bf16[256,256]{1,0:T(8,128)(2,1)S(1)}, u32[]{:S(2)}, u32[]{:S(2)}) collective-permute-start(bf16[256,256]{1,0:T(8,128)(2,1)S(1)} %get-tuple-element.42), channel_id=1, source_target_pairs={{0,2},{1,3},{2,0},{3,1},{4,6},{5,7},{6,4},{7,5},{8,10},{9,11},{10,... | collective-permute-start | bytes 393224 | tf_op jit(solution)/shard_map/ppermute | solution.py:24
  11.7 6.8 %collective-permute-start.4 = (bf16[256,256]{1,0:T(8,128)(2,1)S(1)}, bf16[256,256]{1,0:T(8,128)(2,1)S(1)}, u32[]{:S(2)}, u32[]{:S(2)}) collective-permute-start(bf16[256,256]{1,0:T(8,128)(2,1)S(1)} %get-tuple-element.43), channel_id=1, source_target_pairs={{0,3},{1,2},{2,1},{3,0},{4,7},{5,6},{6,5},{7,4},{8,11},{9,10},{10,... | collective-permute-start | bytes 393224 | tf_op jit(solution)/shard_map/ppermute | solution.py:24
  12.2 6.3 %collective-permute-start.5 = (bf16[256,256]{1,0:T(8,128)(2,1)S(1)}, bf16[256,256]{1,0:T(8,128)(2,1)S(1)}, u32[]{:S(2)}, u32[]{:S(2)}) collective-permute-start(bf16[256,256]{1,0:T(8,128)(2,1)S(1)} %get-tuple-element.44), channel_id=1, source_target_pairs={{0,1},{1,0},{2,3},{3,2},{4,5},{5,4},{6,7},{7,6},{8,9},{9,8},{10,11... | collective-permute-start | bytes 393224 | tf_op jit(solution)/shard_map/ppermute | solution.py:24
  19.3 4.8 %collective-permute-start.6 = (bf16[1,96,384]{2,1,0:T(8,128)(2,1)S(1)}, bf16[1,96,384]{2,1,0:T(8,128)(2,1)S(1)}, u32[]{:S(2)}, u32[]{:S(2)}) collective-permute-start(bf16[1,96,384]{2,1,0:T(8,128)(2,1)S(1)} %get-tuple-element.46), channel_id=1, source_target_pairs={{0,12},{4,8},{8,4},{12,0},{16,28},{20,24},{24,20},{28,16},{1,13},{... | collective-permute-start | bytes 221192 | tf_op jit(solution)/shard_map/ppermute | solution.py:24
  21.8 3.9 %collective-permute-start.7 = (bf16[1,96,384]{2,1,0:T(8,128)(2,1)S(1)}, bf16[1,96,384]{2,1,0:T(8,128)(2,1)S(1)}, u32[]{:S(2)}, u32[]{:S(2)}) collective-permute-start(bf16[1,96,384]{2,1,0:T(8,128)(2,1)S(1)} %get-tuple-element.47), channel_id=1, source_target_pairs={{0,4},{4,0},{8,12},{12,8},{16,20},{20,16},{24,28},{28,24},{1,5},{5... | collective-permute-start | bytes 221192 | tf_op jit(solution)/shard_map/ppermute | solution.py:24
  22.1 3.7 %collective-permute-start.8 = (bf16[1,96,384]{2,1,0:T(8,128)(2,1)S(1)}, bf16[1,96,384]{2,1,0:T(8,128)(2,1)S(1)}, u32[]{:S(2)}, u32[]{:S(2)}) collective-permute-start(bf16[1,96,384]{2,1,0:T(8,128)(2,1)S(1)} %get-tuple-element.48), channel_id=1, source_target_pairs={{0,8},{4,12},{8,0},{12,4},{16,24},{20,28},{24,16},{28,20},{1,9},{5... | collective-permute-start | bytes 221192 | tf_op jit(solution)/shard_map/ppermute | solution.py:24
  25.8 4.4 %collective-permute-start.9 = (bf16[1,96,384]{2,1,0:T(8,128)(2,1)S(1)}, bf16[1,96,384]{2,1,0:T(8,128)(2,1)S(1)}, u32[]{:S(2)}, u32[]{:S(2)}) collective-permute-start(bf16[1,96,384]{2,1,0:T(8,128)(2,1)S(1)} %add_convert_fusion.1), channel_id=1, source_target_pairs={{0,16},{4,20},{8,24},{12,28},{16,0},{20,4},{24,8},{28,12},{1,17},{... | collective-permute-start | bytes 221192 | tf_op jit(solution)/shard_map/ppermute | solution.py:24
  30.2 4.2 %collective-permute-start.10 = (bf16[1,96,384]{2,1,0:T(8,128)(2,1)S(1)}, bf16[1,96,384]{2,1,0:T(8,128)(2,1)S(1)}, u32[]{:S(2)}, u32[]{:S(2)}) collective-permute-start(bf16[1,96,384]{2,1,0:T(8,128)(2,1)S(1)} %add_convert_fusion.refs_0_), channel_id=1, source_target_pairs={{0,12},{4,8},{8,4},{12,0},{16,28},{20,24},{24,20},{28,16},{1,13},{... | collective-permute-start | bytes 221192 | tf_op jit(solution)/shard_map/ppermute | solution.py:24
  31.3 3.8 %collective-permute-start.11 = (bf16[1,96,384]{2,1,0:T(8,128)(2,1)S(1)}, bf16[1,96,384]{2,1,0:T(8,128)(2,1)S(1)}, u32[]{:S(2)}, u32[]{:S(2)}) collective-permute-start(bf16[1,96,384]{2,1,0:T(8,128)(2,1)S(1)} %add_convert_fusion.refs_0_), channel_id=1, source_target_pairs={{0,4},{4,0},{8,12},{12,8},{16,20},{20,16},{24,28},{28,24},{1,5},{5... | collective-permute-start | bytes 221192 | tf_op jit(solution)/shard_map/ppermute | solution.py:24
  33.1 3.2 %collective-permute-start.12 = (bf16[1,96,384]{2,1,0:T(8,128)(2,1)S(1)}, bf16[1,96,384]{2,1,0:T(8,128)(2,1)S(1)}, u32[]{:S(2)}, u32[]{:S(2)}) collective-permute-start(bf16[1,96,384]{2,1,0:T(8,128)(2,1)S(1)} %add_convert_fusion.refs_0_), channel_id=1, source_target_pairs={{0,8},{4,12},{8,0},{12,4},{16,24},{20,28},{24,16},{28,20},{1,9},{5... | collective-permute-start | bytes 221192 | tf_op jit(solution)/shard_map/ppermute | solution.py:24
  37.1 5.2 %collective-permute-start.13 = (bf16[96,384]{1,0:T(8,128)(2,1)S(1)}, bf16[96,384]{1,0:T(8,128)(2,1)S(1)}, u32[]{:S(2)}, u32[]{:S(2)}) collective-permute-start(bf16[96,384]{1,0:T(8,128)(2,1)S(1)} %get-tuple-element.51), channel_id=1, source_target_pairs={{0,2},{1,3},{2,0},{3,1},{4,6},{5,7},{6,4},{7,5},{8,10},{9,11},{10,... | collective-permute-start | bytes 221192 | tf_op jit(solution)/shard_map/ppermute | solution.py:24
  38.4 4.7 %collective-permute-start.14 = (bf16[96,384]{1,0:T(8,128)(2,1)S(1)}, bf16[96,384]{1,0:T(8,128)(2,1)S(1)}, u32[]{:S(2)}, u32[]{:S(2)}) collective-permute-start(bf16[96,384]{1,0:T(8,128)(2,1)S(1)} %get-tuple-element.52), channel_id=1, source_target_pairs={{0,1},{1,0},{2,3},{3,2},{4,5},{5,4},{6,7},{7,6},{8,9},{9,8},{10,11... | collective-permute-start | bytes 221192 | tf_op jit(solution)/shard_map/ppermute | solution.py:24
  42.2 3.9 %collective-permute-start.15 = (bf16[96,384]{1,0:T(8,128)(2,1)S(1)}, bf16[96,384]{1,0:T(8,128)(2,1)S(1)}, u32[]{:S(2)}, u32[]{:S(2)}) collective-permute-start(bf16[96,384]{1,0:T(8,128)(2,1)S(1)} %get-tuple-element.53), channel_id=1, source_target_pairs={{0,3},{1,2},{2,1},{3,0},{4,7},{5,6},{6,5},{7,4},{8,11},{9,10},{10,... | collective-permute-start | bytes 221192 | tf_op jit(solution)/shard_map/ppermute | solution.py:24

commit v6 on v5

--- a/solution.py
+++ b/solution.py
@@ -165,17 +165,19 @@
     aux_rows = parts[0].shape[1]
     width, virtual = vir_coef.shape[1], vir_coef.shape[2]
     span = counts[0] * width
+    rest_rows = (sum(counts) - 1) * width
 
     def kernel(vir_ref, *refs):
-        held, (fitted_ref, rest_ref, own_ref) = refs[: len(parts)], refs[len(parts) :]
+        held, (fitted_ref, rest_ref, last_ref, own_ref) = refs[: len(parts)], refs[len(parts) :]
         first, rest = [], []
         for part in held:
             tail = part[pl.ds(2 * pairs * span, TILE), :][:, :128].astype(jnp.float32)
             found = [vir_ref[tail[slot, 0].astype(jnp.int32)] for slot in range(sum(counts))]
             first.append(found[0])
-            rest += found[1:]
+            rest.append(jnp.concatenate(found[1:], axis=0))
         own_ref[...] = jnp.concatenate(first, axis=0).T
-        rest_ref[...] = jnp.concatenate(rest, axis=0).T
+        rest_ref[...] = jnp.concatenate(rest[:-1], axis=0).T
+        last_ref[...] = rest[-1].T
         for orbital in range(2 * pairs):
             blocks = jnp.concatenate([part[pl.ds(orbital * span, width), :] for part in held], axis=0)
             fitted_ref[orbital] = jnp.dot(own_ref[...], blocks, preferred_element_type=jnp.float32)
@@ -183,10 +185,11 @@
     return pl.pallas_call(
         kernel,
         in_specs=whole(1 + len(parts)),
-        out_specs=whole(2),
+        out_specs=whole(3),
         out_shape=[
             jax.ShapeDtypeStruct((2 * pairs, virtual, aux_rows), jnp.float32),
-            jax.ShapeDtypeStruct((virtual, len(parts) * (sum(counts) - 1) * width), jnp.bfloat16),
+            jax.ShapeDtypeStruct((virtual, (len(parts) - 1) * rest_rows), jnp.bfloat16),
+            jax.ShapeDtypeStruct((virtual, rest_rows), jnp.bfloat16),
         ],
         scratch_shapes=[VMEM((virtual, len(parts) * width), jnp.bfloat16)],
         compiler_params=PARAMS,
@@ -194,31 +197,57 @@
     )(vir_coef, *parts)
 
 
-def coulomb_parts(fitted, rest, first, later, pairs, counts, quad):
-    n_pair = len(first)
-    slots = sum(counts)
-    virtual, aux_rows = fitted.shape[1:]
-    width = rest.shape[1] // (n_pair * (slots - 1))
+def live_slots(later, counts, width):
+    mark = later[pl.ds((counts[1] - 1) * width, TILE), :][:, :128].astype(jnp.float32)[0, 0]
+    return jnp.where(mark < MARK, sum(counts), (mark * (1.0 / MARK)).astype(jnp.int32) - 1)
+
+
+def live_blocks(first, later, live, orbital, counts, width):
+    blocks = []
+    for slot in range(1, sum(counts)):
+        chunk = int(slot >= counts[0])
+        at = (orbital * counts[chunk] + slot - chunk * counts[0]) * width
+        block = (first, later)[chunk][pl.ds(at, width), :]
+        blocks.append(jnp.where(slot < live, block, jnp.zeros_like(block)))
+    return blocks
+
+
+def fitted_more(fitted, rest, first, later, counts, width):
+    count = len(first)
+
+    def kernel(fitted_ref, rest_ref, *refs):
+        held, out_ref = list(zip(refs[:count], refs[count : 2 * count])), refs[-1]
+        live = [live_slots(part[1], counts, width) for part in held]
+        for orbital in range(fitted.shape[0]):
+            blocks = []
+            for part, alive in zip(held, live):
+                blocks += live_blocks(*part, alive, orbital, counts, width)
+            total = jnp.dot(rest_ref[...], jnp.concatenate(blocks, axis=0), preferred_element_type=jnp.float32)
+            out_ref[orbital] = fitted_ref[orbital] + total
+
+    return pl.pallas_call(
+        kernel,
+        in_specs=whole(2 + 2 * count),
+        out_specs=pl.BlockSpec(memory_space=VMEM),
+        out_shape=jax.ShapeDtypeStruct(fitted.shape, fitted.dtype),
+        compiler_params=PARAMS,
+        name="fitted_more",
+    )(fitted, rest, *first, *later)
+
+
+def coulomb_parts(fitted, last, first, later, pairs, counts, width, quad):
+    virtual = fitted.shape[1]
     share = virtual // quad
 
-    def kernel(fitted_ref, rest_ref, *refs):
-        held, outs, block_ref = (refs[:n_pair], refs[n_pair : 2 * n_pair]), refs[2 * n_pair : -1], refs[-1]
+    def kernel(fitted_ref, last_ref, first_ref, later_ref, *refs):
+        outs, block_ref = refs[:-1], refs[-1]
         place = lax.axis_index("aux") % quad
-        live = []
-        for part in held[1]:
-            mark = part[pl.ds((counts[1] - 1) * width, TILE), :][:, :128].astype(jnp.float32)[0, 0]
-            live.append(jnp.where(mark < MARK, slots, (mark * (1.0 / MARK)).astype(jnp.int32) - 1))
+        live = live_slots(later_ref, counts, width)
         for pair in range(pairs):
             sides = []
             for orbital in (2 * pair, 2 * pair + 1):
-                blocks = []
-                for group in range(n_pair):
-                    for slot in range(1, slots):
-                        chunk = int(slot >= counts[0])
-                        at = (orbital * counts[chunk] + slot - chunk * counts[0]) * width
-                        block = held[chunk][group][pl.ds(at, width), :]
-                        blocks.append(jnp.where(slot < live[group], block, jnp.zeros_like(block)))
-                total = jnp.dot(rest_ref[...], jnp.concatenate(blocks, axis=0), preferred_element_type=jnp.float32)
+                blocks = jnp.concatenate(live_blocks(first_ref, later_ref, live, orbital, counts, width), axis=0)
+                total = jnp.dot(last_ref[...], blocks, preferred_element_type=jnp.float32)
                 sides.append((fitted_ref[orbital] + total).astype(jnp.bfloat16))
             block = lax.dot_general(*sides, (((1,), (1,)), ((), ())), preferred_element_type=jnp.float32)
             block_ref[...] = block.astype(jnp.bfloat16)
@@ -228,13 +257,13 @@
 
     return pl.pallas_call(
         kernel,
-        in_specs=whole(2 + 2 * n_pair),
+        in_specs=whole(4),
         out_specs=whole(quad),
         out_shape=[jax.ShapeDtypeStruct((pairs, share, virtual), jnp.bfloat16)] * quad,
         scratch_shapes=[VMEM((virtual, virtual), jnp.bfloat16)],
         compiler_params=PARAMS,
         name="coulomb_parts",
-    )(fitted, rest, *first, *later)
+    )(fitted, last, first, later)
 
 
 def density_parts(inverse, chunks, n_pair):
@@ -393,8 +422,11 @@
     later = list(half_rest(ints, block_count, chosen, tables, n_pair, pairs))
     got = [made[:1] + exchanged(made, "pair", PAIR_ORDER) for made in (first, later)]
 
-    fitted, rest = fitted_first(vir_coef, got[0], pairs, counts)
-    parts = coulomb_parts(fitted, rest, got[0], got[1], pairs, counts, 4)
+    slowest = 1 + PAIR_ORDER.index(max(PAIR_ORDER))
+    ends = [group.pop(slowest) for group in got]
+    fitted, rest, last = fitted_first(vir_coef, got[0] + ends[:1], pairs, counts)
+    fitted = fitted_more(fitted, rest, *got, counts, width)
+    parts = coulomb_parts(fitted, last, *ends, pairs, counts, width, 4)
 
     occ_pick, occ_energy, vir_energy, _ = lax.optimization_barrier((occ_pick, occ_energy, vir_energy, later[0]))
     own_pairs = lax.axis_index("pair") * pairs + jnp.arange(pairs, dtype=jnp.int32)

time: 47 us -> 46.8 us (level)
  waiting for transfers between devices: 16.2 us -> 15 us
  starting transfers between devices: 19.1 us -> 19.7 us
    ppermute x16, waiting for transfers between devices: 16.2 us -> 15 us  [swapped(): lax.ppermute(value, axis, [(source, source ^ mask) for source in range(co...]
    ppermute x16, starting transfers between devices: 19.1 us -> 19.7 us  [swapped(): lax.ppermute(value, axis, [(source, source ^ mask) for source in range(co...]
    pallas_call x2 -> x3, Pallas kernels: 1.11 us -> 1.44 us  [the longest x1 0.55 us: coulomb_parts(): pl.pallas_call(kernel, in_specs=whole(4), out_specs=whole(quad), out_shap...]
  transfers between devices with their start and end apart: 16 -> 16, of which waited for: 11 -> 10; matrix products, arithmetic and copies ran while one was open for 3% -> 3% of each run, Pallas kernels for 7% -> 8%
where the time goes in v6:
time: 46.8 us; the launch traced here: 46.7 us
  starting transfers between devices  19.7 us (42%)
  waiting for transfers between devices  15 us (32%)
  Pallas kernels  8.9 us (19%)
  other arithmetic  1.64 us (4%)
  between operations  1.42 us (3%)
    ppermute x16, starting transfers between devices, swapped(): lax.ppermute(value, axis, [(source, source ^ mask) for source in range(co...  19.7 us
    ppermute x16, waiting for transfers between devices, swapped(): lax.ppermute(value, axis, [(source, source ^ mask) for source in range(co...  15 us
    pallas_call x1, Pallas kernels, half_first(): pl.pallas_call(kernel, in_specs=[pl.BlockSpec(memory_space=pltpu.HBM)] *...  3.16 us
    pallas_call x1, Pallas kernels, half_rest(): pl.pallas_call(kernel, in_specs=[pl.BlockSpec(memory_space=SMEM)] + whole...  2.73 us
  transfers between devices with their start and end apart: 16, of which 10 were waited for; matrix products, arithmetic and copies ran while one was open for 3% of the time, Pallas kernels for 8%

profile of v6, /device:TPU:1, one launch (start us, length us, event | category | flops | bytes accessed | tf_op | source)
XLA Modules:
  0.0 46.7 jit_solution(4067934038554803897)
XLA Ops:
  0.7 3.2 %half_first.1 = (bf16[272,256]{1,0:T(8,128)(2,1)S(1)}, bf16[272,256]{1,0:T(8,128)(2,1)S(1)}, bf16[272,256]{1,0:T(8,128)(2,1)S(1)}, bf16[272,256]{1,0:T(8,128)(2,...) custom-call(s32[2,4]{1,0:T(2,128)} %bitcast.6, s32[512]{0:T(512)} %pick_hbm.1, ...), custom_call_target="tpu_custom_call" | custom-call | tf_op jit(solution)/shard_map/half_first/pallas_call | solution.py:77
  3.8 2.1 %collective-permute-start = (bf16[272,256]{1,0:T(8,128)(2,1)S(1)}, bf16[272,256]{1,0:T(8,128)(2,1)S(1)}, u32[]{:S(2)}, u32[]{:S(2)}) collective-permute-start(bf16[272,256]{1,0:T(8,128)(2,1)S(1)} %get-tuple-element.38), channel_id=1, source_target_pairs={{0,2},{1,3},{2,0},{3,1},{4,6},{5,7},{6,4},{7,5},{8,10},{9,11},{10,... | collective-permute-start | bytes 417800 | tf_op jit(solution)/shard_map/ppermute | solution.py:24
  6.0 1.0 %collective-permute-start.1 = (bf16[272,256]{1,0:T(8,128)(2,1)S(1)}, bf16[272,256]{1,0:T(8,128)(2,1)S(1)}, u32[]{:S(2)}, u32[]{:S(2)}) collective-permute-start(bf16[272,256]{1,0:T(8,128)(2,1)S(1)} %get-tuple-element.39), channel_id=1, source_target_pairs={{0,1},{1,0},{2,3},{3,2},{4,5},{5,4},{6,7},{7,6},{8,9},{9,8},{10,11... | collective-permute-start | bytes 417800 | tf_op jit(solution)/shard_map/ppermute | solution.py:24
  7.6 2.7 %half_rest.1 = (bf16[256,256]{1,0:T(8,128)(2,1)S(1)}, bf16[256,256]{1,0:T(8,128)(2,1)S(1)}, bf16[256,256]{1,0:T(8,128)(2,1)S(1)}, bf16[256,256]{1,0:T(8,128)(2,1)S(1)}) custom-call(s32[1]{0:T(128)S(6)} %copy.10.count_ref, bf16[64,512]{1,0:T(8,128)(2,1)S(1)} %get-tuple-element.32.chosen_ref, bf16[2,64,512]{2,1,0:T(8,128)(2,1)S(1)} %get-tuple-element.33.tables_ref, ...), custom_call_target="tpu_custom_call" | custom-call | tf_op jit(solution)/shard_map/half_rest/pallas_call | solution.py:150
  10.3 1.4 %collective-permute-start.3 = (bf16[256,256]{1,0:T(8,128)(2,1)S(1)}, bf16[256,256]{1,0:T(8,128)(2,1)S(1)}, u32[]{:S(2)}, u32[]{:S(2)}) collective-permute-start(bf16[256,256]{1,0:T(8,128)(2,1)S(1)} %get-tuple-element.43), channel_id=1, source_target_pairs={{0,2},{1,3},{2,0},{3,1},{4,6},{5,7},{6,4},{7,5},{8,10},{9,11},{10,... | collective-permute-start | bytes 393224 | tf_op jit(solution)/shard_map/ppermute | solution.py:24
  11.7 0.8 %collective-permute-start.4 = (bf16[256,256]{1,0:T(8,128)(2,1)S(1)}, bf16[256,256]{1,0:T(8,128)(2,1)S(1)}, u32[]{:S(2)}, u32[]{:S(2)}) collective-permute-start(bf16[256,256]{1,0:T(8,128)(2,1)S(1)} %get-tuple-element.44), channel_id=1, source_target_pairs={{0,1},{1,0},{2,3},{3,2},{4,5},{5,4},{6,7},{7,6},{8,9},{9,8},{10,11... | collective-permute-start | bytes 393224 | tf_op jit(solution)/shard_map/ppermute | solution.py:24
  13.7 1.8 %collective-permute-done.3.refs_4_ = bf16[256,256]{1,0:T(8,128)(2,1)S(1)} collective-permute-done((bf16[256,256]{1,0:T(8,128)(2,1)S(1)}, bf16[256,256]{1,0:T(8,128)(2,1)S(1)}, u32[]{:S(2)}, u32[]{:S(2)}) %collective-permute-start.3) | collective-permute-done | bytes 131104 | tf_op jit(solution)/shard_map/ppermute | solution.py:24
  16.0 2.5 %collective-permute-done.5.later_ref = bf16[256,256]{1,0:T(8,128)(2,1)S(1)} collective-permute-done((bf16[256,256]{1,0:T(8,128)(2,1)S(1)}, bf16[256,256]{1,0:T(8,128)(2,1)S(1)}, u32[]{:S(2)}, u32[]{:S(2)}) %collective-permute-start.5) | collective-permute-done | bytes 131104 | tf_op jit(solution)/shard_map/ppermute | solution.py:24
  19.1 2.5 %collective-permute-start.6 = (bf16[1,96,384]{2,1,0:T(8,128)(2,1)S(1)}, bf16[1,96,384]{2,1,0:T(8,128)(2,1)S(1)}, u32[]{:S(2)}, u32[]{:S(2)}) collective-permute-start(bf16[1,96,384]{2,1,0:T(8,128)(2,1)S(1)} %get-tuple-element.48), channel_id=1, source_target_pairs={{0,12},{4,8},{8,4},{12,0},{16,28},{20,24},{24,20},{28,16},{1,13},{... | collective-permute-start | bytes 221192 | tf_op jit(solution)/shard_map/ppermute | solution.py:24
  22.5 1.4 %collective-permute-done.6 = bf16[1,96,384]{2,1,0:T(8,128)(2,1)S(1)} collective-permute-done((bf16[1,96,384]{2,1,0:T(8,128)(2,1)S(1)}, bf16[1,96,384]{2,1,0:T(8,128)(2,1)S(1)}, u32[]{:S(2)}, u32[]{:S(2)}) %collective-permute-start.6) | collective-permute-done | bytes 73760 | tf_op jit(solution)/shard_map/ppermute | solution.py:24
  23.9 1.6 %collective-permute-done.7 = bf16[1,96,384]{2,1,0:T(8,128)(2,1)S(1)} collective-permute-done((bf16[1,96,384]{2,1,0:T(8,128)(2,1)S(1)}, bf16[1,96,384]{2,1,0:T(8,128)(2,1)S(1)}, u32[]{:S(2)}, u32[]{:S(2)}) %collective-permute-start.7) | collective-permute-done | bytes 73760 | tf_op jit(solution)/shard_map/ppermute | solution.py:24
  25.5 2.6 %collective-permute-start.9 = (bf16[1,96,384]{2,1,0:T(8,128)(2,1)S(1)}, bf16[1,96,384]{2,1,0:T(8,128)(2,1)S(1)}, u32[]{:S(2)}, u32[]{:S(2)}) collective-permute-start(bf16[1,96,384]{2,1,0:T(8,128)(2,1)S(1)} %add_convert_fusion.1), channel_id=1, source_target_pairs={{0,16},{4,20},{8,24},{12,28},{16,0},{20,4},{24,8},{28,12},{1,17},{... | collective-permute-start | bytes 221192 | tf_op jit(solution)/shard_map/ppermute | solution.py:24
  28.8 1.1 %collective-permute-done.9 = bf16[1,96,384]{2,1,0:T(8,128)(2,1)S(1)} collective-permute-done((bf16[1,96,384]{2,1,0:T(8,128)(2,1)S(1)}, bf16[1,96,384]{2,1,0:T(8,128)(2,1)S(1)}, u32[]{:S(2)}, u32[]{:S(2)}) %collective-permute-start.9) | collective-permute-done | bytes 73760 | tf_op jit(solution)/shard_map/ppermute | solution.py:24
  30.0 1.1 %collective-permute-start.10 = (bf16[1,96,384]{2,1,0:T(8,128)(2,1)S(1)}, bf16[1,96,384]{2,1,0:T(8,128)(2,1)S(1)}, u32[]{:S(2)}, u32[]{:S(2)}) collective-permute-start(bf16[1,96,384]{2,1,0:T(8,128)(2,1)S(1)} %add_convert_fusion.refs_0_), channel_id=1, source_target_pairs={{0,12},{4,8},{8,4},{12,0},{16,28},{20,24},{24,20},{28,16},{1,13},{... | collective-permute-start | bytes 221192 | tf_op jit(solution)/shard_map/ppermute | solution.py:24
  31.1 1.8 %collective-permute-start.11 = (bf16[1,96,384]{2,1,0:T(8,128)(2,1)S(1)}, bf16[1,96,384]{2,1,0:T(8,128)(2,1)S(1)}, u32[]{:S(2)}, u32[]{:S(2)}) collective-permute-start(bf16[1,96,384]{2,1,0:T(8,128)(2,1)S(1)} %add_convert_fusion.refs_0_), channel_id=1, source_target_pairs={{0,4},{4,0},{8,12},{12,8},{16,20},{20,16},{24,28},{28,24},{1,5},{5... | collective-permute-start | bytes 221192 | tf_op jit(solution)/shard_map/ppermute | solution.py:24
  33.2 0.9 %collective-permute-done.10.refs_1_ = bf16[1,96,384]{2,1,0:T(8,128)(2,1)S(1)} collective-permute-done((bf16[1,96,384]{2,1,0:T(8,128)(2,1)S(1)}, bf16[1,96,384]{2,1,0:T(8,128)(2,1)S(1)}, u32[]{:S(2)}, u32[]{:S(2)}) %collective-permute-start.10) | collective-permute-done | bytes 73760 | tf_op jit(solution)/shard_map/ppermute | solution.py:24
  34.1 0.8 %collective-permute-done.11.refs_2_ = bf16[1,96,384]{2,1,0:T(8,128)(2,1)S(1)} collective-permute-done((bf16[1,96,384]{2,1,0:T(8,128)(2,1)S(1)}, bf16[1,96,384]{2,1,0:T(8,128)(2,1)S(1)}, u32[]{:S(2)}, u32[]{:S(2)}) %collective-permute-start.11) | collective-permute-done | bytes 73760 | tf_op jit(solution)/shard_map/ppermute | solution.py:24
  34.9 1.2 %collective-permute-done.12.refs_3_ = bf16[1,96,384]{2,1,0:T(8,128)(2,1)S(1)} collective-permute-done((bf16[1,96,384]{2,1,0:T(8,128)(2,1)S(1)}, bf16[1,96,384]{2,1,0:T(8,128)(2,1)S(1)}, u32[]{:S(2)}, u32[]{:S(2)}) %collective-permute-start.12) | collective-permute-done | bytes 73760 | tf_op jit(solution)/shard_map/ppermute | solution.py:24
  36.1 0.8 %density_parts.1 = (f32[96,384]{1,0:T(8,128)S(1)}, bf16[96,384]{1,0:T(8,128)(2,1)S(1)}, bf16[96,384]{1,0:T(8,128)(2,1)S(1)}, bf16[96,384]{1,0:T(8,128)(2,1)S(1)}, f32[1,384]{1,0:T(1,128)S(1)}) custom-call(f32[1,384,384]{2,1,0:T(8,128)S(1)} %subtract_divide_fusion.inverse_ref, bf16[1,96,384]{2,1,0:T(8,128)(2,1)S(1)} %add_convert_fusion.refs_0_, ...), custom_call_target="tpu_custom_call" | custom-call | tf_op jit(solution)/shard_map/density_parts/pallas_call | solution.py:318
  36.9 1.3 %collective-permute-start.13 = (bf16[96,384]{1,0:T(8,128)(2,1)S(1)}, bf16[96,384]{1,0:T(8,128)(2,1)S(1)}, u32[]{:S(2)}, u32[]{:S(2)}) collective-permute-start(bf16[96,384]{1,0:T(8,128)(2,1)S(1)} %get-tuple-element.53), channel_id=1, source_target_pairs={{0,2},{1,3},{2,0},{3,1},{4,6},{5,7},{6,4},{7,5},{8,10},{9,11},{10,... | collective-permute-start | bytes 221192 | tf_op jit(solution)/shard_map/ppermute | solution.py:24
  38.2 3.8 %collective-permute-start.14 = (bf16[96,384]{1,0:T(8,128)(2,1)S(1)}, bf16[96,384]{1,0:T(8,128)(2,1)S(1)}, u32[]{:S(2)}, u32[]{:S(2)}) collective-permute-start(bf16[96,384]{1,0:T(8,128)(2,1)S(1)} %get-tuple-element.54), channel_id=1, source_target_pairs={{0,1},{1,0},{2,3},{3,2},{4,5},{5,4},{6,7},{7,6},{8,9},{9,8},{10,11... | collective-permute-start | bytes 221192 | tf_op jit(solution)/shard_map/ppermute | solution.py:24
  42.1 0.8 %collective-permute-done.14.refs_1_ = bf16[96,384]{1,0:T(8,128)(2,1)S(1)} collective-permute-done((bf16[96,384]{1,0:T(8,128)(2,1)S(1)}, bf16[96,384]{1,0:T(8,128)(2,1)S(1)}, u32[]{:S(2)}, u32[]{:S(2)}) %collective-permute-start.14) | collective-permute-done | bytes 73760 | tf_op jit(solution)/shard_map/ppermute | solution.py:24
  42.9 3.0 %collective-permute-done.15.refs_2_ = bf16[96,384]{1,0:T(8,128)(2,1)S(1)} collective-permute-done((bf16[96,384]{1,0:T(8,128)(2,1)S(1)}, bf16[96,384]{1,0:T(8,128)(2,1)S(1)}, u32[]{:S(2)}, u32[]{:S(2)}) %collective-permute-start.15) | collective-permute-done | bytes 73760 | tf_op jit(solution)/shard_map/ppermute | solution.py:24
  45.9 0.8 %closing.1 = (f32[96,384]{1,0:T(8,128)}, f32[1]{0:T(128)}) custom-call(f32[96,384]{1,0:T(8,128)S(1)} %get-tuple-element.51.own_ref, f32[1,384]{1,0:T(1,128)S(1)} %get-tuple-element.52.energy_ref, bf16[96,384]{1,0:T(8,128)(2,1)S(1)} %collective-permute-done.13.refs_0_, bf16[96,384]{1,0:T(8,128)(2,1)S(1)} %collective-permute-done.14.refs_1_, ...), custom_call_target="tpu_custom_call" | custom-call | tf_op jit(solution)/shard_map/closing/pallas_call | solution.py:368
  (29 shorter events, 4.3 us)
Async XLA Ops:
  0.6 12.5 %copy-start.2 = (f32[512]{0:T(512)S(1)}, f32[512]{0:T(512)}, u32[]{:S(2)}) copy-start(f32[512]{0:T(512)} %param.14) | copy-start | bytes 6148
  0.6 12.5 %slice-start = ((s32[512]{0:T(512)}), s32[8]{0:T(128)S(1)}, s32[]{:S(2)}) async-start(s32[512]{0:T(512)} %pick_hbm.1), calls=%async_computation | async-start | bytes 1024 | tf_op jit(solution)/shard_map/slice | solution.py:434
  0.7 12.7 %copy-start = (bf16[16,64,384]{2,1,0:T(8,128)(2,1)S(1)}, bf16[16,64,384]{2,1,0:T(8,128)(2,1)}, u32[]{:S(2)}) copy-start(bf16[16,64,384]{2,1,0:T(8,128)(2,1)} %vir_ref.1) | copy-start | bytes 2359300
  3.8 24.4 %copy-start.1 = (f32[384]{0:T(512)S(1)}, f32[384]{0:T(512)}, u32[]{:S(2)}) copy-start(f32[384]{0:T(512)} %param.15) | copy-start | bytes 4612
  3.8 8.7 %collective-permute-start = (bf16[272,256]{1,0:T(8,128)(2,1)S(1)}, bf16[272,256]{1,0:T(8,128)(2,1)S(1)}, u32[]{:S(2)}, u32[]{:S(2)}) collective-permute-start(bf16[272,256]{1,0:T(8,128)(2,1)S(1)} %get-tuple-element.38), channel_id=1, source_target_pairs={{0,2},{1,3},{2,0},{3,1},{4,6},{5,7},{6,4},{7,5},{8,10},{9,11},{10,... | collective-permute-start | bytes 417800 | tf_op jit(solution)/shard_map/ppermute | solution.py:24
  6.0 7.3 %collective-permute-start.1 = (bf16[272,256]{1,0:T(8,128)(2,1)S(1)}, bf16[272,256]{1,0:T(8,128)(2,1)S(1)}, u32[]{:S(2)}, u32[]{:S(2)}) collective-permute-start(bf16[272,256]{1,0:T(8,128)(2,1)S(1)} %get-tuple-element.39), channel_id=1, source_target_pairs={{0,1},{1,0},{2,3},{3,2},{4,5},{5,4},{6,7},{7,6},{8,9},{9,8},{10,11... | collective-permute-start | bytes 417800 | tf_op jit(solution)/shard_map/ppermute | solution.py:24
  6.9 6.4 %collective-permute-start.2 = (bf16[272,256]{1,0:T(8,128)(2,1)S(1)}, bf16[272,256]{1,0:T(8,128)(2,1)S(1)}, u32[]{:S(2)}, u32[]{:S(2)}) collective-permute-start(bf16[272,256]{1,0:T(8,128)(2,1)S(1)} %get-tuple-element.40), channel_id=1, source_target_pairs={{0,3},{1,2},{2,1},{3,0},{4,7},{5,6},{6,5},{7,4},{8,11},{9,10},{10,... | collective-permute-start | bytes 417800 | tf_op jit(solution)/shard_map/ppermute | solution.py:24
  10.3 5.2 %collective-permute-start.3 = (bf16[256,256]{1,0:T(8,128)(2,1)S(1)}, bf16[256,256]{1,0:T(8,128)(2,1)S(1)}, u32[]{:S(2)}, u32[]{:S(2)}) collective-permute-start(bf16[256,256]{1,0:T(8,128)(2,1)S(1)} %get-tuple-element.43), channel_id=1, source_target_pairs={{0,2},{1,3},{2,0},{3,1},{4,6},{5,7},{6,4},{7,5},{8,10},{9,11},{10,... | collective-permute-start | bytes 393224 | tf_op jit(solution)/shard_map/ppermute | solution.py:24
  11.7 3.7 %collective-permute-start.4 = (bf16[256,256]{1,0:T(8,128)(2,1)S(1)}, bf16[256,256]{1,0:T(8,128)(2,1)S(1)}, u32[]{:S(2)}, u32[]{:S(2)}) collective-permute-start(bf16[256,256]{1,0:T(8,128)(2,1)S(1)} %get-tuple-element.44), channel_id=1, source_target_pairs={{0,1},{1,0},{2,3},{3,2},{4,5},{5,4},{6,7},{7,6},{8,9},{9,8},{10,11... | collective-permute-start | bytes 393224 | tf_op jit(solution)/shard_map/ppermute | solution.py:24
  12.5 6.0 %collective-permute-start.5 = (bf16[256,256]{1,0:T(8,128)(2,1)S(1)}, bf16[256,256]{1,0:T(8,128)(2,1)S(1)}, u32[]{:S(2)}, u32[]{:S(2)}) collective-permute-start(bf16[256,256]{1,0:T(8,128)(2,1)S(1)} %get-tuple-element.46), channel_id=1, source_target_pairs={{0,3},{1,2},{2,1},{3,0},{4,7},{5,6},{6,5},{7,4},{8,11},{9,10},{10,... | collective-permute-start | bytes 393224 | tf_op jit(solution)/shard_map/ppermute | solution.py:24
  19.1 4.9 %collective-permute-start.6 = (bf16[1,96,384]{2,1,0:T(8,128)(2,1)S(1)}, bf16[1,96,384]{2,1,0:T(8,128)(2,1)S(1)}, u32[]{:S(2)}, u32[]{:S(2)}) collective-permute-start(bf16[1,96,384]{2,1,0:T(8,128)(2,1)S(1)} %get-tuple-element.48), channel_id=1, source_target_pairs={{0,12},{4,8},{8,4},{12,0},{16,28},{20,24},{24,20},{28,16},{1,13},{... | collective-permute-start | bytes 221192 | tf_op jit(solution)/shard_map/ppermute | solution.py:24
  21.6 3.9 %collective-permute-start.7 = (bf16[1,96,384]{2,1,0:T(8,128)(2,1)S(1)}, bf16[1,96,384]{2,1,0:T(8,128)(2,1)S(1)}, u32[]{:S(2)}, u32[]{:S(2)}) collective-permute-start(bf16[1,96,384]{2,1,0:T(8,128)(2,1)S(1)} %get-tuple-element.49), channel_id=1, source_target_pairs={{0,4},{4,0},{8,12},{12,8},{16,20},{20,16},{24,28},{28,24},{1,5},{5... | collective-permute-start | bytes 221192 | tf_op jit(solution)/shard_map/ppermute | solution.py:24
  21.8 3.6 %collective-permute-start.8 = (bf16[1,96,384]{2,1,0:T(8,128)(2,1)S(1)}, bf16[1,96,384]{2,1,0:T(8,128)(2,1)S(1)}, u32[]{:S(2)}, u32[]{:S(2)}) collective-permute-start(bf16[1,96,384]{2,1,0:T(8,128)(2,1)S(1)} %get-tuple-element.50), channel_id=1, source_target_pairs={{0,8},{4,12},{8,0},{12,4},{16,24},{20,28},{24,16},{28,20},{1,9},{5... | collective-permute-start | bytes 221192 | tf_op jit(solution)/shard_map/ppermute | solution.py:24
  25.5 4.4 %collective-permute-start.9 = (bf16[1,96,384]{2,1,0:T(8,128)(2,1)S(1)}, bf16[1,96,384]{2,1,0:T(8,128)(2,1)S(1)}, u32[]{:S(2)}, u32[]{:S(2)}) collective-permute-start(bf16[1,96,384]{2,1,0:T(8,128)(2,1)S(1)} %add_convert_fusion.1), channel_id=1, source_target_pairs={{0,16},{4,20},{8,24},{12,28},{16,0},{20,4},{24,8},{28,12},{1,17},{... | collective-permute-start | bytes 221192 | tf_op jit(solution)/shard_map/ppermute | solution.py:24
  30.0 4.2 %collective-permute-start.10 = (bf16[1,96,384]{2,1,0:T(8,128)(2,1)S(1)}, bf16[1,96,384]{2,1,0:T(8,128)(2,1)S(1)}, u32[]{:S(2)}, u32[]{:S(2)}) collective-permute-start(bf16[1,96,384]{2,1,0:T(8,128)(2,1)S(1)} %add_convert_fusion.refs_0_), channel_id=1, source_target_pairs={{0,12},{4,8},{8,4},{12,0},{16,28},{20,24},{24,20},{28,16},{1,13},{... | collective-permute-start | bytes 221192 | tf_op jit(solution)/shard_map/ppermute | solution.py:24
  31.1 3.8 %collective-permute-start.11 = (bf16[1,96,384]{2,1,0:T(8,128)(2,1)S(1)}, bf16[1,96,384]{2,1,0:T(8,128)(2,1)S(1)}, u32[]{:S(2)}, u32[]{:S(2)}) collective-permute-start(bf16[1,96,384]{2,1,0:T(8,128)(2,1)S(1)} %add_convert_fusion.refs_0_), channel_id=1, source_target_pairs={{0,4},{4,0},{8,12},{12,8},{16,20},{20,16},{24,28},{28,24},{1,5},{5... | collective-permute-start | bytes 221192 | tf_op jit(solution)/shard_map/ppermute | solution.py:24
  32.9 3.2 %collective-permute-start.12 = (bf16[1,96,384]{2,1,0:T(8,128)(2,1)S(1)}, bf16[1,96,384]{2,1,0:T(8,128)(2,1)S(1)}, u32[]{:S(2)}, u32[]{:S(2)}) collective-permute-start(bf16[1,96,384]{2,1,0:T(8,128)(2,1)S(1)} %add_convert_fusion.refs_0_), channel_id=1, source_target_pairs={{0,8},{4,12},{8,0},{12,4},{16,24},{20,28},{24,16},{28,20},{1,9},{5... | collective-permute-start | bytes 221192 | tf_op jit(solution)/shard_map/ppermute | solution.py:24
  36.9 5.2 %collective-permute-start.13 = (bf16[96,384]{1,0:T(8,128)(2,1)S(1)}, bf16[96,384]{1,0:T(8,128)(2,1)S(1)}, u32[]{:S(2)}, u32[]{:S(2)}) collective-permute-start(bf16[96,384]{1,0:T(8,128)(2,1)S(1)} %get-tuple-element.53), channel_id=1, source_target_pairs={{0,2},{1,3},{2,0},{3,1},{4,6},{5,7},{6,4},{7,5},{8,10},{9,11},{10,... | collective-permute-start | bytes 221192 | tf_op jit(solution)/shard_map/ppermute | solution.py:24
  38.2 4.7 %collective-permute-start.14 = (bf16[96,384]{1,0:T(8,128)(2,1)S(1)}, bf16[96,384]{1,0:T(8,128)(2,1)S(1)}, u32[]{:S(2)}, u32[]{:S(2)}) collective-permute-start(bf16[96,384]{1,0:T(8,128)(2,1)S(1)} %get-tuple-element.54), channel_id=1, source_target_pairs={{0,1},{1,0},{2,3},{3,2},{4,5},{5,4},{6,7},{7,6},{8,9},{9,8},{10,11... | collective-permute-start | bytes 221192 | tf_op jit(solution)/shard_map/ppermute | solution.py:24
  42.0 3.9 %collective-permute-start.15 = (bf16[96,384]{1,0:T(8,128)(2,1)S(1)}, bf16[96,384]{1,0:T(8,128)(2,1)S(1)}, u32[]{:S(2)}, u32[]{:S(2)}) collective-permute-start(bf16[96,384]{1,0:T(8,128)(2,1)S(1)} %get-tuple-element.55), channel_id=1, source_target_pairs={{0,3},{1,2},{2,1},{3,0},{4,7},{5,6},{6,5},{7,4},{8,11},{9,10},{10,... | collective-permute-start | bytes 221192 | tf_op jit(solution)/shard_map/ppermute | solution.py:24

commit v7 on v6

--- a/solution.py
+++ b/solution.py
@@ -286,7 +286,7 @@
             block = block_ref[...].astype(jnp.float32)
             flipped = block_ref[...].T.astype(jnp.float32)
             inverse = inverse_ref[pair]
-            energy = jnp.sum(block * (2.0 * block - flipped) * inverse)
+            energies.append(jnp.sum(block * (2.0 * block - flipped) * inverse))
             even = ((block + flipped) * inverse).astype(jnp.bfloat16)
             odd = ((block - flipped) * (inverse * 3.0**0.5)).astype(jnp.bfloat16)
             left = jnp.concatenate([even, odd], axis=1)
@@ -295,7 +295,6 @@
             total_ref[...] = term if pair == 0 else total_ref[...] + term
         for part in range(n_pair):
             totals[part] = total_ref[pl.ds(pl.multiple_of((pair_at ^ part) * rows, rows), rows), :]
-            energies.append(energy)
         own_ref[...] = totals[0]
         energy_ref[...] = jnp.zeros_like(energy_ref)
         for pair, energy in enumerate(energies):
@@ -352,7 +351,7 @@
                 spot = lane - first - 3 * at
                 found += jnp.where(here & (spot >= 0) & (spot < 3), part[rows - 1 :], 0.0)
                 total += part
-        value_ref[0] = jnp.sum(found)
+        value_ref[...] = jnp.sum(found, axis=1, keepdims=True)
         density_ref[...] = total
         head = -(-3 * pairs // TILE) * TILE
         top = total[:head]
@@ -368,8 +367,8 @@
     return pl.pallas_call(
         kernel,
         in_specs=whole(2 + len(others)),
-        out_specs=[pl.BlockSpec(memory_space=VMEM), pl.BlockSpec(memory_space=SMEM)],
-        out_shape=[jax.ShapeDtypeStruct((rows, virtual), jnp.float32), jax.ShapeDtypeStruct((1,), jnp.float32)],
+        out_specs=whole(2),
+        out_shape=[jax.ShapeDtypeStruct((rows, virtual), jnp.float32), jax.ShapeDtypeStruct((1, 1), jnp.float32)],
         compiler_params=PARAMS,
         name="closing",
     )(own, energies, *others)
@@ -441,7 +440,7 @@
     outs = density_parts(inverse, chunks, n_pair)
     others = exchanged(outs, "pair", ROW_ORDER)
     density, energy = closing(outs[0], outs[-1], others, pairs, n_half)
-    return (energy, density)
+    return (energy.reshape(1), density)
 
 
 def solution(mesh):

time: 46.8 us -> 46.8 us (level)
  no operation moved by 1% of the time
where the time goes in v7:
time: 46.8 us; the launch traced here: 46.6 us
  starting transfers between devices  19.7 us (42%)
  waiting for transfers between devices  15 us (32%)
  Pallas kernels  8.86 us (19%)
  other arithmetic  1.64 us (4%)
  between operations  1.42 us (3%)
    ppermute x16, starting transfers between devices, swapped(): lax.ppermute(value, axis, [(source, source ^ mask) for source in range(co...  19.7 us
    ppermute x16, waiting for transfers between devices, swapped(): lax.ppermute(value, axis, [(source, source ^ mask) for source in range(co...  15 us
    pallas_call x1, Pallas kernels, half_first(): pl.pallas_call(kernel, in_specs=[pl.BlockSpec(memory_space=pltpu.HBM)] *...  3.16 us
    pallas_call x1, Pallas kernels, half_rest(): pl.pallas_call(kernel, in_specs=[pl.BlockSpec(memory_space=SMEM)] + whole...  2.73 us
  transfers between devices with their start and end apart: 16, of which 10 were waited for; matrix products, arithmetic and copies ran while one was open for 3% of the time, Pallas kernels for 8%

profile of v7, /device:TPU:1, one launch (start us, length us, event | category | flops | bytes accessed | tf_op | source)
XLA Modules:
  0.0 46.6 jit_solution(2122090867990239372)
XLA Ops:
  0.7 3.2 %half_first.1 = (bf16[272,256]{1,0:T(8,128)(2,1)S(1)}, bf16[272,256]{1,0:T(8,128)(2,1)S(1)}, bf16[272,256]{1,0:T(8,128)(2,1)S(1)}, bf16[272,256]{1,0:T(8,128)(2,...) custom-call(s32[2,4]{1,0:T(2,128)} %bitcast.7, s32[512]{0:T(512)} %pick_hbm.1, ...), custom_call_target="tpu_custom_call" | custom-call | tf_op jit(solution)/shard_map/half_first/pallas_call | solution.py:77
  3.8 2.1 %collective-permute-start = (bf16[272,256]{1,0:T(8,128)(2,1)S(1)}, bf16[272,256]{1,0:T(8,128)(2,1)S(1)}, u32[]{:S(2)}, u32[]{:S(2)}) collective-permute-start(bf16[272,256]{1,0:T(8,128)(2,1)S(1)} %get-tuple-element.38), channel_id=1, source_target_pairs={{0,2},{1,3},{2,0},{3,1},{4,6},{5,7},{6,4},{7,5},{8,10},{9,11},{10,... | collective-permute-start | bytes 417800 | tf_op jit(solution)/shard_map/ppermute | solution.py:24
  6.0 1.0 %collective-permute-start.1 = (bf16[272,256]{1,0:T(8,128)(2,1)S(1)}, bf16[272,256]{1,0:T(8,128)(2,1)S(1)}, u32[]{:S(2)}, u32[]{:S(2)}) collective-permute-start(bf16[272,256]{1,0:T(8,128)(2,1)S(1)} %get-tuple-element.39), channel_id=1, source_target_pairs={{0,1},{1,0},{2,3},{3,2},{4,5},{5,4},{6,7},{7,6},{8,9},{9,8},{10,11... | collective-permute-start | bytes 417800 | tf_op jit(solution)/shard_map/ppermute | solution.py:24
  7.6 2.7 %half_rest.1 = (bf16[256,256]{1,0:T(8,128)(2,1)S(1)}, bf16[256,256]{1,0:T(8,128)(2,1)S(1)}, bf16[256,256]{1,0:T(8,128)(2,1)S(1)}, bf16[256,256]{1,0:T(8,128)(2,1)S(1)}) custom-call(s32[1]{0:T(128)S(6)} %copy.10.count_ref, bf16[64,512]{1,0:T(8,128)(2,1)S(1)} %get-tuple-element.32.chosen_ref, bf16[2,64,512]{2,1,0:T(8,128)(2,1)S(1)} %get-tuple-element.33.tables_ref, ...), custom_call_target="tpu_custom_call" | custom-call | tf_op jit(solution)/shard_map/half_rest/pallas_call | solution.py:150
  10.3 1.4 %collective-permute-start.3 = (bf16[256,256]{1,0:T(8,128)(2,1)S(1)}, bf16[256,256]{1,0:T(8,128)(2,1)S(1)}, u32[]{:S(2)}, u32[]{:S(2)}) collective-permute-start(bf16[256,256]{1,0:T(8,128)(2,1)S(1)} %get-tuple-element.43), channel_id=1, source_target_pairs={{0,2},{1,3},{2,0},{3,1},{4,6},{5,7},{6,4},{7,5},{8,10},{9,11},{10,... | collective-permute-start | bytes 393224 | tf_op jit(solution)/shard_map/ppermute | solution.py:24
  11.7 0.8 %collective-permute-start.4 = (bf16[256,256]{1,0:T(8,128)(2,1)S(1)}, bf16[256,256]{1,0:T(8,128)(2,1)S(1)}, u32[]{:S(2)}, u32[]{:S(2)}) collective-permute-start(bf16[256,256]{1,0:T(8,128)(2,1)S(1)} %get-tuple-element.44), channel_id=1, source_target_pairs={{0,1},{1,0},{2,3},{3,2},{4,5},{5,4},{6,7},{7,6},{8,9},{9,8},{10,11... | collective-permute-start | bytes 393224 | tf_op jit(solution)/shard_map/ppermute | solution.py:24
  13.7 1.8 %collective-permute-done.3.refs_4_ = bf16[256,256]{1,0:T(8,128)(2,1)S(1)} collective-permute-done((bf16[256,256]{1,0:T(8,128)(2,1)S(1)}, bf16[256,256]{1,0:T(8,128)(2,1)S(1)}, u32[]{:S(2)}, u32[]{:S(2)}) %collective-permute-start.3) | collective-permute-done | bytes 131104 | tf_op jit(solution)/shard_map/ppermute | solution.py:24
  16.0 2.5 %collective-permute-done.5.later_ref = bf16[256,256]{1,0:T(8,128)(2,1)S(1)} collective-permute-done((bf16[256,256]{1,0:T(8,128)(2,1)S(1)}, bf16[256,256]{1,0:T(8,128)(2,1)S(1)}, u32[]{:S(2)}, u32[]{:S(2)}) %collective-permute-start.5) | collective-permute-done | bytes 131104 | tf_op jit(solution)/shard_map/ppermute | solution.py:24
  19.1 2.5 %collective-permute-start.6 = (bf16[1,96,384]{2,1,0:T(8,128)(2,1)S(1)}, bf16[1,96,384]{2,1,0:T(8,128)(2,1)S(1)}, u32[]{:S(2)}, u32[]{:S(2)}) collective-permute-start(bf16[1,96,384]{2,1,0:T(8,128)(2,1)S(1)} %get-tuple-element.48), channel_id=1, source_target_pairs={{0,12},{4,8},{8,4},{12,0},{16,28},{20,24},{24,20},{28,16},{1,13},{... | collective-permute-start | bytes 221192 | tf_op jit(solution)/shard_map/ppermute | solution.py:24
  22.5 1.4 %collective-permute-done.6 = bf16[1,96,384]{2,1,0:T(8,128)(2,1)S(1)} collective-permute-done((bf16[1,96,384]{2,1,0:T(8,128)(2,1)S(1)}, bf16[1,96,384]{2,1,0:T(8,128)(2,1)S(1)}, u32[]{:S(2)}, u32[]{:S(2)}) %collective-permute-start.6) | collective-permute-done | bytes 73760 | tf_op jit(solution)/shard_map/ppermute | solution.py:24
  23.9 1.6 %collective-permute-done.7 = bf16[1,96,384]{2,1,0:T(8,128)(2,1)S(1)} collective-permute-done((bf16[1,96,384]{2,1,0:T(8,128)(2,1)S(1)}, bf16[1,96,384]{2,1,0:T(8,128)(2,1)S(1)}, u32[]{:S(2)}, u32[]{:S(2)}) %collective-permute-start.7) | collective-permute-done | bytes 73760 | tf_op jit(solution)/shard_map/ppermute | solution.py:24
  25.5 2.6 %collective-permute-start.9 = (bf16[1,96,384]{2,1,0:T(8,128)(2,1)S(1)}, bf16[1,96,384]{2,1,0:T(8,128)(2,1)S(1)}, u32[]{:S(2)}, u32[]{:S(2)}) collective-permute-start(bf16[1,96,384]{2,1,0:T(8,128)(2,1)S(1)} %add_convert_fusion.1), channel_id=1, source_target_pairs={{0,16},{4,20},{8,24},{12,28},{16,0},{20,4},{24,8},{28,12},{1,17},{... | collective-permute-start | bytes 221192 | tf_op jit(solution)/shard_map/ppermute | solution.py:24
  28.8 1.1 %collective-permute-done.9 = bf16[1,96,384]{2,1,0:T(8,128)(2,1)S(1)} collective-permute-done((bf16[1,96,384]{2,1,0:T(8,128)(2,1)S(1)}, bf16[1,96,384]{2,1,0:T(8,128)(2,1)S(1)}, u32[]{:S(2)}, u32[]{:S(2)}) %collective-permute-start.9) | collective-permute-done | bytes 73760 | tf_op jit(solution)/shard_map/ppermute | solution.py:24
  30.0 1.1 %collective-permute-start.10 = (bf16[1,96,384]{2,1,0:T(8,128)(2,1)S(1)}, bf16[1,96,384]{2,1,0:T(8,128)(2,1)S(1)}, u32[]{:S(2)}, u32[]{:S(2)}) collective-permute-start(bf16[1,96,384]{2,1,0:T(8,128)(2,1)S(1)} %add_convert_fusion.refs_0_), channel_id=1, source_target_pairs={{0,12},{4,8},{8,4},{12,0},{16,28},{20,24},{24,20},{28,16},{1,13},{... | collective-permute-start | bytes 221192 | tf_op jit(solution)/shard_map/ppermute | solution.py:24
  31.1 1.8 %collective-permute-start.11 = (bf16[1,96,384]{2,1,0:T(8,128)(2,1)S(1)}, bf16[1,96,384]{2,1,0:T(8,128)(2,1)S(1)}, u32[]{:S(2)}, u32[]{:S(2)}) collective-permute-start(bf16[1,96,384]{2,1,0:T(8,128)(2,1)S(1)} %add_convert_fusion.refs_0_), channel_id=1, source_target_pairs={{0,4},{4,0},{8,12},{12,8},{16,20},{20,16},{24,28},{28,24},{1,5},{5... | collective-permute-start | bytes 221192 | tf_op jit(solution)/shard_map/ppermute | solution.py:24
  33.2 0.9 %collective-permute-done.10.refs_1_ = bf16[1,96,384]{2,1,0:T(8,128)(2,1)S(1)} collective-permute-done((bf16[1,96,384]{2,1,0:T(8,128)(2,1)S(1)}, bf16[1,96,384]{2,1,0:T(8,128)(2,1)S(1)}, u32[]{:S(2)}, u32[]{:S(2)}) %collective-permute-start.10) | collective-permute-done | bytes 73760 | tf_op jit(solution)/shard_map/ppermute | solution.py:24
  34.1 0.8 %collective-permute-done.11.refs_2_ = bf16[1,96,384]{2,1,0:T(8,128)(2,1)S(1)} collective-permute-done((bf16[1,96,384]{2,1,0:T(8,128)(2,1)S(1)}, bf16[1,96,384]{2,1,0:T(8,128)(2,1)S(1)}, u32[]{:S(2)}, u32[]{:S(2)}) %collective-permute-start.11) | collective-permute-done | bytes 73760 | tf_op jit(solution)/shard_map/ppermute | solution.py:24
  34.9 1.2 %collective-permute-done.12.refs_3_ = bf16[1,96,384]{2,1,0:T(8,128)(2,1)S(1)} collective-permute-done((bf16[1,96,384]{2,1,0:T(8,128)(2,1)S(1)}, bf16[1,96,384]{2,1,0:T(8,128)(2,1)S(1)}, u32[]{:S(2)}, u32[]{:S(2)}) %collective-permute-start.12) | collective-permute-done | bytes 73760 | tf_op jit(solution)/shard_map/ppermute | solution.py:24
  36.1 0.8 %density_parts.1 = (f32[96,384]{1,0:T(8,128)S(1)}, bf16[96,384]{1,0:T(8,128)(2,1)S(1)}, bf16[96,384]{1,0:T(8,128)(2,1)S(1)}, bf16[96,384]{1,0:T(8,128)(2,1)S(1)}, f32[1,384]{1,0:T(1,128)S(1)}) custom-call(f32[1,384,384]{2,1,0:T(8,128)S(1)} %subtract_divide_fusion.inverse_ref, bf16[1,96,384]{2,1,0:T(8,128)(2,1)S(1)} %add_convert_fusion.refs_0_, ...), custom_call_target="tpu_custom_call" | custom-call | tf_op jit(solution)/shard_map/density_parts/pallas_call | solution.py:317
  36.9 1.3 %collective-permute-start.13 = (bf16[96,384]{1,0:T(8,128)(2,1)S(1)}, bf16[96,384]{1,0:T(8,128)(2,1)S(1)}, u32[]{:S(2)}, u32[]{:S(2)}) collective-permute-start(bf16[96,384]{1,0:T(8,128)(2,1)S(1)} %get-tuple-element.53), channel_id=1, source_target_pairs={{0,2},{1,3},{2,0},{3,1},{4,6},{5,7},{6,4},{7,5},{8,10},{9,11},{10,... | collective-permute-start | bytes 221192 | tf_op jit(solution)/shard_map/ppermute | solution.py:24
  38.2 3.8 %collective-permute-start.14 = (bf16[96,384]{1,0:T(8,128)(2,1)S(1)}, bf16[96,384]{1,0:T(8,128)(2,1)S(1)}, u32[]{:S(2)}, u32[]{:S(2)}) collective-permute-start(bf16[96,384]{1,0:T(8,128)(2,1)S(1)} %get-tuple-element.54), channel_id=1, source_target_pairs={{0,1},{1,0},{2,3},{3,2},{4,5},{5,4},{6,7},{7,6},{8,9},{9,8},{10,11... | collective-permute-start | bytes 221192 | tf_op jit(solution)/shard_map/ppermute | solution.py:24
  42.1 0.8 %collective-permute-done.14.refs_1_ = bf16[96,384]{1,0:T(8,128)(2,1)S(1)} collective-permute-done((bf16[96,384]{1,0:T(8,128)(2,1)S(1)}, bf16[96,384]{1,0:T(8,128)(2,1)S(1)}, u32[]{:S(2)}, u32[]{:S(2)}) %collective-permute-start.14) | collective-permute-done | bytes 73760 | tf_op jit(solution)/shard_map/ppermute | solution.py:24
  42.9 3.0 %collective-permute-done.15.refs_2_ = bf16[96,384]{1,0:T(8,128)(2,1)S(1)} collective-permute-done((bf16[96,384]{1,0:T(8,128)(2,1)S(1)}, bf16[96,384]{1,0:T(8,128)(2,1)S(1)}, u32[]{:S(2)}, u32[]{:S(2)}) %collective-permute-start.15) | collective-permute-done | bytes 73760 | tf_op jit(solution)/shard_map/ppermute | solution.py:24
  45.9 0.8 %closing.1 = (f32[96,384]{1,0:T(8,128)}, f32[1,1]{1,0:T(1,128)}) custom-call(f32[96,384]{1,0:T(8,128)S(1)} %get-tuple-element.51.own_ref, f32[1,384]{1,0:T(1,128)S(1)} %get-tuple-element.52.energy_ref, bf16[96,384]{1,0:T(8,128)(2,1)S(1)} %collective-permute-done.13.refs_0_, bf16[96,384]{1,0:T(8,128)(2,1)S(1)} %collective-permute-done.14.refs_1_, ...), custom_call_target="tpu_custom_call" | custom-call | tf_op jit(solution)/shard_map/closing/pallas_call | solution.py:367
  (29 shorter events, 4.3 us)
Async XLA Ops:
  0.6 12.5 %copy-start.2 = (f32[512]{0:T(512)S(1)}, f32[512]{0:T(512)}, u32[]{:S(2)}) copy-start(f32[512]{0:T(512)} %param.14) | copy-start | bytes 6148
  0.6 12.5 %slice-start = ((s32[512]{0:T(512)}), s32[8]{0:T(128)S(1)}, s32[]{:S(2)}) async-start(s32[512]{0:T(512)} %pick_hbm.1), calls=%async_computation | async-start | bytes 1024 | tf_op jit(solution)/shard_map/slice | solution.py:433
  0.7 12.7 %copy-start = (bf16[16,64,384]{2,1,0:T(8,128)(2,1)S(1)}, bf16[16,64,384]{2,1,0:T(8,128)(2,1)}, u32[]{:S(2)}) copy-start(bf16[16,64,384]{2,1,0:T(8,128)(2,1)} %vir_ref.1) | copy-start | bytes 2359300
  3.8 24.4 %copy-start.1 = (f32[384]{0:T(512)S(1)}, f32[384]{0:T(512)}, u32[]{:S(2)}) copy-start(f32[384]{0:T(512)} %param.15) | copy-start | bytes 4612
  3.8 8.7 %collective-permute-start = (bf16[272,256]{1,0:T(8,128)(2,1)S(1)}, bf16[272,256]{1,0:T(8,128)(2,1)S(1)}, u32[]{:S(2)}, u32[]{:S(2)}) collective-permute-start(bf16[272,256]{1,0:T(8,128)(2,1)S(1)} %get-tuple-element.38), channel_id=1, source_target_pairs={{0,2},{1,3},{2,0},{3,1},{4,6},{5,7},{6,4},{7,5},{8,10},{9,11},{10,... | collective-permute-start | bytes 417800 | tf_op jit(solution)/shard_map/ppermute | solution.py:24
  6.0 7.3 %collective-permute-start.1 = (bf16[272,256]{1,0:T(8,128)(2,1)S(1)}, bf16[272,256]{1,0:T(8,128)(2,1)S(1)}, u32[]{:S(2)}, u32[]{:S(2)}) collective-permute-start(bf16[272,256]{1,0:T(8,128)(2,1)S(1)} %get-tuple-element.39), channel_id=1, source_target_pairs={{0,1},{1,0},{2,3},{3,2},{4,5},{5,4},{6,7},{7,6},{8,9},{9,8},{10,11... | collective-permute-start | bytes 417800 | tf_op jit(solution)/shard_map/ppermute | solution.py:24
  6.9 6.4 %collective-permute-start.2 = (bf16[272,256]{1,0:T(8,128)(2,1)S(1)}, bf16[272,256]{1,0:T(8,128)(2,1)S(1)}, u32[]{:S(2)}, u32[]{:S(2)}) collective-permute-start(bf16[272,256]{1,0:T(8,128)(2,1)S(1)} %get-tuple-element.40), channel_id=1, source_target_pairs={{0,3},{1,2},{2,1},{3,0},{4,7},{5,6},{6,5},{7,4},{8,11},{9,10},{10,... | collective-permute-start | bytes 417800 | tf_op jit(solution)/shard_map/ppermute | solution.py:24
  10.3 5.2 %collective-permute-start.3 = (bf16[256,256]{1,0:T(8,128)(2,1)S(1)}, bf16[256,256]{1,0:T(8,128)(2,1)S(1)}, u32[]{:S(2)}, u32[]{:S(2)}) collective-permute-start(bf16[256,256]{1,0:T(8,128)(2,1)S(1)} %get-tuple-element.43), channel_id=1, source_target_pairs={{0,2},{1,3},{2,0},{3,1},{4,6},{5,7},{6,4},{7,5},{8,10},{9,11},{10,... | collective-permute-start | bytes 393224 | tf_op jit(solution)/shard_map/ppermute | solution.py:24
  11.7 3.7 %collective-permute-start.4 = (bf16[256,256]{1,0:T(8,128)(2,1)S(1)}, bf16[256,256]{1,0:T(8,128)(2,1)S(1)}, u32[]{:S(2)}, u32[]{:S(2)}) collective-permute-start(bf16[256,256]{1,0:T(8,128)(2,1)S(1)} %get-tuple-element.44), channel_id=1, source_target_pairs={{0,1},{1,0},{2,3},{3,2},{4,5},{5,4},{6,7},{7,6},{8,9},{9,8},{10,11... | collective-permute-start | bytes 393224 | tf_op jit(solution)/shard_map/ppermute | solution.py:24
  12.5 6.0 %collective-permute-start.5 = (bf16[256,256]{1,0:T(8,128)(2,1)S(1)}, bf16[256,256]{1,0:T(8,128)(2,1)S(1)}, u32[]{:S(2)}, u32[]{:S(2)}) collective-permute-start(bf16[256,256]{1,0:T(8,128)(2,1)S(1)} %get-tuple-element.46), channel_id=1, source_target_pairs={{0,3},{1,2},{2,1},{3,0},{4,7},{5,6},{6,5},{7,4},{8,11},{9,10},{10,... | collective-permute-start | bytes 393224 | tf_op jit(solution)/shard_map/ppermute | solution.py:24
  19.1 4.9 %collective-permute-start.6 = (bf16[1,96,384]{2,1,0:T(8,128)(2,1)S(1)}, bf16[1,96,384]{2,1,0:T(8,128)(2,1)S(1)}, u32[]{:S(2)}, u32[]{:S(2)}) collective-permute-start(bf16[1,96,384]{2,1,0:T(8,128)(2,1)S(1)} %get-tuple-element.48), channel_id=1, source_target_pairs={{0,12},{4,8},{8,4},{12,0},{16,28},{20,24},{24,20},{28,16},{1,13},{... | collective-permute-start | bytes 221192 | tf_op jit(solution)/shard_map/ppermute | solution.py:24
  21.6 3.9 %collective-permute-start.7 = (bf16[1,96,384]{2,1,0:T(8,128)(2,1)S(1)}, bf16[1,96,384]{2,1,0:T(8,128)(2,1)S(1)}, u32[]{:S(2)}, u32[]{:S(2)}) collective-permute-start(bf16[1,96,384]{2,1,0:T(8,128)(2,1)S(1)} %get-tuple-element.49), channel_id=1, source_target_pairs={{0,4},{4,0},{8,12},{12,8},{16,20},{20,16},{24,28},{28,24},{1,5},{5... | collective-permute-start | bytes 221192 | tf_op jit(solution)/shard_map/ppermute | solution.py:24
  21.8 3.6 %collective-permute-start.8 = (bf16[1,96,384]{2,1,0:T(8,128)(2,1)S(1)}, bf16[1,96,384]{2,1,0:T(8,128)(2,1)S(1)}, u32[]{:S(2)}, u32[]{:S(2)}) collective-permute-start(bf16[1,96,384]{2,1,0:T(8,128)(2,1)S(1)} %get-tuple-element.50), channel_id=1, source_target_pairs={{0,8},{4,12},{8,0},{12,4},{16,24},{20,28},{24,16},{28,20},{1,9},{5... | collective-permute-start | bytes 221192 | tf_op jit(solution)/shard_map/ppermute | solution.py:24
  25.5 4.4 %collective-permute-start.9 = (bf16[1,96,384]{2,1,0:T(8,128)(2,1)S(1)}, bf16[1,96,384]{2,1,0:T(8,128)(2,1)S(1)}, u32[]{:S(2)}, u32[]{:S(2)}) collective-permute-start(bf16[1,96,384]{2,1,0:T(8,128)(2,1)S(1)} %add_convert_fusion.1), channel_id=1, source_target_pairs={{0,16},{4,20},{8,24},{12,28},{16,0},{20,4},{24,8},{28,12},{1,17},{... | collective-permute-start | bytes 221192 | tf_op jit(solution)/shard_map/ppermute | solution.py:24
  30.0 4.2 %collective-permute-start.10 = (bf16[1,96,384]{2,1,0:T(8,128)(2,1)S(1)}, bf16[1,96,384]{2,1,0:T(8,128)(2,1)S(1)}, u32[]{:S(2)}, u32[]{:S(2)}) collective-permute-start(bf16[1,96,384]{2,1,0:T(8,128)(2,1)S(1)} %add_convert_fusion.refs_0_), channel_id=1, source_target_pairs={{0,12},{4,8},{8,4},{12,0},{16,28},{20,24},{24,20},{28,16},{1,13},{... | collective-permute-start | bytes 221192 | tf_op jit(solution)/shard_map/ppermute | solution.py:24
  31.1 3.8 %collective-permute-start.11 = (bf16[1,96,384]{2,1,0:T(8,128)(2,1)S(1)}, bf16[1,96,384]{2,1,0:T(8,128)(2,1)S(1)}, u32[]{:S(2)}, u32[]{:S(2)}) collective-permute-start(bf16[1,96,384]{2,1,0:T(8,128)(2,1)S(1)} %add_convert_fusion.refs_0_), channel_id=1, source_target_pairs={{0,4},{4,0},{8,12},{12,8},{16,20},{20,16},{24,28},{28,24},{1,5},{5... | collective-permute-start | bytes 221192 | tf_op jit(solution)/shard_map/ppermute | solution.py:24
  32.9 3.2 %collective-permute-start.12 = (bf16[1,96,384]{2,1,0:T(8,128)(2,1)S(1)}, bf16[1,96,384]{2,1,0:T(8,128)(2,1)S(1)}, u32[]{:S(2)}, u32[]{:S(2)}) collective-permute-start(bf16[1,96,384]{2,1,0:T(8,128)(2,1)S(1)} %add_convert_fusion.refs_0_), channel_id=1, source_target_pairs={{0,8},{4,12},{8,0},{12,4},{16,24},{20,28},{24,16},{28,20},{1,9},{5... | collective-permute-start | bytes 221192 | tf_op jit(solution)/shard_map/ppermute | solution.py:24
  36.9 5.2 %collective-permute-start.13 = (bf16[96,384]{1,0:T(8,128)(2,1)S(1)}, bf16[96,384]{1,0:T(8,128)(2,1)S(1)}, u32[]{:S(2)}, u32[]{:S(2)}) collective-permute-start(bf16[96,384]{1,0:T(8,128)(2,1)S(1)} %get-tuple-element.53), channel_id=1, source_target_pairs={{0,2},{1,3},{2,0},{3,1},{4,6},{5,7},{6,4},{7,5},{8,10},{9,11},{10,... | collective-permute-start | bytes 221192 | tf_op jit(solution)/shard_map/ppermute | solution.py:24
  38.2 4.7 %collective-permute-start.14 = (bf16[96,384]{1,0:T(8,128)(2,1)S(1)}, bf16[96,384]{1,0:T(8,128)(2,1)S(1)}, u32[]{:S(2)}, u32[]{:S(2)}) collective-permute-start(bf16[96,384]{1,0:T(8,128)(2,1)S(1)} %get-tuple-element.54), channel_id=1, source_target_pairs={{0,1},{1,0},{2,3},{3,2},{4,5},{5,4},{6,7},{7,6},{8,9},{9,8},{10,11... | collective-permute-start | bytes 221192 | tf_op jit(solution)/shard_map/ppermute | solution.py:24
  42.0 3.9 %collective-permute-start.15 = (bf16[96,384]{1,0:T(8,128)(2,1)S(1)}, bf16[96,384]{1,0:T(8,128)(2,1)S(1)}, u32[]{:S(2)}, u32[]{:S(2)}) collective-permute-start(bf16[96,384]{1,0:T(8,128)(2,1)S(1)} %get-tuple-element.55), channel_id=1, source_target_pairs={{0,3},{1,2},{2,1},{3,0},{4,7},{5,6},{6,5},{7,4},{8,11},{9,10},{10,... | collective-permute-start | bytes 221192 | tf_op jit(solution)/shard_map/ppermute | solution.py:24

commit v8 on v7

--- a/solution.py
+++ b/solution.py
@@ -10,6 +10,7 @@
 TILE = 16
 SUB = 8
 MARK = 128
+FAR = 3
 PARAMS = pltpu.CompilerParams(vmem_limit_bytes=48 * 1024 * 1024)
 
 
@@ -65,7 +66,7 @@
         blocks = jnp.zeros((TILE, aux_rows), jnp.float32)
         for slot in range(slots):
             blocks = jnp.where(row == slot, ids_ref[0, slot].astype(jnp.float32), blocks)
-        for out in outs:
+        for out in outs[:FAR]:
             out[pl.ds(rows, TILE), :] = blocks.astype(jnp.bfloat16)
         chosen_ref[...] = chosen
         for slot in range(count, slots):
@@ -78,7 +79,7 @@
         kernel,
         in_specs=[pl.BlockSpec(memory_space=pltpu.HBM)] * 4,
         out_specs=whole(n_pair + 2),
-        out_shape=[jax.ShapeDtypeStruct((rows + TILE, aux_rows), jnp.bfloat16)] * n_pair
+        out_shape=[jax.ShapeDtypeStruct((rows + TILE * (mate < FAR), aux_rows), jnp.bfloat16) for mate in range(n_pair)]
         + [
             jax.ShapeDtypeStruct((n_aux * SUB, nocc), jnp.bfloat16),
             jax.ShapeDtypeStruct((slots - count, width, nocc), jnp.bfloat16),
@@ -161,17 +162,18 @@
     )(block_count, chosen, tables, *in_hbm(ints.reshape(-1, aux_rows)))
 
 
-def fitted_first(vir_coef, parts, pairs, counts):
+def fitted_first(vir_coef, parts, names, pairs, counts):
     aux_rows = parts[0].shape[1]
     width, virtual = vir_coef.shape[1], vir_coef.shape[2]
     span = counts[0] * width
     rest_rows = (sum(counts) - 1) * width
 
-    def kernel(vir_ref, *refs):
+    def kernel(vir_ref, names_ref, *refs):
         held, (fitted_ref, rest_ref, last_ref, own_ref) = refs[: len(parts)], refs[len(parts) :]
         first, rest = [], []
-        for part in held:
-            tail = part[pl.ds(2 * pairs * span, TILE), :][:, :128].astype(jnp.float32)
+        for at, part in enumerate(held):
+            tail = names_ref[...] if at + 1 == len(held) else part[pl.ds(2 * pairs * span, TILE), :]
+            tail = tail[:, :128].astype(jnp.float32)
             found = [vir_ref[tail[slot, 0].astype(jnp.int32)] for slot in range(sum(counts))]
             first.append(found[0])
             rest.append(jnp.concatenate(found[1:], axis=0))
@@ -184,7 +186,7 @@
 
     return pl.pallas_call(
         kernel,
-        in_specs=whole(1 + len(parts)),
+        in_specs=whole(2 + len(parts)),
         out_specs=whole(3),
         out_shape=[
             jax.ShapeDtypeStruct((2 * pairs, virtual, aux_rows), jnp.float32),
@@ -194,7 +196,7 @@
         scratch_shapes=[VMEM((virtual, len(parts) * width), jnp.bfloat16)],
         compiler_params=PARAMS,
         name="fitted_first",
-    )(vir_coef, *parts)
+    )(vir_coef, names, *parts)
 
 
 def live_slots(later, counts, width):
@@ -423,7 +425,9 @@
 
     slowest = 1 + PAIR_ORDER.index(max(PAIR_ORDER))
     ends = [group.pop(slowest) for group in got]
-    fitted, rest, last = fitted_first(vir_coef, got[0] + ends[:1], pairs, counts)
+    near = got[0][1 + [d for d in PAIR_ORDER if d != FAR].index(FAR ^ 1)]
+    names = swapped(near[-TILE:], "pair", 1)
+    fitted, rest, last = fitted_first(vir_coef, got[0] + ends[:1], names, pairs, counts)
     fitted = fitted_more(fitted, rest, *got, counts, width)
     parts = coulomb_parts(fitted, last, *ends, pairs, counts, width, 4)
 

time: 46.8 us -> 46.9 us (level)
    ppermute x16 -> x17, waiting for transfers between devices: 15 us -> 15.4 us  [swapped(): lax.ppermute(value, axis, [(source, source ^ mask) for source in range(co...]
    ppermute x16 -> x17, starting transfers between devices: 19.7 us -> 19.4 us  [swapped(): lax.ppermute(value, axis, [(source, source ^ mask) for source in range(co...]
  transfers between devices with their start and end apart: 16 -> 17, of which waited for: 10 -> 10; matrix products, arithmetic and copies ran while one was open for 3% -> 3% of each run, Pallas kernels for 8% -> 8%
where the time goes in v8:
time: 46.9 us; the launch traced here: 46.8 us
  starting transfers between devices  19.4 us (41%)
  waiting for transfers between devices  15.4 us (33%)
  Pallas kernels  8.86 us (19%)
  other arithmetic  1.64 us (3%)
  between operations  1.43 us (3%)
    ppermute x17, starting transfers between devices, swapped(): lax.ppermute(value, axis, [(source, source ^ mask) for source in range(co...  19.4 us
    ppermute x17, waiting for transfers between devices, swapped(): lax.ppermute(value, axis, [(source, source ^ mask) for source in range(co...  15.4 us
    pallas_call x1, Pallas kernels, half_first(): pl.pallas_call(kernel, in_specs=[pl.BlockSpec(memory_space=pltpu.HBM)] *...  3.16 us
    pallas_call x1, Pallas kernels, half_rest(): pl.pallas_call(kernel, in_specs=[pl.BlockSpec(memory_space=SMEM)] + whole...  2.73 us
  transfers between devices with their start and end apart: 17, of which 10 were waited for; matrix products, arithmetic and copies ran while one was open for 3% of the time, Pallas kernels for 8%

profile of v8, /device:TPU:1, one launch (start us, length us, event | category | flops | bytes accessed | tf_op | source)
XLA Modules:
  0.0 46.8 jit_solution(15677893677406497770)
XLA Ops:
  0.7 3.2 %half_first.1 = (bf16[272,256]{1,0:T(8,128)(2,1)S(1)}, bf16[272,256]{1,0:T(8,128)(2,1)S(1)}, bf16[272,256]{1,0:T(8,128)(2,1)S(1)}, bf16[256,256]{1,0:T(8,128)(2,...) custom-call(s32[2,4]{1,0:T(2,128)} %bitcast.7, s32[512]{0:T(512)} %pick_hbm.1, ...), custom_call_target="tpu_custom_call" | custom-call | tf_op jit(solution)/shard_map/half_first/pallas_call | solution.py:78
  3.8 2.1 %collective-permute-start = (bf16[272,256]{1,0:T(8,128)(2,1)S(1)}, bf16[272,256]{1,0:T(8,128)(2,1)S(1)}, u32[]{:S(2)}, u32[]{:S(2)}) collective-permute-start(bf16[272,256]{1,0:T(8,128)(2,1)S(1)} %get-tuple-element.38), channel_id=1, source_target_pairs={{0,2},{1,3},{2,0},{3,1},{4,6},{5,7},{6,4},{7,5},{8,10},{9,11},{10,... | collective-permute-start | bytes 417800 | tf_op jit(solution)/shard_map/ppermute | solution.py:25
  7.6 2.7 %half_rest.1 = (bf16[256,256]{1,0:T(8,128)(2,1)S(1)}, bf16[256,256]{1,0:T(8,128)(2,1)S(1)}, bf16[256,256]{1,0:T(8,128)(2,1)S(1)}, bf16[256,256]{1,0:T(8,128)(2,1)S(1)}) custom-call(s32[1]{0:T(128)S(6)} %copy.10.count_ref, bf16[64,512]{1,0:T(8,128)(2,1)S(1)} %get-tuple-element.32.chosen_ref, bf16[2,64,512]{2,1,0:T(8,128)(2,1)S(1)} %get-tuple-element.33.tables_ref, ...), custom_call_target="tpu_custom_call" | custom-call | tf_op jit(solution)/shard_map/half_rest/pallas_call | solution.py:151
  10.3 1.4 %collective-permute-start.4 = (bf16[256,256]{1,0:T(8,128)(2,1)S(1)}, bf16[256,256]{1,0:T(8,128)(2,1)S(1)}, u32[]{:S(2)}, u32[]{:S(2)}) collective-permute-start(bf16[256,256]{1,0:T(8,128)(2,1)S(1)} %get-tuple-element.43), channel_id=1, source_target_pairs={{0,2},{1,3},{2,0},{3,1},{4,6},{5,7},{6,4},{7,5},{8,10},{9,11},{10,... | collective-permute-start | bytes 393224 | tf_op jit(solution)/shard_map/ppermute | solution.py:25
  11.7 0.8 %collective-permute-start.5 = (bf16[256,256]{1,0:T(8,128)(2,1)S(1)}, bf16[256,256]{1,0:T(8,128)(2,1)S(1)}, u32[]{:S(2)}, u32[]{:S(2)}) collective-permute-start(bf16[256,256]{1,0:T(8,128)(2,1)S(1)} %get-tuple-element.44), channel_id=1, source_target_pairs={{0,1},{1,0},{2,3},{3,2},{4,5},{5,4},{6,7},{7,6},{8,9},{9,8},{10,11... | collective-permute-start | bytes 393224 | tf_op jit(solution)/shard_map/ppermute | solution.py:25
  13.3 1.0 %collective-permute-done.1.names_ref = bf16[16,256]{1,0:T(8,128)(2,1)S(1)} collective-permute-done((bf16[16,256]{1,0:T(8,128)(2,1)S(1)}, bf16[16,256]{1,0:T(8,128)(2,1)S(1)}, u32[]{:S(2)}, u32[]{:S(2)}) %collective-permute-start.1) | collective-permute-done | bytes 8224 | tf_op jit(solution)/shard_map/ppermute | solution.py:25
  15.8 2.6 %collective-permute-done.6.later_ref = bf16[256,256]{1,0:T(8,128)(2,1)S(1)} collective-permute-done((bf16[256,256]{1,0:T(8,128)(2,1)S(1)}, bf16[256,256]{1,0:T(8,128)(2,1)S(1)}, u32[]{:S(2)}, u32[]{:S(2)}) %collective-permute-start.6) | collective-permute-done | bytes 131104 | tf_op jit(solution)/shard_map/ppermute | solution.py:25
  19.0 2.4 %collective-permute-start.7 = (bf16[1,96,384]{2,1,0:T(8,128)(2,1)S(1)}, bf16[1,96,384]{2,1,0:T(8,128)(2,1)S(1)}, u32[]{:S(2)}, u32[]{:S(2)}) collective-permute-start(bf16[1,96,384]{2,1,0:T(8,128)(2,1)S(1)} %get-tuple-element.48), channel_id=1, source_target_pairs={{0,12},{4,8},{8,4},{12,0},{16,28},{20,24},{24,20},{28,16},{1,13},{... | collective-permute-start | bytes 221192 | tf_op jit(solution)/shard_map/ppermute | solution.py:25
  22.4 1.4 %collective-permute-done.7 = bf16[1,96,384]{2,1,0:T(8,128)(2,1)S(1)} collective-permute-done((bf16[1,96,384]{2,1,0:T(8,128)(2,1)S(1)}, bf16[1,96,384]{2,1,0:T(8,128)(2,1)S(1)}, u32[]{:S(2)}, u32[]{:S(2)}) %collective-permute-start.7) | collective-permute-done | bytes 73760 | tf_op jit(solution)/shard_map/ppermute | solution.py:25
  23.8 1.7 %collective-permute-done.8 = bf16[1,96,384]{2,1,0:T(8,128)(2,1)S(1)} collective-permute-done((bf16[1,96,384]{2,1,0:T(8,128)(2,1)S(1)}, bf16[1,96,384]{2,1,0:T(8,128)(2,1)S(1)}, u32[]{:S(2)}, u32[]{:S(2)}) %collective-permute-start.8) | collective-permute-done | bytes 73760 | tf_op jit(solution)/shard_map/ppermute | solution.py:25
  25.6 2.5 %collective-permute-start.10 = (bf16[1,96,384]{2,1,0:T(8,128)(2,1)S(1)}, bf16[1,96,384]{2,1,0:T(8,128)(2,1)S(1)}, u32[]{:S(2)}, u32[]{:S(2)}) collective-permute-start(bf16[1,96,384]{2,1,0:T(8,128)(2,1)S(1)} %add_convert_fusion.1), channel_id=1, source_target_pairs={{0,16},{4,20},{8,24},{12,28},{16,0},{20,4},{24,8},{28,12},{1,17},{... | collective-permute-start | bytes 221192 | tf_op jit(solution)/shard_map/ppermute | solution.py:25
  28.1 0.6 %broadcast_subtract_fusion = f32[384]{0:T(512)S(1)} fusion(f32[384]{0:T(512)S(1)} %copy-done.1, f32[]{:T(128)} %fusion), kind=kLoop, calls=%fused_computation.7 | loop fusion | flops 384 | bytes 3076 | tf_op jit(solution)/shard_map/sub | solution.py:441
  28.8 1.1 %collective-permute-done.10 = bf16[1,96,384]{2,1,0:T(8,128)(2,1)S(1)} collective-permute-done((bf16[1,96,384]{2,1,0:T(8,128)(2,1)S(1)}, bf16[1,96,384]{2,1,0:T(8,128)(2,1)S(1)}, u32[]{:S(2)}, u32[]{:S(2)}) %collective-permute-start.10) | collective-permute-done | bytes 73760 | tf_op jit(solution)/shard_map/ppermute | solution.py:25
  29.9 1.4 %collective-permute-start.11 = (bf16[1,96,384]{2,1,0:T(8,128)(2,1)S(1)}, bf16[1,96,384]{2,1,0:T(8,128)(2,1)S(1)}, u32[]{:S(2)}, u32[]{:S(2)}) collective-permute-start(bf16[1,96,384]{2,1,0:T(8,128)(2,1)S(1)} %add_convert_fusion.refs_0_), channel_id=1, source_target_pairs={{0,12},{4,8},{8,4},{12,0},{16,28},{20,24},{24,20},{28,16},{1,13},{... | collective-permute-start | bytes 221192 | tf_op jit(solution)/shard_map/ppermute | solution.py:25
  31.3 2.6 %collective-permute-start.12 = (bf16[1,96,384]{2,1,0:T(8,128)(2,1)S(1)}, bf16[1,96,384]{2,1,0:T(8,128)(2,1)S(1)}, u32[]{:S(2)}, u32[]{:S(2)}) collective-permute-start(bf16[1,96,384]{2,1,0:T(8,128)(2,1)S(1)} %add_convert_fusion.refs_0_), channel_id=1, source_target_pairs={{0,4},{4,0},{8,12},{12,8},{16,20},{20,16},{24,28},{28,24},{1,5},{5... | collective-permute-start | bytes 221192 | tf_op jit(solution)/shard_map/ppermute | solution.py:25
  33.9 0.9 %collective-permute-start.13 = (bf16[1,96,384]{2,1,0:T(8,128)(2,1)S(1)}, bf16[1,96,384]{2,1,0:T(8,128)(2,1)S(1)}, u32[]{:S(2)}, u32[]{:S(2)}) collective-permute-start(bf16[1,96,384]{2,1,0:T(8,128)(2,1)S(1)} %add_convert_fusion.refs_0_), channel_id=1, source_target_pairs={{0,8},{4,12},{8,0},{12,4},{16,24},{20,28},{24,16},{28,20},{1,9},{5... | collective-permute-start | bytes 221192 | tf_op jit(solution)/shard_map/ppermute | solution.py:25
  35.0 0.7 %collective-permute-done.12.refs_2_ = bf16[1,96,384]{2,1,0:T(8,128)(2,1)S(1)} collective-permute-done((bf16[1,96,384]{2,1,0:T(8,128)(2,1)S(1)}, bf16[1,96,384]{2,1,0:T(8,128)(2,1)S(1)}, u32[]{:S(2)}, u32[]{:S(2)}) %collective-permute-start.12) | collective-permute-done | bytes 73760 | tf_op jit(solution)/shard_map/ppermute | solution.py:25
  35.6 2.4 %collective-permute-done.13.refs_3_ = bf16[1,96,384]{2,1,0:T(8,128)(2,1)S(1)} collective-permute-done((bf16[1,96,384]{2,1,0:T(8,128)(2,1)S(1)}, bf16[1,96,384]{2,1,0:T(8,128)(2,1)S(1)}, u32[]{:S(2)}, u32[]{:S(2)}) %collective-permute-start.13) | collective-permute-done | bytes 73760 | tf_op jit(solution)/shard_map/ppermute | solution.py:25
  38.0 0.8 %density_parts.1 = (f32[96,384]{1,0:T(8,128)S(1)}, bf16[96,384]{1,0:T(8,128)(2,1)S(1)}, bf16[96,384]{1,0:T(8,128)(2,1)S(1)}, bf16[96,384]{1,0:T(8,128)(2,1)S(1)}, f32[1,384]{1,0:T(1,128)S(1)}) custom-call(f32[1,384,384]{2,1,0:T(8,128)S(1)} %subtract_divide_fusion.inverse_ref, bf16[1,96,384]{2,1,0:T(8,128)(2,1)S(1)} %add_convert_fusion.refs_0_, ...), custom_call_target="tpu_custom_call" | custom-call | tf_op jit(solution)/shard_map/density_parts/pallas_call | solution.py:319
  38.8 1.5 %collective-permute-start.14 = (bf16[96,384]{1,0:T(8,128)(2,1)S(1)}, bf16[96,384]{1,0:T(8,128)(2,1)S(1)}, u32[]{:S(2)}, u32[]{:S(2)}) collective-permute-start(bf16[96,384]{1,0:T(8,128)(2,1)S(1)} %get-tuple-element.53), channel_id=1, source_target_pairs={{0,2},{1,3},{2,0},{3,1},{4,6},{5,7},{6,4},{7,5},{8,10},{9,11},{10,... | collective-permute-start | bytes 221192 | tf_op jit(solution)/shard_map/ppermute | solution.py:25
  40.4 1.7 %collective-permute-start.15 = (bf16[96,384]{1,0:T(8,128)(2,1)S(1)}, bf16[96,384]{1,0:T(8,128)(2,1)S(1)}, u32[]{:S(2)}, u32[]{:S(2)}) collective-permute-start(bf16[96,384]{1,0:T(8,128)(2,1)S(1)} %get-tuple-element.54), channel_id=1, source_target_pairs={{0,1},{1,0},{2,3},{3,2},{4,5},{5,4},{6,7},{7,6},{8,9},{9,8},{10,11... | collective-permute-start | bytes 221192 | tf_op jit(solution)/shard_map/ppermute | solution.py:25
  42.1 0.9 %collective-permute-done.15.refs_1_ = bf16[96,384]{1,0:T(8,128)(2,1)S(1)} collective-permute-done((bf16[96,384]{1,0:T(8,128)(2,1)S(1)}, bf16[96,384]{1,0:T(8,128)(2,1)S(1)}, u32[]{:S(2)}, u32[]{:S(2)}) %collective-permute-start.15) | collective-permute-done | bytes 73760 | tf_op jit(solution)/shard_map/ppermute | solution.py:25
  43.0 3.0 %collective-permute-done.16.refs_2_ = bf16[96,384]{1,0:T(8,128)(2,1)S(1)} collective-permute-done((bf16[96,384]{1,0:T(8,128)(2,1)S(1)}, bf16[96,384]{1,0:T(8,128)(2,1)S(1)}, u32[]{:S(2)}, u32[]{:S(2)}) %collective-permute-start.16) | collective-permute-done | bytes 73760 | tf_op jit(solution)/shard_map/ppermute | solution.py:25
  46.0 0.8 %closing.1 = (f32[96,384]{1,0:T(8,128)}, f32[1,1]{1,0:T(1,128)}) custom-call(f32[96,384]{1,0:T(8,128)S(1)} %get-tuple-element.51.own_ref, f32[1,384]{1,0:T(1,128)S(1)} %get-tuple-element.52.energy_ref, bf16[96,384]{1,0:T(8,128)(2,1)S(1)} %collective-permute-done.14.refs_0_, bf16[96,384]{1,0:T(8,128)(2,1)S(1)} %collective-permute-done.15.refs_1_, ...), custom_call_target="tpu_custom_call" | custom-call | tf_op jit(solution)/shard_map/closing/pallas_call | solution.py:369
  (32 shorter events, 5.0 us)
Async XLA Ops:
  0.6 12.5 %copy-start.2 = (f32[512]{0:T(512)S(1)}, f32[512]{0:T(512)}, u32[]{:S(2)}) copy-start(f32[512]{0:T(512)} %param.14) | copy-start | bytes 6148
  0.6 12.5 %slice-start = ((s32[512]{0:T(512)}), s32[8]{0:T(128)S(1)}, s32[]{:S(2)}) async-start(s32[512]{0:T(512)} %pick_hbm.1), calls=%async_computation | async-start | bytes 1024 | tf_op jit(solution)/shard_map/slice | solution.py:437
  0.7 13.6 %copy-start = (bf16[16,64,384]{2,1,0:T(8,128)(2,1)S(1)}, bf16[16,64,384]{2,1,0:T(8,128)(2,1)}, u32[]{:S(2)}) copy-start(bf16[16,64,384]{2,1,0:T(8,128)(2,1)} %vir_ref.1) | copy-start | bytes 2359300
  3.8 24.3 %copy-start.1 = (f32[384]{0:T(512)S(1)}, f32[384]{0:T(512)}, u32[]{:S(2)}) copy-start(f32[384]{0:T(512)} %param.15) | copy-start | bytes 4612
  3.8 8.7 %collective-permute-start = (bf16[272,256]{1,0:T(8,128)(2,1)S(1)}, bf16[272,256]{1,0:T(8,128)(2,1)S(1)}, u32[]{:S(2)}, u32[]{:S(2)}) collective-permute-start(bf16[272,256]{1,0:T(8,128)(2,1)S(1)} %get-tuple-element.38), channel_id=1, source_target_pairs={{0,2},{1,3},{2,0},{3,1},{4,6},{5,7},{6,4},{7,5},{8,10},{9,11},{10,... | collective-permute-start | bytes 417800 | tf_op jit(solution)/shard_map/ppermute | solution.py:25
  6.0 7.1 %collective-permute-start.3 = (bf16[256,256]{1,0:T(8,128)(2,1)S(1)}, bf16[256,256]{1,0:T(8,128)(2,1)S(1)}, u32[]{:S(2)}, u32[]{:S(2)}) collective-permute-start(bf16[256,256]{1,0:T(8,128)(2,1)S(1)} %get-tuple-element.40), channel_id=1, source_target_pairs={{0,3},{1,2},{2,1},{3,0},{4,7},{5,6},{6,5},{7,4},{8,11},{9,10},{10,... | collective-permute-start | bytes 393224 | tf_op jit(solution)/shard_map/ppermute | solution.py:25
  6.6 6.7 %collective-permute-start.2 = (bf16[272,256]{1,0:T(8,128)(2,1)S(1)}, bf16[272,256]{1,0:T(8,128)(2,1)S(1)}, u32[]{:S(2)}, u32[]{:S(2)}) collective-permute-start(bf16[272,256]{1,0:T(8,128)(2,1)S(1)} %get-tuple-element.39), channel_id=1, source_target_pairs={{0,1},{1,0},{2,3},{3,2},{4,5},{5,4},{6,7},{7,6},{8,9},{9,8},{10,11... | collective-permute-start | bytes 417800 | tf_op jit(solution)/shard_map/ppermute | solution.py:25
  10.3 5.0 %collective-permute-start.4 = (bf16[256,256]{1,0:T(8,128)(2,1)S(1)}, bf16[256,256]{1,0:T(8,128)(2,1)S(1)}, u32[]{:S(2)}, u32[]{:S(2)}) collective-permute-start(bf16[256,256]{1,0:T(8,128)(2,1)S(1)} %get-tuple-element.43), channel_id=1, source_target_pairs={{0,2},{1,3},{2,0},{3,1},{4,6},{5,7},{6,4},{7,5},{8,10},{9,11},{10,... | collective-permute-start | bytes 393224 | tf_op jit(solution)/shard_map/ppermute | solution.py:25
  11.7 3.6 %collective-permute-start.5 = (bf16[256,256]{1,0:T(8,128)(2,1)S(1)}, bf16[256,256]{1,0:T(8,128)(2,1)S(1)}, u32[]{:S(2)}, u32[]{:S(2)}) collective-permute-start(bf16[256,256]{1,0:T(8,128)(2,1)S(1)} %get-tuple-element.44), channel_id=1, source_target_pairs={{0,1},{1,0},{2,3},{3,2},{4,5},{5,4},{6,7},{7,6},{8,9},{9,8},{10,11... | collective-permute-start | bytes 393224 | tf_op jit(solution)/shard_map/ppermute | solution.py:25
  12.5 5.9 %collective-permute-start.6 = (bf16[256,256]{1,0:T(8,128)(2,1)S(1)}, bf16[256,256]{1,0:T(8,128)(2,1)S(1)}, u32[]{:S(2)}, u32[]{:S(2)}) collective-permute-start(bf16[256,256]{1,0:T(8,128)(2,1)S(1)} %get-tuple-element.46), channel_id=1, source_target_pairs={{0,3},{1,2},{2,1},{3,0},{4,7},{5,6},{6,5},{7,4},{8,11},{9,10},{10,... | collective-permute-start | bytes 393224 | tf_op jit(solution)/shard_map/ppermute | solution.py:25
  13.1 1.2 %collective-permute-start.1 = (bf16[16,256]{1,0:T(8,128)(2,1)S(1)}, bf16[16,256]{1,0:T(8,128)(2,1)S(1)}, u32[]{:S(2)}, u32[]{:S(2)}) collective-permute-start(bf16[16,256]{1,0:T(8,128)(2,1)S(1)} %slice.8), channel_id=1, source_target_pairs={{0,1},{1,0},{2,3},{3,2},{4,5},{5,4},{6,7},{7,6},{8,9},{9,8},{10,11... | collective-permute-start | bytes 24584 | tf_op jit(solution)/shard_map/ppermute | solution.py:25
  19.0 4.8 %collective-permute-start.7 = (bf16[1,96,384]{2,1,0:T(8,128)(2,1)S(1)}, bf16[1,96,384]{2,1,0:T(8,128)(2,1)S(1)}, u32[]{:S(2)}, u32[]{:S(2)}) collective-permute-start(bf16[1,96,384]{2,1,0:T(8,128)(2,1)S(1)} %get-tuple-element.48), channel_id=1, source_target_pairs={{0,12},{4,8},{8,4},{12,0},{16,28},{20,24},{24,20},{28,16},{1,13},{... | collective-permute-start | bytes 221192 | tf_op jit(solution)/shard_map/ppermute | solution.py:25
  21.4 4.1 %collective-permute-start.8 = (bf16[1,96,384]{2,1,0:T(8,128)(2,1)S(1)}, bf16[1,96,384]{2,1,0:T(8,128)(2,1)S(1)}, u32[]{:S(2)}, u32[]{:S(2)}) collective-permute-start(bf16[1,96,384]{2,1,0:T(8,128)(2,1)S(1)} %get-tuple-element.49), channel_id=1, source_target_pairs={{0,4},{4,0},{8,12},{12,8},{16,20},{20,16},{24,28},{28,24},{1,5},{5... | collective-permute-start | bytes 221192 | tf_op jit(solution)/shard_map/ppermute | solution.py:25
  21.7 3.9 %collective-permute-start.9 = (bf16[1,96,384]{2,1,0:T(8,128)(2,1)S(1)}, bf16[1,96,384]{2,1,0:T(8,128)(2,1)S(1)}, u32[]{:S(2)}, u32[]{:S(2)}) collective-permute-start(bf16[1,96,384]{2,1,0:T(8,128)(2,1)S(1)} %get-tuple-element.50), channel_id=1, source_target_pairs={{0,8},{4,12},{8,0},{12,4},{16,24},{20,28},{24,16},{28,20},{1,9},{5... | collective-permute-start | bytes 221192 | tf_op jit(solution)/shard_map/ppermute | solution.py:25
  25.6 4.3 %collective-permute-start.10 = (bf16[1,96,384]{2,1,0:T(8,128)(2,1)S(1)}, bf16[1,96,384]{2,1,0:T(8,128)(2,1)S(1)}, u32[]{:S(2)}, u32[]{:S(2)}) collective-permute-start(bf16[1,96,384]{2,1,0:T(8,128)(2,1)S(1)} %add_convert_fusion.1), channel_id=1, source_target_pairs={{0,16},{4,20},{8,24},{12,28},{16,0},{20,4},{24,8},{28,12},{1,17},{... | collective-permute-start | bytes 221192 | tf_op jit(solution)/shard_map/ppermute | solution.py:25
  29.9 5.1 %collective-permute-start.11 = (bf16[1,96,384]{2,1,0:T(8,128)(2,1)S(1)}, bf16[1,96,384]{2,1,0:T(8,128)(2,1)S(1)}, u32[]{:S(2)}, u32[]{:S(2)}) collective-permute-start(bf16[1,96,384]{2,1,0:T(8,128)(2,1)S(1)} %add_convert_fusion.refs_0_), channel_id=1, source_target_pairs={{0,12},{4,8},{8,4},{12,0},{16,28},{20,24},{24,20},{28,16},{1,13},{... | collective-permute-start | bytes 221192 | tf_op jit(solution)/shard_map/ppermute | solution.py:25
  31.3 4.3 %collective-permute-start.12 = (bf16[1,96,384]{2,1,0:T(8,128)(2,1)S(1)}, bf16[1,96,384]{2,1,0:T(8,128)(2,1)S(1)}, u32[]{:S(2)}, u32[]{:S(2)}) collective-permute-start(bf16[1,96,384]{2,1,0:T(8,128)(2,1)S(1)} %add_convert_fusion.refs_0_), channel_id=1, source_target_pairs={{0,4},{4,0},{8,12},{12,8},{16,20},{20,16},{24,28},{28,24},{1,5},{5... | collective-permute-start | bytes 221192 | tf_op jit(solution)/shard_map/ppermute | solution.py:25
  33.9 4.1 %collective-permute-start.13 = (bf16[1,96,384]{2,1,0:T(8,128)(2,1)S(1)}, bf16[1,96,384]{2,1,0:T(8,128)(2,1)S(1)}, u32[]{:S(2)}, u32[]{:S(2)}) collective-permute-start(bf16[1,96,384]{2,1,0:T(8,128)(2,1)S(1)} %add_convert_fusion.refs_0_), channel_id=1, source_target_pairs={{0,8},{4,12},{8,0},{12,4},{16,24},{20,28},{24,16},{28,20},{1,9},{5... | collective-permute-start | bytes 221192 | tf_op jit(solution)/shard_map/ppermute | solution.py:25
  38.8 3.3 %collective-permute-start.14 = (bf16[96,384]{1,0:T(8,128)(2,1)S(1)}, bf16[96,384]{1,0:T(8,128)(2,1)S(1)}, u32[]{:S(2)}, u32[]{:S(2)}) collective-permute-start(bf16[96,384]{1,0:T(8,128)(2,1)S(1)} %get-tuple-element.53), channel_id=1, source_target_pairs={{0,2},{1,3},{2,0},{3,1},{4,6},{5,7},{6,4},{7,5},{8,10},{9,11},{10,... | collective-permute-start | bytes 221192 | tf_op jit(solution)/shard_map/ppermute | solution.py:25
  40.4 2.7 %collective-permute-start.15 = (bf16[96,384]{1,0:T(8,128)(2,1)S(1)}, bf16[96,384]{1,0:T(8,128)(2,1)S(1)}, u32[]{:S(2)}, u32[]{:S(2)}) collective-permute-start(bf16[96,384]{1,0:T(8,128)(2,1)S(1)} %get-tuple-element.54), channel_id=1, source_target_pairs={{0,1},{1,0},{2,3},{3,2},{4,5},{5,4},{6,7},{7,6},{8,9},{9,8},{10,11... | collective-permute-start | bytes 221192 | tf_op jit(solution)/shard_map/ppermute | solution.py:25
  42.1 3.9 %collective-permute-start.16 = (bf16[96,384]{1,0:T(8,128)(2,1)S(1)}, bf16[96,384]{1,0:T(8,128)(2,1)S(1)}, u32[]{:S(2)}, u32[]{:S(2)}) collective-permute-start(bf16[96,384]{1,0:T(8,128)(2,1)S(1)} %get-tuple-element.55), channel_id=1, source_target_pairs={{0,3},{1,2},{2,1},{3,0},{4,7},{5,6},{6,5},{7,4},{8,11},{9,10},{10,... | collective-permute-start | bytes 221192 | tf_op jit(solution)/shard_map/ppermute | solution.py:25

commit v9 on v7

--- a/solution.py
+++ b/solution.py
@@ -240,7 +240,7 @@
     share = virtual // quad
 
     def kernel(fitted_ref, last_ref, first_ref, later_ref, *refs):
-        outs, block_ref = refs[:-1], refs[-1]
+        outs, left_ref = refs[:-1], refs[-1]
         place = lax.axis_index("aux") % quad
         live = live_slots(later_ref, counts, width)
         for pair in range(pairs):
@@ -249,18 +249,20 @@
                 blocks = jnp.concatenate(live_blocks(first_ref, later_ref, live, orbital, counts, width), axis=0)
                 total = jnp.dot(last_ref[...], blocks, preferred_element_type=jnp.float32)
                 sides.append((fitted_ref[orbital] + total).astype(jnp.bfloat16))
-            block = lax.dot_general(*sides, (((1,), (1,)), ((), ())), preferred_element_type=jnp.float32)
-            block_ref[...] = block.astype(jnp.bfloat16)
+            left_ref[...] = sides[0]
+            left = [left_ref[pl.ds(pl.multiple_of((place ^ part) * share, share), share), :] for part in range(quad)]
+            block = lax.dot_general(
+                jnp.concatenate(left, axis=0), sides[1], (((1,), (1,)), ((), ())), preferred_element_type=jnp.float32
+            )
             for part, out in enumerate(outs):
-                at = pl.multiple_of((place ^ part) * share, share)
-                out[pair] = block_ref[pl.ds(at, share), :]
+                out[pair] = block[part * share : (part + 1) * share].astype(jnp.bfloat16)
 
     return pl.pallas_call(
         kernel,
         in_specs=whole(4),
         out_specs=whole(quad),
         out_shape=[jax.ShapeDtypeStruct((pairs, share, virtual), jnp.bfloat16)] * quad,
-        scratch_shapes=[VMEM((virtual, virtual), jnp.bfloat16)],
+        scratch_shapes=[VMEM(fitted.shape[1:], jnp.bfloat16)],
         compiler_params=PARAMS,
         name="coulomb_parts",
     )(fitted, last, first, later)
@@ -273,7 +275,7 @@
 
     def kernel(inverse_ref, *refs):
         held, own_ref, outs = refs[:quad], refs[quad], refs[quad + 1 : quad + n_pair]
-        energy_ref, block_ref, total_ref = refs[quad + n_pair :]
+        energy_ref, block_ref, left_ref = refs[quad + n_pair :]
         place = lax.axis_index("aux") % quad
         pair_at = lax.axis_index("pair")
         lane = lax.broadcasted_iota(jnp.int32, (1, virtual), 1)
@@ -289,12 +291,13 @@
             energies.append(jnp.sum(block * (2.0 * block - flipped) * inverse))
             even = ((block + flipped) * inverse).astype(jnp.bfloat16)
             odd = ((block - flipped) * (inverse * 3.0**0.5)).astype(jnp.bfloat16)
-            left = jnp.concatenate([even, odd], axis=1)
+            left_ref[...] = jnp.concatenate([even, odd], axis=1)
+            left = [left_ref[pl.ds(pl.multiple_of((pair_at ^ part) * rows, rows), rows), :] for part in range(n_pair)]
             right = jnp.concatenate([even, -odd], axis=0)
-            term = 0.5 * jnp.dot(left, right, preferred_element_type=jnp.float32)
-            total_ref[...] = term if pair == 0 else total_ref[...] + term
-        for part in range(n_pair):
-            totals[part] = total_ref[pl.ds(pl.multiple_of((pair_at ^ part) * rows, rows), rows), :]
+            term = 0.5 * jnp.dot(jnp.concatenate(left, axis=0), right, preferred_element_type=jnp.float32)
+            for part in range(n_pair):
+                piece = term[part * rows : (part + 1) * rows]
+                totals[part] = piece if pair == 0 else totals[part] + piece
         own_ref[...] = totals[0]
         energy_ref[...] = jnp.zeros_like(energy_ref)
         for pair, energy in enumerate(energies):
@@ -323,7 +326,7 @@
         + [jax.ShapeDtypeStruct((1, virtual), jnp.float32)],
         scratch_shapes=[
             VMEM((virtual, virtual), jnp.bfloat16),
-            VMEM((virtual, virtual), jnp.float32),
+            VMEM((virtual, 2 * virtual), jnp.bfloat16),
         ],
         compiler_params=PARAMS,
         name="density_parts",

time: 46.8 us -> 46.8 us (level)
  no operation moved by 1% of the time
where the time goes in v9:
time: 46.8 us; the launch traced here: 46.6 us
  starting transfers between devices  19.6 us (42%)
  waiting for transfers between devices  15 us (32%)
  Pallas kernels  8.86 us (19%)
  other arithmetic  1.64 us (4%)
  between operations  1.42 us (3%)
    ppermute x16, starting transfers between devices, swapped(): lax.ppermute(value, axis, [(source, source ^ mask) for source in range(co...  19.6 us
    ppermute x16, waiting for transfers between devices, swapped(): lax.ppermute(value, axis, [(source, source ^ mask) for source in range(co...  15 us
    pallas_call x1, Pallas kernels, half_first(): pl.pallas_call(kernel, in_specs=[pl.BlockSpec(memory_space=pltpu.HBM)] *...  3.16 us
    pallas_call x1, Pallas kernels, half_rest(): pl.pallas_call(kernel, in_specs=[pl.BlockSpec(memory_space=SMEM)] + whole...  2.73 us
  transfers between devices with their start and end apart: 16, of which 10 were waited for; matrix products, arithmetic and copies ran while one was open for 3% of the time, Pallas kernels for 8%

profile of v9, /device:TPU:1, one launch (start us, length us, event | category | flops | bytes accessed | tf_op | source)
XLA Modules:
  0.0 46.6 jit_solution(9296160477616460379)
XLA Ops:
  0.7 3.2 %half_first.1 = (bf16[272,256]{1,0:T(8,128)(2,1)S(1)}, bf16[272,256]{1,0:T(8,128)(2,1)S(1)}, bf16[272,256]{1,0:T(8,128)(2,1)S(1)}, bf16[272,256]{1,0:T(8,128)(2,...) custom-call(s32[2,4]{1,0:T(2,128)} %bitcast.7, s32[512]{0:T(512)} %pick_hbm.1, ...), custom_call_target="tpu_custom_call" | custom-call | tf_op jit(solution)/shard_map/half_first/pallas_call | solution.py:77
  3.8 2.1 %collective-permute-start = (bf16[272,256]{1,0:T(8,128)(2,1)S(1)}, bf16[272,256]{1,0:T(8,128)(2,1)S(1)}, u32[]{:S(2)}, u32[]{:S(2)}) collective-permute-start(bf16[272,256]{1,0:T(8,128)(2,1)S(1)} %get-tuple-element.38), channel_id=1, source_target_pairs={{0,2},{1,3},{2,0},{3,1},{4,6},{5,7},{6,4},{7,5},{8,10},{9,11},{10,... | collective-permute-start | bytes 417800 | tf_op jit(solution)/shard_map/ppermute | solution.py:24
  6.0 1.0 %collective-permute-start.1 = (bf16[272,256]{1,0:T(8,128)(2,1)S(1)}, bf16[272,256]{1,0:T(8,128)(2,1)S(1)}, u32[]{:S(2)}, u32[]{:S(2)}) collective-permute-start(bf16[272,256]{1,0:T(8,128)(2,1)S(1)} %get-tuple-element.39), channel_id=1, source_target_pairs={{0,1},{1,0},{2,3},{3,2},{4,5},{5,4},{6,7},{7,6},{8,9},{9,8},{10,11... | collective-permute-start | bytes 417800 | tf_op jit(solution)/shard_map/ppermute | solution.py:24
  7.6 2.7 %half_rest.1 = (bf16[256,256]{1,0:T(8,128)(2,1)S(1)}, bf16[256,256]{1,0:T(8,128)(2,1)S(1)}, bf16[256,256]{1,0:T(8,128)(2,1)S(1)}, bf16[256,256]{1,0:T(8,128)(2,1)S(1)}) custom-call(s32[1]{0:T(128)S(6)} %copy.10.count_ref, bf16[64,512]{1,0:T(8,128)(2,1)S(1)} %get-tuple-element.32.chosen_ref, bf16[2,64,512]{2,1,0:T(8,128)(2,1)S(1)} %get-tuple-element.33.tables_ref, ...), custom_call_target="tpu_custom_call" | custom-call | tf_op jit(solution)/shard_map/half_rest/pallas_call | solution.py:150
  10.3 1.4 %collective-permute-start.3 = (bf16[256,256]{1,0:T(8,128)(2,1)S(1)}, bf16[256,256]{1,0:T(8,128)(2,1)S(1)}, u32[]{:S(2)}, u32[]{:S(2)}) collective-permute-start(bf16[256,256]{1,0:T(8,128)(2,1)S(1)} %get-tuple-element.43), channel_id=1, source_target_pairs={{0,2},{1,3},{2,0},{3,1},{4,6},{5,7},{6,4},{7,5},{8,10},{9,11},{10,... | collective-permute-start | bytes 393224 | tf_op jit(solution)/shard_map/ppermute | solution.py:24
  11.7 0.8 %collective-permute-start.4 = (bf16[256,256]{1,0:T(8,128)(2,1)S(1)}, bf16[256,256]{1,0:T(8,128)(2,1)S(1)}, u32[]{:S(2)}, u32[]{:S(2)}) collective-permute-start(bf16[256,256]{1,0:T(8,128)(2,1)S(1)} %get-tuple-element.44), channel_id=1, source_target_pairs={{0,1},{1,0},{2,3},{3,2},{4,5},{5,4},{6,7},{7,6},{8,9},{9,8},{10,11... | collective-permute-start | bytes 393224 | tf_op jit(solution)/shard_map/ppermute | solution.py:24
  13.7 1.8 %collective-permute-done.3.refs_4_ = bf16[256,256]{1,0:T(8,128)(2,1)S(1)} collective-permute-done((bf16[256,256]{1,0:T(8,128)(2,1)S(1)}, bf16[256,256]{1,0:T(8,128)(2,1)S(1)}, u32[]{:S(2)}, u32[]{:S(2)}) %collective-permute-start.3) | collective-permute-done | bytes 131104 | tf_op jit(solution)/shard_map/ppermute | solution.py:24
  16.0 2.5 %collective-permute-done.5.later_ref = bf16[256,256]{1,0:T(8,128)(2,1)S(1)} collective-permute-done((bf16[256,256]{1,0:T(8,128)(2,1)S(1)}, bf16[256,256]{1,0:T(8,128)(2,1)S(1)}, u32[]{:S(2)}, u32[]{:S(2)}) %collective-permute-start.5) | collective-permute-done | bytes 131104 | tf_op jit(solution)/shard_map/ppermute | solution.py:24
  19.0 2.5 %collective-permute-start.6 = (bf16[1,96,384]{2,1,0:T(8,128)(2,1)S(1)}, bf16[1,96,384]{2,1,0:T(8,128)(2,1)S(1)}, u32[]{:S(2)}, u32[]{:S(2)}) collective-permute-start(bf16[1,96,384]{2,1,0:T(8,128)(2,1)S(1)} %get-tuple-element.48), channel_id=1, source_target_pairs={{0,12},{4,8},{8,4},{12,0},{16,28},{20,24},{24,20},{28,16},{1,13},{... | collective-permute-start | bytes 221192 | tf_op jit(solution)/shard_map/ppermute | solution.py:24
  22.5 1.4 %collective-permute-done.6 = bf16[1,96,384]{2,1,0:T(8,128)(2,1)S(1)} collective-permute-done((bf16[1,96,384]{2,1,0:T(8,128)(2,1)S(1)}, bf16[1,96,384]{2,1,0:T(8,128)(2,1)S(1)}, u32[]{:S(2)}, u32[]{:S(2)}) %collective-permute-start.6) | collective-permute-done | bytes 73760 | tf_op jit(solution)/shard_map/ppermute | solution.py:24
  23.9 1.6 %collective-permute-done.7 = bf16[1,96,384]{2,1,0:T(8,128)(2,1)S(1)} collective-permute-done((bf16[1,96,384]{2,1,0:T(8,128)(2,1)S(1)}, bf16[1,96,384]{2,1,0:T(8,128)(2,1)S(1)}, u32[]{:S(2)}, u32[]{:S(2)}) %collective-permute-start.7) | collective-permute-done | bytes 73760 | tf_op jit(solution)/shard_map/ppermute | solution.py:24
  25.5 2.6 %collective-permute-start.9 = (bf16[1,96,384]{2,1,0:T(8,128)(2,1)S(1)}, bf16[1,96,384]{2,1,0:T(8,128)(2,1)S(1)}, u32[]{:S(2)}, u32[]{:S(2)}) collective-permute-start(bf16[1,96,384]{2,1,0:T(8,128)(2,1)S(1)} %add_convert_fusion.1), channel_id=1, source_target_pairs={{0,16},{4,20},{8,24},{12,28},{16,0},{20,4},{24,8},{28,12},{1,17},{... | collective-permute-start | bytes 221192 | tf_op jit(solution)/shard_map/ppermute | solution.py:24
  28.8 1.1 %collective-permute-done.9 = bf16[1,96,384]{2,1,0:T(8,128)(2,1)S(1)} collective-permute-done((bf16[1,96,384]{2,1,0:T(8,128)(2,1)S(1)}, bf16[1,96,384]{2,1,0:T(8,128)(2,1)S(1)}, u32[]{:S(2)}, u32[]{:S(2)}) %collective-permute-start.9) | collective-permute-done | bytes 73760 | tf_op jit(solution)/shard_map/ppermute | solution.py:24
  29.9 1.1 %collective-permute-start.10 = (bf16[1,96,384]{2,1,0:T(8,128)(2,1)S(1)}, bf16[1,96,384]{2,1,0:T(8,128)(2,1)S(1)}, u32[]{:S(2)}, u32[]{:S(2)}) collective-permute-start(bf16[1,96,384]{2,1,0:T(8,128)(2,1)S(1)} %add_convert_fusion.refs_0_), channel_id=1, source_target_pairs={{0,12},{4,8},{8,4},{12,0},{16,28},{20,24},{24,20},{28,16},{1,13},{... | collective-permute-start | bytes 221192 | tf_op jit(solution)/shard_map/ppermute | solution.py:24
  31.1 1.8 %collective-permute-start.11 = (bf16[1,96,384]{2,1,0:T(8,128)(2,1)S(1)}, bf16[1,96,384]{2,1,0:T(8,128)(2,1)S(1)}, u32[]{:S(2)}, u32[]{:S(2)}) collective-permute-start(bf16[1,96,384]{2,1,0:T(8,128)(2,1)S(1)} %add_convert_fusion.refs_0_), channel_id=1, source_target_pairs={{0,4},{4,0},{8,12},{12,8},{16,20},{20,16},{24,28},{28,24},{1,5},{5... | collective-permute-start | bytes 221192 | tf_op jit(solution)/shard_map/ppermute | solution.py:24
  33.2 0.9 %collective-permute-done.10.refs_1_ = bf16[1,96,384]{2,1,0:T(8,128)(2,1)S(1)} collective-permute-done((bf16[1,96,384]{2,1,0:T(8,128)(2,1)S(1)}, bf16[1,96,384]{2,1,0:T(8,128)(2,1)S(1)}, u32[]{:S(2)}, u32[]{:S(2)}) %collective-permute-start.10) | collective-permute-done | bytes 73760 | tf_op jit(solution)/shard_map/ppermute | solution.py:24
  34.1 0.8 %collective-permute-done.11.refs_2_ = bf16[1,96,384]{2,1,0:T(8,128)(2,1)S(1)} collective-permute-done((bf16[1,96,384]{2,1,0:T(8,128)(2,1)S(1)}, bf16[1,96,384]{2,1,0:T(8,128)(2,1)S(1)}, u32[]{:S(2)}, u32[]{:S(2)}) %collective-permute-start.11) | collective-permute-done | bytes 73760 | tf_op jit(solution)/shard_map/ppermute | solution.py:24
  34.9 1.2 %collective-permute-done.12.refs_3_ = bf16[1,96,384]{2,1,0:T(8,128)(2,1)S(1)} collective-permute-done((bf16[1,96,384]{2,1,0:T(8,128)(2,1)S(1)}, bf16[1,96,384]{2,1,0:T(8,128)(2,1)S(1)}, u32[]{:S(2)}, u32[]{:S(2)}) %collective-permute-start.12) | collective-permute-done | bytes 73760 | tf_op jit(solution)/shard_map/ppermute | solution.py:24
  36.1 0.8 %density_parts.1 = (f32[96,384]{1,0:T(8,128)S(1)}, bf16[96,384]{1,0:T(8,128)(2,1)S(1)}, bf16[96,384]{1,0:T(8,128)(2,1)S(1)}, bf16[96,384]{1,0:T(8,128)(2,1)S(1)}, f32[1,384]{1,0:T(1,128)S(1)}) custom-call(f32[1,384,384]{2,1,0:T(8,128)S(1)} %subtract_divide_fusion.inverse_ref, bf16[1,96,384]{2,1,0:T(8,128)(2,1)S(1)} %add_convert_fusion.refs_0_, ...), custom_call_target="tpu_custom_call" | custom-call | tf_op jit(solution)/shard_map/density_parts/pallas_call | solution.py:320
  36.9 1.3 %collective-permute-start.13 = (bf16[96,384]{1,0:T(8,128)(2,1)S(1)}, bf16[96,384]{1,0:T(8,128)(2,1)S(1)}, u32[]{:S(2)}, u32[]{:S(2)}) collective-permute-start(bf16[96,384]{1,0:T(8,128)(2,1)S(1)} %get-tuple-element.53), channel_id=1, source_target_pairs={{0,2},{1,3},{2,0},{3,1},{4,6},{5,7},{6,4},{7,5},{8,10},{9,11},{10,... | collective-permute-start | bytes 221192 | tf_op jit(solution)/shard_map/ppermute | solution.py:24
  38.2 3.8 %collective-permute-start.14 = (bf16[96,384]{1,0:T(8,128)(2,1)S(1)}, bf16[96,384]{1,0:T(8,128)(2,1)S(1)}, u32[]{:S(2)}, u32[]{:S(2)}) collective-permute-start(bf16[96,384]{1,0:T(8,128)(2,1)S(1)} %get-tuple-element.54), channel_id=1, source_target_pairs={{0,1},{1,0},{2,3},{3,2},{4,5},{5,4},{6,7},{7,6},{8,9},{9,8},{10,11... | collective-permute-start | bytes 221192 | tf_op jit(solution)/shard_map/ppermute | solution.py:24
  42.1 0.8 %collective-permute-done.14.refs_1_ = bf16[96,384]{1,0:T(8,128)(2,1)S(1)} collective-permute-done((bf16[96,384]{1,0:T(8,128)(2,1)S(1)}, bf16[96,384]{1,0:T(8,128)(2,1)S(1)}, u32[]{:S(2)}, u32[]{:S(2)}) %collective-permute-start.14) | collective-permute-done | bytes 73760 | tf_op jit(solution)/shard_map/ppermute | solution.py:24
  42.9 3.0 %collective-permute-done.15.refs_2_ = bf16[96,384]{1,0:T(8,128)(2,1)S(1)} collective-permute-done((bf16[96,384]{1,0:T(8,128)(2,1)S(1)}, bf16[96,384]{1,0:T(8,128)(2,1)S(1)}, u32[]{:S(2)}, u32[]{:S(2)}) %collective-permute-start.15) | collective-permute-done | bytes 73760 | tf_op jit(solution)/shard_map/ppermute | solution.py:24
  45.9 0.8 %closing.1 = (f32[96,384]{1,0:T(8,128)}, f32[1,1]{1,0:T(1,128)}) custom-call(f32[96,384]{1,0:T(8,128)S(1)} %get-tuple-element.51.own_ref, f32[1,384]{1,0:T(1,128)S(1)} %get-tuple-element.52.energy_ref, bf16[96,384]{1,0:T(8,128)(2,1)S(1)} %collective-permute-done.13.refs_0_, bf16[96,384]{1,0:T(8,128)(2,1)S(1)} %collective-permute-done.14.refs_1_, ...), custom_call_target="tpu_custom_call" | custom-call | tf_op jit(solution)/shard_map/closing/pallas_call | solution.py:370
  (29 shorter events, 4.2 us)
Async XLA Ops:
  0.6 12.5 %copy-start.2 = (f32[512]{0:T(512)S(1)}, f32[512]{0:T(512)}, u32[]{:S(2)}) copy-start(f32[512]{0:T(512)} %param.14) | copy-start | bytes 6148
  0.6 12.5 %slice-start = ((s32[512]{0:T(512)}), s32[8]{0:T(128)S(1)}, s32[]{:S(2)}) async-start(s32[512]{0:T(512)} %pick_hbm.1), calls=%async_computation | async-start | bytes 1024 | tf_op jit(solution)/shard_map/slice | solution.py:436
  0.7 12.7 %copy-start = (bf16[16,64,384]{2,1,0:T(8,128)(2,1)S(1)}, bf16[16,64,384]{2,1,0:T(8,128)(2,1)}, u32[]{:S(2)}) copy-start(bf16[16,64,384]{2,1,0:T(8,128)(2,1)} %vir_ref.1) | copy-start | bytes 2359300
  3.8 24.3 %copy-start.1 = (f32[384]{0:T(512)S(1)}, f32[384]{0:T(512)}, u32[]{:S(2)}) copy-start(f32[384]{0:T(512)} %param.15) | copy-start | bytes 4612
  3.8 8.7 %collective-permute-start = (bf16[272,256]{1,0:T(8,128)(2,1)S(1)}, bf16[272,256]{1,0:T(8,128)(2,1)S(1)}, u32[]{:S(2)}, u32[]{:S(2)}) collective-permute-start(bf16[272,256]{1,0:T(8,128)(2,1)S(1)} %get-tuple-element.38), channel_id=1, source_target_pairs={{0,2},{1,3},{2,0},{3,1},{4,6},{5,7},{6,4},{7,5},{8,10},{9,11},{10,... | collective-permute-start | bytes 417800 | tf_op jit(solution)/shard_map/ppermute | solution.py:24
  6.0 7.3 %collective-permute-start.1 = (bf16[272,256]{1,0:T(8,128)(2,1)S(1)}, bf16[272,256]{1,0:T(8,128)(2,1)S(1)}, u32[]{:S(2)}, u32[]{:S(2)}) collective-permute-start(bf16[272,256]{1,0:T(8,128)(2,1)S(1)} %get-tuple-element.39), channel_id=1, source_target_pairs={{0,1},{1,0},{2,3},{3,2},{4,5},{5,4},{6,7},{7,6},{8,9},{9,8},{10,11... | collective-permute-start | bytes 417800 | tf_op jit(solution)/shard_map/ppermute | solution.py:24
  6.9 6.4 %collective-permute-start.2 = (bf16[272,256]{1,0:T(8,128)(2,1)S(1)}, bf16[272,256]{1,0:T(8,128)(2,1)S(1)}, u32[]{:S(2)}, u32[]{:S(2)}) collective-permute-start(bf16[272,256]{1,0:T(8,128)(2,1)S(1)} %get-tuple-element.40), channel_id=1, source_target_pairs={{0,3},{1,2},{2,1},{3,0},{4,7},{5,6},{6,5},{7,4},{8,11},{9,10},{10,... | collective-permute-start | bytes 417800 | tf_op jit(solution)/shard_map/ppermute | solution.py:24
  10.3 5.2 %collective-permute-start.3 = (bf16[256,256]{1,0:T(8,128)(2,1)S(1)}, bf16[256,256]{1,0:T(8,128)(2,1)S(1)}, u32[]{:S(2)}, u32[]{:S(2)}) collective-permute-start(bf16[256,256]{1,0:T(8,128)(2,1)S(1)} %get-tuple-element.43), channel_id=1, source_target_pairs={{0,2},{1,3},{2,0},{3,1},{4,6},{5,7},{6,4},{7,5},{8,10},{9,11},{10,... | collective-permute-start | bytes 393224 | tf_op jit(solution)/shard_map/ppermute | solution.py:24
  11.7 3.7 %collective-permute-start.4 = (bf16[256,256]{1,0:T(8,128)(2,1)S(1)}, bf16[256,256]{1,0:T(8,128)(2,1)S(1)}, u32[]{:S(2)}, u32[]{:S(2)}) collective-permute-start(bf16[256,256]{1,0:T(8,128)(2,1)S(1)} %get-tuple-element.44), channel_id=1, source_target_pairs={{0,1},{1,0},{2,3},{3,2},{4,5},{5,4},{6,7},{7,6},{8,9},{9,8},{10,11... | collective-permute-start | bytes 393224 | tf_op jit(solution)/shard_map/ppermute | solution.py:24
  12.5 6.0 %collective-permute-start.5 = (bf16[256,256]{1,0:T(8,128)(2,1)S(1)}, bf16[256,256]{1,0:T(8,128)(2,1)S(1)}, u32[]{:S(2)}, u32[]{:S(2)}) collective-permute-start(bf16[256,256]{1,0:T(8,128)(2,1)S(1)} %get-tuple-element.46), channel_id=1, source_target_pairs={{0,3},{1,2},{2,1},{3,0},{4,7},{5,6},{6,5},{7,4},{8,11},{9,10},{10,... | collective-permute-start | bytes 393224 | tf_op jit(solution)/shard_map/ppermute | solution.py:24
  19.0 4.9 %collective-permute-start.6 = (bf16[1,96,384]{2,1,0:T(8,128)(2,1)S(1)}, bf16[1,96,384]{2,1,0:T(8,128)(2,1)S(1)}, u32[]{:S(2)}, u32[]{:S(2)}) collective-permute-start(bf16[1,96,384]{2,1,0:T(8,128)(2,1)S(1)} %get-tuple-element.48), channel_id=1, source_target_pairs={{0,12},{4,8},{8,4},{12,0},{16,28},{20,24},{24,20},{28,16},{1,13},{... | collective-permute-start | bytes 221192 | tf_op jit(solution)/shard_map/ppermute | solution.py:24
  21.6 3.9 %collective-permute-start.7 = (bf16[1,96,384]{2,1,0:T(8,128)(2,1)S(1)}, bf16[1,96,384]{2,1,0:T(8,128)(2,1)S(1)}, u32[]{:S(2)}, u32[]{:S(2)}) collective-permute-start(bf16[1,96,384]{2,1,0:T(8,128)(2,1)S(1)} %get-tuple-element.49), channel_id=1, source_target_pairs={{0,4},{4,0},{8,12},{12,8},{16,20},{20,16},{24,28},{28,24},{1,5},{5... | collective-permute-start | bytes 221192 | tf_op jit(solution)/shard_map/ppermute | solution.py:24
  21.8 3.6 %collective-permute-start.8 = (bf16[1,96,384]{2,1,0:T(8,128)(2,1)S(1)}, bf16[1,96,384]{2,1,0:T(8,128)(2,1)S(1)}, u32[]{:S(2)}, u32[]{:S(2)}) collective-permute-start(bf16[1,96,384]{2,1,0:T(8,128)(2,1)S(1)} %get-tuple-element.50), channel_id=1, source_target_pairs={{0,8},{4,12},{8,0},{12,4},{16,24},{20,28},{24,16},{28,20},{1,9},{5... | collective-permute-start | bytes 221192 | tf_op jit(solution)/shard_map/ppermute | solution.py:24
  25.5 4.4 %collective-permute-start.9 = (bf16[1,96,384]{2,1,0:T(8,128)(2,1)S(1)}, bf16[1,96,384]{2,1,0:T(8,128)(2,1)S(1)}, u32[]{:S(2)}, u32[]{:S(2)}) collective-permute-start(bf16[1,96,384]{2,1,0:T(8,128)(2,1)S(1)} %add_convert_fusion.1), channel_id=1, source_target_pairs={{0,16},{4,20},{8,24},{12,28},{16,0},{20,4},{24,8},{28,12},{1,17},{... | collective-permute-start | bytes 221192 | tf_op jit(solution)/shard_map/ppermute | solution.py:24
  29.9 4.2 %collective-permute-start.10 = (bf16[1,96,384]{2,1,0:T(8,128)(2,1)S(1)}, bf16[1,96,384]{2,1,0:T(8,128)(2,1)S(1)}, u32[]{:S(2)}, u32[]{:S(2)}) collective-permute-start(bf16[1,96,384]{2,1,0:T(8,128)(2,1)S(1)} %add_convert_fusion.refs_0_), channel_id=1, source_target_pairs={{0,12},{4,8},{8,4},{12,0},{16,28},{20,24},{24,20},{28,16},{1,13},{... | collective-permute-start | bytes 221192 | tf_op jit(solution)/shard_map/ppermute | solution.py:24
  31.1 3.8 %collective-permute-start.11 = (bf16[1,96,384]{2,1,0:T(8,128)(2,1)S(1)}, bf16[1,96,384]{2,1,0:T(8,128)(2,1)S(1)}, u32[]{:S(2)}, u32[]{:S(2)}) collective-permute-start(bf16[1,96,384]{2,1,0:T(8,128)(2,1)S(1)} %add_convert_fusion.refs_0_), channel_id=1, source_target_pairs={{0,4},{4,0},{8,12},{12,8},{16,20},{20,16},{24,28},{28,24},{1,5},{5... | collective-permute-start | bytes 221192 | tf_op jit(solution)/shard_map/ppermute | solution.py:24
  32.9 3.2 %collective-permute-start.12 = (bf16[1,96,384]{2,1,0:T(8,128)(2,1)S(1)}, bf16[1,96,384]{2,1,0:T(8,128)(2,1)S(1)}, u32[]{:S(2)}, u32[]{:S(2)}) collective-permute-start(bf16[1,96,384]{2,1,0:T(8,128)(2,1)S(1)} %add_convert_fusion.refs_0_), channel_id=1, source_target_pairs={{0,8},{4,12},{8,0},{12,4},{16,24},{20,28},{24,16},{28,20},{1,9},{5... | collective-permute-start | bytes 221192 | tf_op jit(solution)/shard_map/ppermute | solution.py:24
  36.9 5.2 %collective-permute-start.13 = (bf16[96,384]{1,0:T(8,128)(2,1)S(1)}, bf16[96,384]{1,0:T(8,128)(2,1)S(1)}, u32[]{:S(2)}, u32[]{:S(2)}) collective-permute-start(bf16[96,384]{1,0:T(8,128)(2,1)S(1)} %get-tuple-element.53), channel_id=1, source_target_pairs={{0,2},{1,3},{2,0},{3,1},{4,6},{5,7},{6,4},{7,5},{8,10},{9,11},{10,... | collective-permute-start | bytes 221192 | tf_op jit(solution)/shard_map/ppermute | solution.py:24
  38.2 4.7 %collective-permute-start.14 = (bf16[96,384]{1,0:T(8,128)(2,1)S(1)}, bf16[96,384]{1,0:T(8,128)(2,1)S(1)}, u32[]{:S(2)}, u32[]{:S(2)}) collective-permute-start(bf16[96,384]{1,0:T(8,128)(2,1)S(1)} %get-tuple-element.54), channel_id=1, source_target_pairs={{0,1},{1,0},{2,3},{3,2},{4,5},{5,4},{6,7},{7,6},{8,9},{9,8},{10,11... | collective-permute-start | bytes 221192 | tf_op jit(solution)/shard_map/ppermute | solution.py:24
  42.0 3.9 %collective-permute-start.15 = (bf16[96,384]{1,0:T(8,128)(2,1)S(1)}, bf16[96,384]{1,0:T(8,128)(2,1)S(1)}, u32[]{:S(2)}, u32[]{:S(2)}) collective-permute-start(bf16[96,384]{1,0:T(8,128)(2,1)S(1)} %get-tuple-element.55), channel_id=1, source_target_pairs={{0,3},{1,2},{2,1},{3,0},{4,7},{5,6},{6,5},{7,4},{8,11},{9,10},{10,... | collective-permute-start | bytes 221192 | tf_op jit(solution)/shard_map/ppermute | solution.py:24

commit v10 on v7

--- a/solution.py
+++ b/solution.py
@@ -42,15 +42,25 @@
     def kernel(ids_hbm, pick_hbm, occ_hbm, ints_hbm, *refs):
         outs, chosen_ref, tables_ref = refs[:n_pair], refs[n_pair], refs[n_pair + 1]
         ids_ref, pick_ref, occ_ref, held, small, large = refs[n_pair + 2 :]
-        tables = [
-            pltpu.make_async_copy(source, target, small.at[at])
-            for at, (source, target) in enumerate(((ids_hbm, ids_ref), (pick_hbm, pick_ref), (occ_hbm, occ_ref)))
+        names = [
+            pltpu.make_async_copy(ids_hbm, ids_ref, small.at[slots]),
+            pltpu.make_async_copy(pick_hbm, pick_ref, small.at[slots + 1]),
         ]
-        for copy in tables:
+        for copy in names:
             copy.start()
-        copies = started(ints_hbm, held, large, 0, count, width * width)
-        for copy in tables:
+        copies = []
+        for slot in range(count):
+            span = pl.ds(slot * width * width, width * width)
+            copies.append(pltpu.make_async_copy(ints_hbm.at[span, :], held.at[span, :], large.at[slot]))
+        copies[0].start()
+        for copy in names:
             copy.wait()
+        tables = []
+        for slot in range(slots):
+            target = occ_ref.at[slot] if slot < count else tables_ref.at[slot - count]
+            tables.append(pltpu.make_async_copy(occ_hbm.at[ids_ref[1, slot]], target, small.at[slot]))
+        for copy in tables[:count] + copies[1:] + tables[count:]:
+            copy.start()
         pair_at = lax.axis_index("pair")
         lane = lax.broadcasted_iota(jnp.int32, (SUB, nocc), 1)
         chosen = []
@@ -60,19 +70,25 @@
                     orbital = pick_ref[(pair_at ^ mate) * pairs + pair + side * n_half]
                     chosen.append(jnp.where(lane == orbital, 1.0, 0.0))
         chosen = jnp.concatenate(chosen, axis=0).astype(jnp.bfloat16)
-        weights = [slot_weights(chosen, occ_ref[ids_ref[1, slot]]) for slot in range(count)]
-        row = lax.broadcasted_iota(jnp.int32, (TILE, aux_rows), 0)
-        blocks = jnp.zeros((TILE, aux_rows), jnp.float32)
-        for slot in range(slots):
-            blocks = jnp.where(row == slot, ids_ref[0, slot].astype(jnp.float32), blocks)
-        for out in outs:
-            out[pl.ds(rows, TILE), :] = blocks.astype(jnp.bfloat16)
-        chosen_ref[...] = chosen
-        for slot in range(count, slots):
-            tables_ref[slot - count] = occ_ref[ids_ref[1, slot]]
+        for copy in tables[:count]:
+            copy.wait()
+        weights = slot_weights(chosen, occ_ref[0])
         for slot in range(count):
             copies[slot].wait()
-            halves(weights[slot], held, outs, slot, count, width, pairs)
+            if slot + 1 < count:
+                following = slot_weights(chosen, occ_ref[slot + 1])
+            else:
+                row = lax.broadcasted_iota(jnp.int32, (TILE, aux_rows), 0)
+                blocks = jnp.zeros((TILE, aux_rows), jnp.float32)
+                for at in range(slots):
+                    blocks = jnp.where(row == at, ids_ref[0, at].astype(jnp.float32), blocks)
+                for out in outs:
+                    out[pl.ds(rows, TILE), :] = blocks.astype(jnp.bfloat16)
+                chosen_ref[...] = chosen
+            halves(weights, held, outs, slot, count, width, pairs)
+            weights = following
+        for copy in tables[count:]:
+            copy.wait()
 
     return pl.pallas_call(
         kernel,
@@ -86,9 +102,9 @@
         scratch_shapes=[
             SMEM((2, slots), jnp.int32),
             SMEM((nocc,), jnp.int32),
-            VMEM(occ_coef.shape, jnp.bfloat16),
+            VMEM((count, width, nocc), jnp.bfloat16),
             VMEM((count * width * width, aux_rows), jnp.bfloat16),
-            pltpu.SemaphoreType.DMA((3,)),
+            pltpu.SemaphoreType.DMA((slots + 2,)),
             pltpu.SemaphoreType.DMA((count,)),
         ],
         compiler_params=PARAMS,

time: 46.8 us -> 46.9 us (level)
  no operation moved by 1% of the time
where the time goes in v10:
time: 46.9 us; the launch traced here: 46.7 us
  starting transfers between devices  19.7 us (42%)
  waiting for transfers between devices  15 us (32%)
  Pallas kernels  8.92 us (19%)
  other arithmetic  1.64 us (3%)
  between operations  1.42 us (3%)
    ppermute x16, starting transfers between devices, swapped(): lax.ppermute(value, axis, [(source, source ^ mask) for source in range(co...  19.7 us
    ppermute x16, waiting for transfers between devices, swapped(): lax.ppermute(value, axis, [(source, source ^ mask) for source in range(co...  15 us
    pallas_call x1, Pallas kernels, half_first(): pl.pallas_call(kernel, in_specs=[pl.BlockSpec(memory_space=pltpu.HBM)] *...  3.22 us
    pallas_call x1, Pallas kernels, half_rest(): pl.pallas_call(kernel, in_specs=[pl.BlockSpec(memory_space=SMEM)] + whole...  2.73 us
  transfers between devices with their start and end apart: 16, of which 10 were waited for; matrix products, arithmetic and copies ran while one was open for 3% of the time, Pallas kernels for 8%

profile of v10, /device:TPU:1, one launch (start us, length us, event | category | flops | bytes accessed | tf_op | source)
XLA Modules:
  0.0 46.7 jit_solution(95227515789700324)
XLA Ops:
  0.7 3.2 %half_first.1 = (bf16[272,256]{1,0:T(8,128)(2,1)S(1)}, bf16[272,256]{1,0:T(8,128)(2,1)S(1)}, bf16[272,256]{1,0:T(8,128)(2,1)S(1)}, bf16[272,256]{1,0:T(8,128)(2,...) custom-call(s32[2,4]{1,0:T(2,128)} %bitcast.7, s32[512]{0:T(512)} %pick_hbm.1, ...), custom_call_target="tpu_custom_call" | custom-call | tf_op jit(solution)/shard_map/half_first/pallas_call | solution.py:93
  3.9 2.1 %collective-permute-start = (bf16[272,256]{1,0:T(8,128)(2,1)S(1)}, bf16[272,256]{1,0:T(8,128)(2,1)S(1)}, u32[]{:S(2)}, u32[]{:S(2)}) collective-permute-start(bf16[272,256]{1,0:T(8,128)(2,1)S(1)} %get-tuple-element.38), channel_id=1, source_target_pairs={{0,2},{1,3},{2,0},{3,1},{4,6},{5,7},{6,4},{7,5},{8,10},{9,11},{10,... | collective-permute-start | bytes 417800 | tf_op jit(solution)/shard_map/ppermute | solution.py:24
  6.0 1.0 %collective-permute-start.1 = (bf16[272,256]{1,0:T(8,128)(2,1)S(1)}, bf16[272,256]{1,0:T(8,128)(2,1)S(1)}, u32[]{:S(2)}, u32[]{:S(2)}) collective-permute-start(bf16[272,256]{1,0:T(8,128)(2,1)S(1)} %get-tuple-element.39), channel_id=1, source_target_pairs={{0,1},{1,0},{2,3},{3,2},{4,5},{5,4},{6,7},{7,6},{8,9},{9,8},{10,11... | collective-permute-start | bytes 417800 | tf_op jit(solution)/shard_map/ppermute | solution.py:24
  7.6 2.7 %half_rest.1 = (bf16[256,256]{1,0:T(8,128)(2,1)S(1)}, bf16[256,256]{1,0:T(8,128)(2,1)S(1)}, bf16[256,256]{1,0:T(8,128)(2,1)S(1)}, bf16[256,256]{1,0:T(8,128)(2,1)S(1)}) custom-call(s32[1]{0:T(128)S(6)} %copy.10.count_ref, bf16[64,512]{1,0:T(8,128)(2,1)S(1)} %get-tuple-element.32.chosen_ref, bf16[2,64,512]{2,1,0:T(8,128)(2,1)S(1)} %get-tuple-element.33.tables_ref, ...), custom_call_target="tpu_custom_call" | custom-call | tf_op jit(solution)/shard_map/half_rest/pallas_call | solution.py:166
  10.4 1.4 %collective-permute-start.3 = (bf16[256,256]{1,0:T(8,128)(2,1)S(1)}, bf16[256,256]{1,0:T(8,128)(2,1)S(1)}, u32[]{:S(2)}, u32[]{:S(2)}) collective-permute-start(bf16[256,256]{1,0:T(8,128)(2,1)S(1)} %get-tuple-element.43), channel_id=1, source_target_pairs={{0,2},{1,3},{2,0},{3,1},{4,6},{5,7},{6,4},{7,5},{8,10},{9,11},{10,... | collective-permute-start | bytes 393224 | tf_op jit(solution)/shard_map/ppermute | solution.py:24
  11.8 0.8 %collective-permute-start.4 = (bf16[256,256]{1,0:T(8,128)(2,1)S(1)}, bf16[256,256]{1,0:T(8,128)(2,1)S(1)}, u32[]{:S(2)}, u32[]{:S(2)}) collective-permute-start(bf16[256,256]{1,0:T(8,128)(2,1)S(1)} %get-tuple-element.44), channel_id=1, source_target_pairs={{0,1},{1,0},{2,3},{3,2},{4,5},{5,4},{6,7},{7,6},{8,9},{9,8},{10,11... | collective-permute-start | bytes 393224 | tf_op jit(solution)/shard_map/ppermute | solution.py:24
  13.8 1.8 %collective-permute-done.3.refs_4_ = bf16[256,256]{1,0:T(8,128)(2,1)S(1)} collective-permute-done((bf16[256,256]{1,0:T(8,128)(2,1)S(1)}, bf16[256,256]{1,0:T(8,128)(2,1)S(1)}, u32[]{:S(2)}, u32[]{:S(2)}) %collective-permute-start.3) | collective-permute-done | bytes 131104 | tf_op jit(solution)/shard_map/ppermute | solution.py:24
  16.1 2.5 %collective-permute-done.5.later_ref = bf16[256,256]{1,0:T(8,128)(2,1)S(1)} collective-permute-done((bf16[256,256]{1,0:T(8,128)(2,1)S(1)}, bf16[256,256]{1,0:T(8,128)(2,1)S(1)}, u32[]{:S(2)}, u32[]{:S(2)}) %collective-permute-start.5) | collective-permute-done | bytes 131104 | tf_op jit(solution)/shard_map/ppermute | solution.py:24
  19.1 2.5 %collective-permute-start.6 = (bf16[1,96,384]{2,1,0:T(8,128)(2,1)S(1)}, bf16[1,96,384]{2,1,0:T(8,128)(2,1)S(1)}, u32[]{:S(2)}, u32[]{:S(2)}) collective-permute-start(bf16[1,96,384]{2,1,0:T(8,128)(2,1)S(1)} %get-tuple-element.48), channel_id=1, source_target_pairs={{0,12},{4,8},{8,4},{12,0},{16,28},{20,24},{24,20},{28,16},{1,13},{... | collective-permute-start | bytes 221192 | tf_op jit(solution)/shard_map/ppermute | solution.py:24
  22.6 1.4 %collective-permute-done.6 = bf16[1,96,384]{2,1,0:T(8,128)(2,1)S(1)} collective-permute-done((bf16[1,96,384]{2,1,0:T(8,128)(2,1)S(1)}, bf16[1,96,384]{2,1,0:T(8,128)(2,1)S(1)}, u32[]{:S(2)}, u32[]{:S(2)}) %collective-permute-start.6) | collective-permute-done | bytes 73760 | tf_op jit(solution)/shard_map/ppermute | solution.py:24
  24.0 1.6 %collective-permute-done.7 = bf16[1,96,384]{2,1,0:T(8,128)(2,1)S(1)} collective-permute-done((bf16[1,96,384]{2,1,0:T(8,128)(2,1)S(1)}, bf16[1,96,384]{2,1,0:T(8,128)(2,1)S(1)}, u32[]{:S(2)}, u32[]{:S(2)}) %collective-permute-start.7) | collective-permute-done | bytes 73760 | tf_op jit(solution)/shard_map/ppermute | solution.py:24
  25.6 2.6 %collective-permute-start.9 = (bf16[1,96,384]{2,1,0:T(8,128)(2,1)S(1)}, bf16[1,96,384]{2,1,0:T(8,128)(2,1)S(1)}, u32[]{:S(2)}, u32[]{:S(2)}) collective-permute-start(bf16[1,96,384]{2,1,0:T(8,128)(2,1)S(1)} %add_convert_fusion.1), channel_id=1, source_target_pairs={{0,16},{4,20},{8,24},{12,28},{16,0},{20,4},{24,8},{28,12},{1,17},{... | collective-permute-start | bytes 221192 | tf_op jit(solution)/shard_map/ppermute | solution.py:24
  28.9 1.1 %collective-permute-done.9 = bf16[1,96,384]{2,1,0:T(8,128)(2,1)S(1)} collective-permute-done((bf16[1,96,384]{2,1,0:T(8,128)(2,1)S(1)}, bf16[1,96,384]{2,1,0:T(8,128)(2,1)S(1)}, u32[]{:S(2)}, u32[]{:S(2)}) %collective-permute-start.9) | collective-permute-done | bytes 73760 | tf_op jit(solution)/shard_map/ppermute | solution.py:24
  30.0 1.1 %collective-permute-start.10 = (bf16[1,96,384]{2,1,0:T(8,128)(2,1)S(1)}, bf16[1,96,384]{2,1,0:T(8,128)(2,1)S(1)}, u32[]{:S(2)}, u32[]{:S(2)}) collective-permute-start(bf16[1,96,384]{2,1,0:T(8,128)(2,1)S(1)} %add_convert_fusion.refs_0_), channel_id=1, source_target_pairs={{0,12},{4,8},{8,4},{12,0},{16,28},{20,24},{24,20},{28,16},{1,13},{... | collective-permute-start | bytes 221192 | tf_op jit(solution)/shard_map/ppermute | solution.py:24
  31.2 1.8 %collective-permute-start.11 = (bf16[1,96,384]{2,1,0:T(8,128)(2,1)S(1)}, bf16[1,96,384]{2,1,0:T(8,128)(2,1)S(1)}, u32[]{:S(2)}, u32[]{:S(2)}) collective-permute-start(bf16[1,96,384]{2,1,0:T(8,128)(2,1)S(1)} %add_convert_fusion.refs_0_), channel_id=1, source_target_pairs={{0,4},{4,0},{8,12},{12,8},{16,20},{20,16},{24,28},{28,24},{1,5},{5... | collective-permute-start | bytes 221192 | tf_op jit(solution)/shard_map/ppermute | solution.py:24
  33.3 0.9 %collective-permute-done.10.refs_1_ = bf16[1,96,384]{2,1,0:T(8,128)(2,1)S(1)} collective-permute-done((bf16[1,96,384]{2,1,0:T(8,128)(2,1)S(1)}, bf16[1,96,384]{2,1,0:T(8,128)(2,1)S(1)}, u32[]{:S(2)}, u32[]{:S(2)}) %collective-permute-start.10) | collective-permute-done | bytes 73760 | tf_op jit(solution)/shard_map/ppermute | solution.py:24
  34.2 0.8 %collective-permute-done.11.refs_2_ = bf16[1,96,384]{2,1,0:T(8,128)(2,1)S(1)} collective-permute-done((bf16[1,96,384]{2,1,0:T(8,128)(2,1)S(1)}, bf16[1,96,384]{2,1,0:T(8,128)(2,1)S(1)}, u32[]{:S(2)}, u32[]{:S(2)}) %collective-permute-start.11) | collective-permute-done | bytes 73760 | tf_op jit(solution)/shard_map/ppermute | solution.py:24
  35.0 1.2 %collective-permute-done.12.refs_3_ = bf16[1,96,384]{2,1,0:T(8,128)(2,1)S(1)} collective-permute-done((bf16[1,96,384]{2,1,0:T(8,128)(2,1)S(1)}, bf16[1,96,384]{2,1,0:T(8,128)(2,1)S(1)}, u32[]{:S(2)}, u32[]{:S(2)}) %collective-permute-start.12) | collective-permute-done | bytes 73760 | tf_op jit(solution)/shard_map/ppermute | solution.py:24
  36.2 0.8 %density_parts.1 = (f32[96,384]{1,0:T(8,128)S(1)}, bf16[96,384]{1,0:T(8,128)(2,1)S(1)}, bf16[96,384]{1,0:T(8,128)(2,1)S(1)}, bf16[96,384]{1,0:T(8,128)(2,1)S(1)}, f32[1,384]{1,0:T(1,128)S(1)}) custom-call(f32[1,384,384]{2,1,0:T(8,128)S(1)} %subtract_divide_fusion.inverse_ref, bf16[1,96,384]{2,1,0:T(8,128)(2,1)S(1)} %add_convert_fusion.refs_0_, ...), custom_call_target="tpu_custom_call" | custom-call | tf_op jit(solution)/shard_map/density_parts/pallas_call | solution.py:333
  37.0 1.3 %collective-permute-start.13 = (bf16[96,384]{1,0:T(8,128)(2,1)S(1)}, bf16[96,384]{1,0:T(8,128)(2,1)S(1)}, u32[]{:S(2)}, u32[]{:S(2)}) collective-permute-start(bf16[96,384]{1,0:T(8,128)(2,1)S(1)} %get-tuple-element.53), channel_id=1, source_target_pairs={{0,2},{1,3},{2,0},{3,1},{4,6},{5,7},{6,4},{7,5},{8,10},{9,11},{10,... | collective-permute-start | bytes 221192 | tf_op jit(solution)/shard_map/ppermute | solution.py:24
  38.3 3.8 %collective-permute-start.14 = (bf16[96,384]{1,0:T(8,128)(2,1)S(1)}, bf16[96,384]{1,0:T(8,128)(2,1)S(1)}, u32[]{:S(2)}, u32[]{:S(2)}) collective-permute-start(bf16[96,384]{1,0:T(8,128)(2,1)S(1)} %get-tuple-element.54), channel_id=1, source_target_pairs={{0,1},{1,0},{2,3},{3,2},{4,5},{5,4},{6,7},{7,6},{8,9},{9,8},{10,11... | collective-permute-start | bytes 221192 | tf_op jit(solution)/shard_map/ppermute | solution.py:24
  42.2 0.8 %collective-permute-done.14.refs_1_ = bf16[96,384]{1,0:T(8,128)(2,1)S(1)} collective-permute-done((bf16[96,384]{1,0:T(8,128)(2,1)S(1)}, bf16[96,384]{1,0:T(8,128)(2,1)S(1)}, u32[]{:S(2)}, u32[]{:S(2)}) %collective-permute-start.14) | collective-permute-done | bytes 73760 | tf_op jit(solution)/shard_map/ppermute | solution.py:24
  43.0 3.0 %collective-permute-done.15.refs_2_ = bf16[96,384]{1,0:T(8,128)(2,1)S(1)} collective-permute-done((bf16[96,384]{1,0:T(8,128)(2,1)S(1)}, bf16[96,384]{1,0:T(8,128)(2,1)S(1)}, u32[]{:S(2)}, u32[]{:S(2)}) %collective-permute-start.15) | collective-permute-done | bytes 73760 | tf_op jit(solution)/shard_map/ppermute | solution.py:24
  45.9 0.8 %closing.1 = (f32[96,384]{1,0:T(8,128)}, f32[1,1]{1,0:T(1,128)}) custom-call(f32[96,384]{1,0:T(8,128)S(1)} %get-tuple-element.51.own_ref, f32[1,384]{1,0:T(1,128)S(1)} %get-tuple-element.52.energy_ref, bf16[96,384]{1,0:T(8,128)(2,1)S(1)} %collective-permute-done.13.refs_0_, bf16[96,384]{1,0:T(8,128)(2,1)S(1)} %collective-permute-done.14.refs_1_, ...), custom_call_target="tpu_custom_call" | custom-call | tf_op jit(solution)/shard_map/closing/pallas_call | solution.py:383
  (29 shorter events, 4.3 us)
Async XLA Ops:
  0.6 12.5 %copy-start.2 = (f32[512]{0:T(512)S(1)}, f32[512]{0:T(512)}, u32[]{:S(2)}) copy-start(f32[512]{0:T(512)} %param.14) | copy-start | bytes 6148
  0.6 12.5 %slice-start = ((s32[512]{0:T(512)}), s32[8]{0:T(128)S(1)}, s32[]{:S(2)}) async-start(s32[512]{0:T(512)} %pick_hbm.1), calls=%async_computation | async-start | bytes 1024 | tf_op jit(solution)/shard_map/slice | solution.py:449
  0.7 12.7 %copy-start = (bf16[16,64,384]{2,1,0:T(8,128)(2,1)S(1)}, bf16[16,64,384]{2,1,0:T(8,128)(2,1)}, u32[]{:S(2)}) copy-start(bf16[16,64,384]{2,1,0:T(8,128)(2,1)} %vir_ref.1) | copy-start | bytes 2359300
  3.9 24.4 %copy-start.1 = (f32[384]{0:T(512)S(1)}, f32[384]{0:T(512)}, u32[]{:S(2)}) copy-start(f32[384]{0:T(512)} %param.15) | copy-start | bytes 4612
  3.9 8.7 %collective-permute-start = (bf16[272,256]{1,0:T(8,128)(2,1)S(1)}, bf16[272,256]{1,0:T(8,128)(2,1)S(1)}, u32[]{:S(2)}, u32[]{:S(2)}) collective-permute-start(bf16[272,256]{1,0:T(8,128)(2,1)S(1)} %get-tuple-element.38), channel_id=1, source_target_pairs={{0,2},{1,3},{2,0},{3,1},{4,6},{5,7},{6,4},{7,5},{8,10},{9,11},{10,... | collective-permute-start | bytes 417800 | tf_op jit(solution)/shard_map/ppermute | solution.py:24
  6.0 7.3 %collective-permute-start.1 = (bf16[272,256]{1,0:T(8,128)(2,1)S(1)}, bf16[272,256]{1,0:T(8,128)(2,1)S(1)}, u32[]{:S(2)}, u32[]{:S(2)}) collective-permute-start(bf16[272,256]{1,0:T(8,128)(2,1)S(1)} %get-tuple-element.39), channel_id=1, source_target_pairs={{0,1},{1,0},{2,3},{3,2},{4,5},{5,4},{6,7},{7,6},{8,9},{9,8},{10,11... | collective-permute-start | bytes 417800 | tf_op jit(solution)/shard_map/ppermute | solution.py:24
  7.0 6.4 %collective-permute-start.2 = (bf16[272,256]{1,0:T(8,128)(2,1)S(1)}, bf16[272,256]{1,0:T(8,128)(2,1)S(1)}, u32[]{:S(2)}, u32[]{:S(2)}) collective-permute-start(bf16[272,256]{1,0:T(8,128)(2,1)S(1)} %get-tuple-element.40), channel_id=1, source_target_pairs={{0,3},{1,2},{2,1},{3,0},{4,7},{5,6},{6,5},{7,4},{8,11},{9,10},{10,... | collective-permute-start | bytes 417800 | tf_op jit(solution)/shard_map/ppermute | solution.py:24
  10.4 5.2 %collective-permute-start.3 = (bf16[256,256]{1,0:T(8,128)(2,1)S(1)}, bf16[256,256]{1,0:T(8,128)(2,1)S(1)}, u32[]{:S(2)}, u32[]{:S(2)}) collective-permute-start(bf16[256,256]{1,0:T(8,128)(2,1)S(1)} %get-tuple-element.43), channel_id=1, source_target_pairs={{0,2},{1,3},{2,0},{3,1},{4,6},{5,7},{6,4},{7,5},{8,10},{9,11},{10,... | collective-permute-start | bytes 393224 | tf_op jit(solution)/shard_map/ppermute | solution.py:24
  11.8 3.7 %collective-permute-start.4 = (bf16[256,256]{1,0:T(8,128)(2,1)S(1)}, bf16[256,256]{1,0:T(8,128)(2,1)S(1)}, u32[]{:S(2)}, u32[]{:S(2)}) collective-permute-start(bf16[256,256]{1,0:T(8,128)(2,1)S(1)} %get-tuple-element.44), channel_id=1, source_target_pairs={{0,1},{1,0},{2,3},{3,2},{4,5},{5,4},{6,7},{7,6},{8,9},{9,8},{10,11... | collective-permute-start | bytes 393224 | tf_op jit(solution)/shard_map/ppermute | solution.py:24
  12.6 6.0 %collective-permute-start.5 = (bf16[256,256]{1,0:T(8,128)(2,1)S(1)}, bf16[256,256]{1,0:T(8,128)(2,1)S(1)}, u32[]{:S(2)}, u32[]{:S(2)}) collective-permute-start(bf16[256,256]{1,0:T(8,128)(2,1)S(1)} %get-tuple-element.46), channel_id=1, source_target_pairs={{0,3},{1,2},{2,1},{3,0},{4,7},{5,6},{6,5},{7,4},{8,11},{9,10},{10,... | collective-permute-start | bytes 393224 | tf_op jit(solution)/shard_map/ppermute | solution.py:24
  19.1 4.9 %collective-permute-start.6 = (bf16[1,96,384]{2,1,0:T(8,128)(2,1)S(1)}, bf16[1,96,384]{2,1,0:T(8,128)(2,1)S(1)}, u32[]{:S(2)}, u32[]{:S(2)}) collective-permute-start(bf16[1,96,384]{2,1,0:T(8,128)(2,1)S(1)} %get-tuple-element.48), channel_id=1, source_target_pairs={{0,12},{4,8},{8,4},{12,0},{16,28},{20,24},{24,20},{28,16},{1,13},{... | collective-permute-start | bytes 221192 | tf_op jit(solution)/shard_map/ppermute | solution.py:24
  21.6 3.9 %collective-permute-start.7 = (bf16[1,96,384]{2,1,0:T(8,128)(2,1)S(1)}, bf16[1,96,384]{2,1,0:T(8,128)(2,1)S(1)}, u32[]{:S(2)}, u32[]{:S(2)}) collective-permute-start(bf16[1,96,384]{2,1,0:T(8,128)(2,1)S(1)} %get-tuple-element.49), channel_id=1, source_target_pairs={{0,4},{4,0},{8,12},{12,8},{16,20},{20,16},{24,28},{28,24},{1,5},{5... | collective-permute-start | bytes 221192 | tf_op jit(solution)/shard_map/ppermute | solution.py:24
  21.9 3.7 %collective-permute-start.8 = (bf16[1,96,384]{2,1,0:T(8,128)(2,1)S(1)}, bf16[1,96,384]{2,1,0:T(8,128)(2,1)S(1)}, u32[]{:S(2)}, u32[]{:S(2)}) collective-permute-start(bf16[1,96,384]{2,1,0:T(8,128)(2,1)S(1)} %get-tuple-element.50), channel_id=1, source_target_pairs={{0,8},{4,12},{8,0},{12,4},{16,24},{20,28},{24,16},{28,20},{1,9},{5... | collective-permute-start | bytes 221192 | tf_op jit(solution)/shard_map/ppermute | solution.py:24
  25.6 4.4 %collective-permute-start.9 = (bf16[1,96,384]{2,1,0:T(8,128)(2,1)S(1)}, bf16[1,96,384]{2,1,0:T(8,128)(2,1)S(1)}, u32[]{:S(2)}, u32[]{:S(2)}) collective-permute-start(bf16[1,96,384]{2,1,0:T(8,128)(2,1)S(1)} %add_convert_fusion.1), channel_id=1, source_target_pairs={{0,16},{4,20},{8,24},{12,28},{16,0},{20,4},{24,8},{28,12},{1,17},{... | collective-permute-start | bytes 221192 | tf_op jit(solution)/shard_map/ppermute | solution.py:24
  30.0 4.2 %collective-permute-start.10 = (bf16[1,96,384]{2,1,0:T(8,128)(2,1)S(1)}, bf16[1,96,384]{2,1,0:T(8,128)(2,1)S(1)}, u32[]{:S(2)}, u32[]{:S(2)}) collective-permute-start(bf16[1,96,384]{2,1,0:T(8,128)(2,1)S(1)} %add_convert_fusion.refs_0_), channel_id=1, source_target_pairs={{0,12},{4,8},{8,4},{12,0},{16,28},{20,24},{24,20},{28,16},{1,13},{... | collective-permute-start | bytes 221192 | tf_op jit(solution)/shard_map/ppermute | solution.py:24
  31.2 3.8 %collective-permute-start.11 = (bf16[1,96,384]{2,1,0:T(8,128)(2,1)S(1)}, bf16[1,96,384]{2,1,0:T(8,128)(2,1)S(1)}, u32[]{:S(2)}, u32[]{:S(2)}) collective-permute-start(bf16[1,96,384]{2,1,0:T(8,128)(2,1)S(1)} %add_convert_fusion.refs_0_), channel_id=1, source_target_pairs={{0,4},{4,0},{8,12},{12,8},{16,20},{20,16},{24,28},{28,24},{1,5},{5... | collective-permute-start | bytes 221192 | tf_op jit(solution)/shard_map/ppermute | solution.py:24
  33.0 3.2 %collective-permute-start.12 = (bf16[1,96,384]{2,1,0:T(8,128)(2,1)S(1)}, bf16[1,96,384]{2,1,0:T(8,128)(2,1)S(1)}, u32[]{:S(2)}, u32[]{:S(2)}) collective-permute-start(bf16[1,96,384]{2,1,0:T(8,128)(2,1)S(1)} %add_convert_fusion.refs_0_), channel_id=1, source_target_pairs={{0,8},{4,12},{8,0},{12,4},{16,24},{20,28},{24,16},{28,20},{1,9},{5... | collective-permute-start | bytes 221192 | tf_op jit(solution)/shard_map/ppermute | solution.py:24
  37.0 5.2 %collective-permute-start.13 = (bf16[96,384]{1,0:T(8,128)(2,1)S(1)}, bf16[96,384]{1,0:T(8,128)(2,1)S(1)}, u32[]{:S(2)}, u32[]{:S(2)}) collective-permute-start(bf16[96,384]{1,0:T(8,128)(2,1)S(1)} %get-tuple-element.53), channel_id=1, source_target_pairs={{0,2},{1,3},{2,0},{3,1},{4,6},{5,7},{6,4},{7,5},{8,10},{9,11},{10,... | collective-permute-start | bytes 221192 | tf_op jit(solution)/shard_map/ppermute | solution.py:24
  38.3 4.7 %collective-permute-start.14 = (bf16[96,384]{1,0:T(8,128)(2,1)S(1)}, bf16[96,384]{1,0:T(8,128)(2,1)S(1)}, u32[]{:S(2)}, u32[]{:S(2)}) collective-permute-start(bf16[96,384]{1,0:T(8,128)(2,1)S(1)} %get-tuple-element.54), channel_id=1, source_target_pairs={{0,1},{1,0},{2,3},{3,2},{4,5},{5,4},{6,7},{7,6},{8,9},{9,8},{10,11... | collective-permute-start | bytes 221192 | tf_op jit(solution)/shard_map/ppermute | solution.py:24
  42.0 3.9 %collective-permute-start.15 = (bf16[96,384]{1,0:T(8,128)(2,1)S(1)}, bf16[96,384]{1,0:T(8,128)(2,1)S(1)}, u32[]{:S(2)}, u32[]{:S(2)}) collective-permute-start(bf16[96,384]{1,0:T(8,128)(2,1)S(1)} %get-tuple-element.55), channel_id=1, source_target_pairs={{0,3},{1,2},{2,1},{3,0},{4,7},{5,6},{6,5},{7,4},{8,11},{9,10},{10,... | collective-permute-start | bytes 221192 | tf_op jit(solution)/shard_map/ppermute | solution.py:24
